TPU v7x, 32 devices: a whole 2x2x4 slice. The times are simulated.
32 devices in a mesh: section: 4 (over y, core), edge: 8 (over z, x).
Axes of the slice: x: 2, y: 2, z: 4, core: 2. Of those that a mesh axis runs over, the one named last changes fastest.
Arguments:
- layer_nodes: bfloat16 [4, 2, 256, 512], P('section'), may hold values from -6 to 6
- layer_edges: bfloat16 [4, 2, 2048, 512], P('section', None, 'edge'), may hold values from -6 to 6
- top_nodes: bfloat16 [2, 256, 512], replicated, may hold values from -1.5 to 1.5
- top_edges: bfloat16 [2, 2048, 512], P(None, 'edge'), may hold values from -1.5 to 1.5
- tile_blocks: int32 [2, 16, 2], P(None, 'edge'), may hold values from 0 to 1
- senders: int32 [2, 2048], P(None, 'edge'), may hold values from 0 to 127
- receivers: int32 [2, 2048], P(None, 'edge'), may hold values from 0 to 127
- w_send: bfloat16 [4, 512, 512], P('section'), may hold values from -0.0625 to 0.0625
- w_recv: bfloat16 [4, 512, 512], P('section'), may hold values from -0.0625 to 0.0625
- w_edge: bfloat16 [4, 512, 512], P('section'), may hold values from -0.25 to 0.25
- w_msg: bfloat16 [4, 512, 512], P('section'), may hold values from -0.125 to 0.125
- w_node: bfloat16 [4, 512, 512], P('section'), may hold values from -0.25 to 0.25
- w_agg: bfloat16 [4, 512, 512], P('section'), may hold values from -0.25 to 0.25
- w_out: bfloat16 [4, 512, 512], P('section'), may hold values from -0.125 to 0.125
Outputs:
- node_grads: bfloat16 [4, 2, 256, 512], P('section', None, 'edge')
- edge_grads: bfloat16 [4, 2, 2048, 512], P('section', None, 'edge')
- g_send: float32 [4, 512, 512], P('section', 'edge')
- g_recv: float32 [4, 512, 512], P('section', 'edge')
- g_edge: float32 [4, 512, 512], P('section', 'edge')
- g_msg: float32 [4, 512, 512], P('section', 'edge')
- g_node: float32 [4, 512, 512], P('section', 'edge')
- g_agg: float32 [4, 512, 512], P('section', 'edge')
- g_out: float32 [4, 512, 512], P('section', 'edge')
All inputs are finite; a program needn't handle non-finite values.
Results may differ from a plain program's by a relative error of at most 0.029.
Values may be sent and summed in bfloat16 or wider, within the bound.
No kernel may reach another device: no remote copies, remote signals or barrier semaphores. Data moves between devices by JAX's collectives and lax.ppermute only.
A program may use at most 64 MiB of HBM per device.

v0:
```python
import jax
import jax.numpy as jnp
from jax import lax
from jax.sharding import PartitionSpec as P

BLOCK = 128


def shifted(shard, axis, by):
    peers = lax.axis_size(axis)
    pairs = [(i, i + by) for i in range(peers) if 0 <= i + by < peers]
    return lax.ppermute(shard, axis, pairs)


def silu_slope(values):
    sigma = jax.nn.sigmoid(values)
    return sigma * (1.0 + values * (1.0 - sigma))


def matmul(left, right):
    return jnp.dot(left, right, preferred_element_type=jnp.float32)


def times_transposed(left, right):
    return lax.dot_general(
        left, right, (((1,), (1,)), ((), ())), preferred_element_type=jnp.float32
    )


def transposed_times(left, right):
    return lax.dot_general(
        left, right, (((0,), (0,)), ((), ())), preferred_element_type=jnp.float32
    )


def to_edges(values, block_hot, edge_hot):
    width = values.shape[1]
    grouped = values.reshape(block_hot.shape[1], -1, width)
    picked = jnp.einsum(
        "tb,bcd->tcd", block_hot, grouped, preferred_element_type=jnp.float32
    ).astype(jnp.bfloat16)
    spread = jnp.einsum("tec,tcd->ted", edge_hot, picked, preferred_element_type=jnp.float32)
    return spread.reshape(-1, width).astype(jnp.bfloat16)


def to_nodes(values, block_hot, edge_hot):
    width = values.shape[1]
    per_tile = jnp.einsum(
        "tec,ted->tcd",
        edge_hot,
        values.reshape(block_hot.shape[0], -1, width),
        preferred_element_type=jnp.float32,
    )
    summed = jnp.einsum(
        "tb,tcd->bcd", block_hot.astype(jnp.float32), per_tile, precision=lax.Precision.HIGHEST
    )
    return summed.reshape(-1, width)


def body(
    layer_nodes,
    layer_edges,
    top_nodes,
    top_edges,
    tile_blocks,
    senders,
    receivers,
    w_send,
    w_recv,
    w_edge,
    w_msg,
    w_node,
    w_agg,
    w_out,
):
    sections = lax.axis_size("section")
    section = lax.axis_index("section")
    groups = lax.axis_size("edge")
    member = lax.axis_index("edge")
    nodes_all = layer_nodes[0]
    edges_all = layer_edges[0]
    batches = nodes_all.shape[0]
    node_count = nodes_all.shape[1]
    width = nodes_all.shape[2]
    tile_count = tile_blocks.shape[1]
    tile_len = edges_all.shape[1] // tile_count
    block_count = node_count // BLOCK
    row_count = node_count // groups
    weight_send, weight_recv, weight_edge, weight_msg = (w_send[0], w_recv[0], w_edge[0], w_msg[0])
    weight_node, weight_agg, weight_out = (w_node[0], w_agg[0], w_out[0])
    lanes = jnp.arange(BLOCK, dtype=jnp.int32)
    slots = jnp.arange(block_count, dtype=jnp.int32)
    send_hot = (senders.reshape(batches, tile_count, tile_len)[..., None] == lanes).astype(
        jnp.bfloat16
    )
    recv_hot = (receivers.reshape(batches, tile_count, tile_len)[..., None] == lanes).astype(
        jnp.bfloat16
    )
    send_block = (tile_blocks[:, :, 0][..., None] == slots).astype(jnp.bfloat16)
    recv_block = (tile_blocks[:, :, 1][..., None] == slots).astype(jnp.bfloat16)

    def advance(moment, carry):
        node_in_grad, edge_in_grad, totals, node_record, edge_record = carry
        batch_raw = moment - (sections - 1 - section)
        valid = (batch_raw >= 0) & (batch_raw < batches)
        batch = jnp.clip(batch_raw, 0, batches - 1)
        feats = lax.dynamic_index_in_dim(nodes_all, batch, 0, keepdims=False)
        edge_feats = lax.dynamic_index_in_dim(edges_all, batch, 0, keepdims=False)
        send_tiles = lax.dynamic_index_in_dim(send_hot, batch, 0, keepdims=False)
        recv_tiles = lax.dynamic_index_in_dim(recv_hot, batch, 0, keepdims=False)
        send_blocks = lax.dynamic_index_in_dim(send_block, batch, 0, keepdims=False)
        recv_blocks = lax.dynamic_index_in_dim(recv_block, batch, 0, keepdims=False)
        top_node = lax.dynamic_index_in_dim(top_nodes, batch, 0, keepdims=False)
        top_edge = lax.dynamic_index_in_dim(top_edges, batch, 0, keepdims=False)
        is_last = section == sections - 1
        grad_nodes = jnp.where(is_last, top_node, node_in_grad)
        grad_edges = jnp.where(is_last, top_edge, edge_in_grad)
        send_feats = to_edges(feats, send_blocks, send_tiles)
        recv_feats = to_edges(feats, recv_blocks, recv_tiles)
        pre = (
            matmul(send_feats, weight_send)
            + matmul(recv_feats, weight_recv)
            + matmul(edge_feats, weight_edge)
        )
        act = jax.nn.silu(pre).astype(jnp.bfloat16)
        message = matmul(act, weight_msg).astype(jnp.bfloat16)
        partial_agg = to_nodes(message, recv_blocks, recv_tiles)
        aggregate = lax.psum(partial_agg, "edge")
        agg_b = aggregate.astype(jnp.bfloat16)
        node_pre = matmul(feats, weight_node) + matmul(agg_b, weight_agg)
        node_act = jax.nn.silu(node_pre).astype(jnp.bfloat16)
        node_delta = (times_transposed(grad_nodes, weight_out) * silu_slope(node_pre)).astype(
            jnp.bfloat16
        )
        agg_grad = times_transposed(node_delta, weight_agg).astype(jnp.bfloat16)
        node_term = times_transposed(node_delta, weight_node)
        agg_edges = to_edges(agg_grad, recv_blocks, recv_tiles)
        message_grad = (grad_edges.astype(jnp.float32) + agg_edges.astype(jnp.float32)).astype(
            jnp.bfloat16
        )
        edge_delta = (times_transposed(message_grad, weight_msg) * silu_slope(pre)).astype(
            jnp.bfloat16
        )
        edge_out = (
            grad_edges.astype(jnp.float32) + times_transposed(edge_delta, weight_edge)
        ).astype(jnp.bfloat16)
        send_grad = times_transposed(edge_delta, weight_send).astype(jnp.bfloat16)
        recv_grad = times_transposed(edge_delta, weight_recv).astype(jnp.bfloat16)
        partial_back = to_nodes(send_grad, send_blocks, send_tiles) + to_nodes(
            recv_grad, recv_blocks, recv_tiles
        )
        edge_terms = lax.psum(partial_back, "edge")
        node_out = (grad_nodes.astype(jnp.float32) + node_term + edge_terms).astype(jnp.bfloat16)
        fresh = (
            transposed_times(send_feats, edge_delta),
            transposed_times(recv_feats, edge_delta),
            transposed_times(edge_feats, edge_delta),
            transposed_times(act, message_grad),
            transposed_times(feats, node_delta),
            transposed_times(agg_b, node_delta),
            transposed_times(node_act, grad_nodes),
        )
        totals = tuple(
            (jnp.where(valid, before + extra, before) for before, extra in zip(totals, fresh))
        )
        own_out = lax.dynamic_slice_in_dim(node_out, member * row_count, row_count, 0)
        node_record = jnp.where(
            valid, lax.dynamic_update_index_in_dim(node_record, own_out, batch, 0), node_record
        )
        edge_record = jnp.where(
            valid, lax.dynamic_update_index_in_dim(edge_record, edge_out, batch, 0), edge_record
        )
        sent_nodes, sent_edges = shifted((node_out, edge_out), "section", -1)
        return (sent_nodes, sent_edges, totals, node_record, edge_record)

    hidden = weight_send.shape[1]
    square_in = jnp.zeros((width, hidden), jnp.float32)
    square_back = jnp.zeros((hidden, width), jnp.float32)
    start = (
        jnp.zeros((node_count, width), jnp.bfloat16),
        jnp.zeros(edges_all.shape[1:], jnp.bfloat16),
        (square_in, square_in, square_in, square_back, square_in, square_in, square_back),
        jnp.zeros((batches, row_count, width), jnp.bfloat16),
        jnp.zeros(edges_all.shape, jnp.bfloat16),
    )
    finished = lax.fori_loop(0, sections + batches - 1, advance, start)
    totals, node_record, edge_record = (finished[2], finished[3], finished[4])
    sum_send, sum_recv, sum_edge, sum_msg, sum_node, sum_agg, sum_out = totals
    sum_send, sum_recv, sum_edge, sum_msg = (
        lax.psum_scatter(sum_send, "edge", scatter_dimension=0, tiled=True),
        lax.psum_scatter(sum_recv, "edge", scatter_dimension=0, tiled=True),
        lax.psum_scatter(sum_edge, "edge", scatter_dimension=0, tiled=True),
        lax.psum_scatter(sum_msg, "edge", scatter_dimension=0, tiled=True),
    )
    sum_node = lax.dynamic_slice_in_dim(sum_node, member * (width // groups), width // groups, 0)
    sum_agg = lax.dynamic_slice_in_dim(sum_agg, member * (width // groups), width // groups, 0)
    sum_out = lax.dynamic_slice_in_dim(sum_out, member * (hidden // groups), hidden // groups, 0)
    return (
        node_record[None],
        edge_record[None],
        sum_send[None],
        sum_recv[None],
        sum_edge[None],
        sum_msg[None],
        sum_node[None],
        sum_agg[None],
        sum_out[None],
    )


def solution(mesh):
    in_specs = (
        P("section", None, None, None),
        P("section", None, "edge", None),
        P(),
        P(None, "edge", None),
        P(None, "edge", None),
        P(None, "edge"),
        P(None, "edge"),
        P("section", None, None),
        P("section", None, None),
        P("section", None, None),
        P("section", None, None),
        P("section", None, None),
        P("section", None, None),
        P("section", None, None),
    )
    out_specs = (
        P("section", None, "edge", None),
        P("section", None, "edge", None),
        P("section", "edge", None),
        P("section", "edge", None),
        P("section", "edge", None),
        P("section", "edge", None),
        P("section", "edge", None),
        P("section", "edge", None),
        P("section", "edge", None),
    )
    return jax.shard_map(body, mesh=mesh, in_specs=in_specs, out_specs=out_specs, check_vma=False)
```

profile of v0, /device:TPU:26, one launch (start us, length us, event | category | flops | bytes accessed | tf_op | source)
XLA Modules:
  0.0 990.2 jit_solution(16638269213786287057)
XLA Ops:
  13.3 699.6 %while.36 = (s32[]{:T(128)}, bf16[256,512]{1,0:T(8,128)(2,1)S(1)}, bf16[256,512]{1,0:T(8,128)(2,1)S(1)}, f32[512,512]{1,0:T(8,128)}, f32[512,512]{1,0:T(8,128)},...) while((s32[]{:T(128)}, bf16[256,512]{1,0:T(8,128)(2,1)S(1)}, ...), condition=%wide.region_3.4_spmd.clone, body=%wide.region_0.3_spmd.clone.sunk | while | flops 2910208000 | bytes 137858000 | solution.py:186
  21.1 39.2 %all-reduce.4 = bf16[256,512]{1,0:T(8,128)(2,1)S(1)} all-reduce(f32[256,512]{1,0:T(8,128)S(1)} %bitcast.271), channel_id=1, replica_groups=mesh['section'=4,'edge'=8] {'edge'}, use_global_device_ids=true, to_apply=%region_1.1 | all-reduce | flops 131072 | bytes 786432 | tf_op jit(solution)/shard_map/while/body/eval_jaxpr/psum | solution.py:128
  74.6 2.2 fusion.248
  78.1 2.5 add_select_fusion.17
  87.2 58.8 %all-reduce.3.cloned.1.call-done = f32[256,512]{1,0:T(8,128)} async-done(((f32[256,512]{1,0:T(8,128)}), f32[256,512]{1,0:T(8,128)}) %all-reduce.3.cloned.1.call-update) | async-done | bytes 524304 | tf_op jit(solution)/shard_map/while/body/eval_jaxpr/psum | solution.py:152
  158.8 40.0 %all-reduce.4 = bf16[256,512]{1,0:T(8,128)(2,1)S(1)} all-reduce(f32[256,512]{1,0:T(8,128)S(1)} %bitcast.271), channel_id=1, replica_groups=mesh['section'=4,'edge'=8] {'edge'}, use_global_device_ids=true, to_apply=%region_1.1 | all-reduce | flops 131072 | bytes 786432 | tf_op jit(solution)/shard_map/while/body/eval_jaxpr/psum | solution.py:128
  213.0 2.2 fusion.248
  216.5 2.9 add_select_fusion.17
  224.7 2.6 add_select_fusion.20
  227.3 59.2 %all-reduce.3.cloned.1.call-done = f32[256,512]{1,0:T(8,128)} async-done(((f32[256,512]{1,0:T(8,128)}), f32[256,512]{1,0:T(8,128)}) %all-reduce.3.cloned.1.call-update) | async-done | bytes 524304 | tf_op jit(solution)/shard_map/while/body/eval_jaxpr/psum | solution.py:152
  299.3 40.0 %all-reduce.4 = bf16[256,512]{1,0:T(8,128)(2,1)S(1)} all-reduce(f32[256,512]{1,0:T(8,128)S(1)} %bitcast.271), channel_id=1, replica_groups=mesh['section'=4,'edge'=8] {'edge'}, use_global_device_ids=true, to_apply=%region_1.1 | all-reduce | flops 131072 | bytes 786432 | tf_op jit(solution)/shard_map/while/body/eval_jaxpr/psum | solution.py:128
  353.5 2.2 fusion.248
  357.0 2.9 add_select_fusion.17
  365.2 2.6 add_select_fusion.20
  367.8 59.2 %all-reduce.3.cloned.1.call-done = f32[256,512]{1,0:T(8,128)} async-done(((f32[256,512]{1,0:T(8,128)}), f32[256,512]{1,0:T(8,128)}) %all-reduce.3.cloned.1.call-update) | async-done | bytes 524304 | tf_op jit(solution)/shard_map/while/body/eval_jaxpr/psum | solution.py:152
  439.8 40.0 %all-reduce.4 = bf16[256,512]{1,0:T(8,128)(2,1)S(1)} all-reduce(f32[256,512]{1,0:T(8,128)S(1)} %bitcast.271), channel_id=1, replica_groups=mesh['section'=4,'edge'=8] {'edge'}, use_global_device_ids=true, to_apply=%region_1.1 | all-reduce | flops 131072 | bytes 786432 | tf_op jit(solution)/shard_map/while/body/eval_jaxpr/psum | solution.py:128
  494.0 2.2 fusion.248
  497.5 2.9 add_select_fusion.17
  505.7 2.6 add_select_fusion.20
  508.3 59.2 %all-reduce.3.cloned.1.call-done = f32[256,512]{1,0:T(8,128)} async-done(((f32[256,512]{1,0:T(8,128)}), f32[256,512]{1,0:T(8,128)}) %all-reduce.3.cloned.1.call-update) | async-done | bytes 524304 | tf_op jit(solution)/shard_map/while/body/eval_jaxpr/psum | solution.py:152
  580.3 40.0 %all-reduce.4 = bf16[256,512]{1,0:T(8,128)(2,1)S(1)} all-reduce(f32[256,512]{1,0:T(8,128)S(1)} %bitcast.271), channel_id=1, replica_groups=mesh['section'=4,'edge'=8] {'edge'}, use_global_device_ids=true, to_apply=%region_1.1 | all-reduce | flops 131072 | bytes 786432 | tf_op jit(solution)/shard_map/while/body/eval_jaxpr/psum | solution.py:128
  634.5 2.2 fusion.248
  638.0 2.9 add_select_fusion.17
  646.2 2.6 add_select_fusion.20
  648.8 59.2 %all-reduce.3.cloned.1.call-done = f32[256,512]{1,0:T(8,128)} async-done(((f32[256,512]{1,0:T(8,128)}), f32[256,512]{1,0:T(8,128)}) %all-reduce.3.cloned.1.call-update) | async-done | bytes 524304 | tf_op jit(solution)/shard_map/while/body/eval_jaxpr/psum | solution.py:152
  715.4 1.6 dynamic-slice_bitcast_fusion
  716.9 1.6 dynamic-slice_bitcast_fusion.2
  718.5 1.6 dynamic-slice_bitcast_fusion.1
  720.1 62.6 %reduce-scatter.5.cloned.1.call-done = f32[64,512]{1,0:T(8,128)} async-done(((f32[512,512]{1,0:T(8,128)}), f32[64,512]{1,0:T(8,128)}) %reduce-scatter.5.cloned.1.call-update) | async-done | bytes 131088 | tf_op jit(solution)/shard_map/reduce_scatter | solution.py:190
  782.7 66.9 %reduce-scatter.7.cloned.1.call-done = f32[64,512]{1,0:T(8,128)} async-done(((f32[512,512]{1,0:T(8,128)}), f32[64,512]{1,0:T(8,128)}) %reduce-scatter.7.cloned.1.call-update) | async-done | bytes 131088 | tf_op jit(solution)/shard_map/reduce_scatter | solution.py:191
  849.6 66.4 %reduce-scatter.9.cloned.1.call-done = f32[64,512]{1,0:T(8,128)} async-done(((f32[512,512]{1,0:T(8,128)}), f32[64,512]{1,0:T(8,128)}) %reduce-scatter.9.cloned.1.call-update) | async-done | bytes 131088 | tf_op jit(solution)/shard_map/reduce_scatter | solution.py:192
  916.0 66.9 %reduce-scatter.11.cloned.1.call-done = f32[64,512]{1,0:T(8,128)} async-done(((f32[512,512]{1,0:T(8,128)}), f32[64,512]{1,0:T(8,128)}) %reduce-scatter.11.cloned.1.call-update) | async-done | bytes 131088 | tf_op jit(solution)/shard_map/reduce_scatter | solution.py:193
  (555 shorter events, 174.6 us)
Async XLA Ops:
  13.3 132.7 %all-reduce.3.cloned.1.call-start = ((), (), s32[]{:S(2)}) async-start(), calls=%async_computation.8 | async-start | bytes 1048576 | tf_op jit(solution)/shard_map/while/body/eval_jaxpr/psum | solution.py:152
  76.8 72.9 %collective-permute-start.1 = (bf16[256,512]{1,0:T(8,128)(2,1)}, bf16[256,512]{1,0:T(8,128)(2,1)S(1)}, u32[]{:S(2)}, u32[]{:S(2)}) collective-permute-start(bf16[256,512]{1,0:T(8,128)(2,1)} %get-tuple-element.1012), channel_id=1, source_target_pairs={{8,0},{16,8},{24,16},{9,1},{17,9},{25,17},{10,2},{18,10},{26,18},{... | collective-permute-start | bytes 786440 | tf_op jit(solution)/shard_map/while/body/eval_jaxpr/ppermute | solution.py:12
  87.2 61.5 %copy-start.11 = (f32[512,512]{1,0:T(8,128)S(1)}, f32[512,512]{1,0:T(8,128)}, u32[]{:S(2)}) copy-start(f32[512,512]{1,0:T(8,128)} %get-tuple-element.1052) | copy-start | bytes 3145732 | tf_op jit(solution)/shard_map/while
  146.0 2.8 copy-start.25
  147.5 3.4 collective-permute-start
  150.9 135.6 %all-reduce.3.cloned.1.call-start = ((), (), s32[]{:S(2)}) async-start(), calls=%async_computation.8 | async-start | bytes 1048576 | tf_op jit(solution)/shard_map/while/body/eval_jaxpr/psum | solution.py:152
  215.2 75.0 %collective-permute-start.1 = (bf16[256,512]{1,0:T(8,128)(2,1)}, bf16[256,512]{1,0:T(8,128)(2,1)S(1)}, u32[]{:S(2)}, u32[]{:S(2)}) collective-permute-start(bf16[256,512]{1,0:T(8,128)(2,1)} %get-tuple-element.1012), channel_id=1, source_target_pairs={{8,0},{16,8},{24,16},{9,1},{17,9},{25,17},{10,2},{18,10},{26,18},{... | collective-permute-start | bytes 786440 | tf_op jit(solution)/shard_map/while/body/eval_jaxpr/ppermute | solution.py:12
  216.5 2.9 copy-start.7
  227.3 62.0 %copy-start.11 = (f32[512,512]{1,0:T(8,128)S(1)}, f32[512,512]{1,0:T(8,128)}, u32[]{:S(2)}) copy-start(f32[512,512]{1,0:T(8,128)} %get-tuple-element.1052) | copy-start | bytes 3145732 | tf_op jit(solution)/shard_map/while
  286.5 2.8 copy-start.25
  288.0 3.4 collective-permute-start
  291.4 135.6 %all-reduce.3.cloned.1.call-start = ((), (), s32[]{:S(2)}) async-start(), calls=%async_computation.8 | async-start | bytes 1048576 | tf_op jit(solution)/shard_map/while/body/eval_jaxpr/psum | solution.py:152
  355.7 75.0 %collective-permute-start.1 = (bf16[256,512]{1,0:T(8,128)(2,1)}, bf16[256,512]{1,0:T(8,128)(2,1)S(1)}, u32[]{:S(2)}, u32[]{:S(2)}) collective-permute-start(bf16[256,512]{1,0:T(8,128)(2,1)} %get-tuple-element.1012), channel_id=1, source_target_pairs={{8,0},{16,8},{24,16},{9,1},{17,9},{25,17},{10,2},{18,10},{26,18},{... | collective-permute-start | bytes 786440 | tf_op jit(solution)/shard_map/while/body/eval_jaxpr/ppermute | solution.py:12
  357.0 2.9 copy-start.7
  367.8 62.0 %copy-start.11 = (f32[512,512]{1,0:T(8,128)S(1)}, f32[512,512]{1,0:T(8,128)}, u32[]{:S(2)}) copy-start(f32[512,512]{1,0:T(8,128)} %get-tuple-element.1052) | copy-start | bytes 3145732 | tf_op jit(solution)/shard_map/while
  427.0 2.8 copy-start.25
  428.5 3.4 collective-permute-start
  431.9 135.6 %all-reduce.3.cloned.1.call-start = ((), (), s32[]{:S(2)}) async-start(), calls=%async_computation.8 | async-start | bytes 1048576 | tf_op jit(solution)/shard_map/while/body/eval_jaxpr/psum | solution.py:152
  496.2 75.0 %collective-permute-start.1 = (bf16[256,512]{1,0:T(8,128)(2,1)}, bf16[256,512]{1,0:T(8,128)(2,1)S(1)}, u32[]{:S(2)}, u32[]{:S(2)}) collective-permute-start(bf16[256,512]{1,0:T(8,128)(2,1)} %get-tuple-element.1012), channel_id=1, source_target_pairs={{8,0},{16,8},{24,16},{9,1},{17,9},{25,17},{10,2},{18,10},{26,18},{... | collective-permute-start | bytes 786440 | tf_op jit(solution)/shard_map/while/body/eval_jaxpr/ppermute | solution.py:12
  497.5 2.9 copy-start.7
  508.3 62.0 %copy-start.11 = (f32[512,512]{1,0:T(8,128)S(1)}, f32[512,512]{1,0:T(8,128)}, u32[]{:S(2)}) copy-start(f32[512,512]{1,0:T(8,128)} %get-tuple-element.1052) | copy-start | bytes 3145732 | tf_op jit(solution)/shard_map/while
  569.0 3.4 collective-permute-start
  572.4 135.6 %all-reduce.3.cloned.1.call-start = ((), (), s32[]{:S(2)}) async-start(), calls=%async_computation.8 | async-start | bytes 1048576 | tf_op jit(solution)/shard_map/while/body/eval_jaxpr/psum | solution.py:152
  636.7 75.0 %collective-permute-start.1 = (bf16[256,512]{1,0:T(8,128)(2,1)}, bf16[256,512]{1,0:T(8,128)(2,1)S(1)}, u32[]{:S(2)}, u32[]{:S(2)}) collective-permute-start(bf16[256,512]{1,0:T(8,128)(2,1)} %get-tuple-element.1012), channel_id=1, source_target_pairs={{8,0},{16,8},{24,16},{9,1},{17,9},{25,17},{10,2},{18,10},{26,18},{... | collective-permute-start | bytes 786440 | tf_op jit(solution)/shard_map/while/body/eval_jaxpr/ppermute | solution.py:12
  638.0 2.9 copy-start.7
  648.8 62.0 %copy-start.11 = (f32[512,512]{1,0:T(8,128)S(1)}, f32[512,512]{1,0:T(8,128)}, u32[]{:S(2)}) copy-start(f32[512,512]{1,0:T(8,128)} %get-tuple-element.1052) | copy-start | bytes 3145732 | tf_op jit(solution)/shard_map/while
  708.0 2.8 copy-start.25
  709.5 3.4 collective-permute-start
  712.9 69.8 %reduce-scatter.5.cloned.1.call-start = ((), (), s32[]{:S(2)}) async-start(), calls=%async_computation.4 | async-start | bytes 1179648 | tf_op jit(solution)/shard_map/reduce_scatter | solution.py:190
  713.5 136.1 %reduce-scatter.7.cloned.1.call-start = ((), (), s32[]{:S(2)}) async-start(), calls=%async_computation.5 | async-start | bytes 1179648 | tf_op jit(solution)/shard_map/reduce_scatter | solution.py:191
  714.1 202.0 %reduce-scatter.9.cloned.1.call-start = ((), (), s32[]{:S(2)}) async-start(), calls=%async_computation.6 | async-start | bytes 1179648 | tf_op jit(solution)/shard_map/reduce_scatter | solution.py:192
  714.6 268.3 %reduce-scatter.11.cloned.1.call-start = ((), (), s32[]{:S(2)}) async-start(), calls=%async_computation.7 | async-start | bytes 1179648 | tf_op jit(solution)/shard_map/reduce_scatter | solution.py:193
  (147 other events, 170.4 us)
Sparse Core Ops, SparseCore 0:
  73.7 72.2 all-reduce.2
  212.1 74.3 all-reduce.2
  352.6 74.3 all-reduce.2
  493.1 74.3 all-reduce.2
  633.6 74.3 all-reduce.2
Sparse Core Ops, SparseCore 1:
  717.3 65.3 reduce-scatter.4
  786.9 62.6 reduce-scatter.6
  853.5 62.5 reduce-scatter.8
  920.4 62.4 reduce-scatter.10
where the time goes:
time: 998 us; the launch traced here: 990 us
  waiting for transfers between devices  567 us (57%)
  blocking collectives  199 us (20%)
  matrix products  118 us (12%)
  local copies, waits for them, and re-layouts  73.2 us (7%)
  between operations  15.5 us (2%)
  starting transfers between devices  13 us (1%)
    psum x5, waiting for transfers between devices, advance(): edge_terms = lax.psum(partial_back, 'edge')  296 us
    psum x5, blocking collectives, advance(): aggregate = lax.psum(partial_agg, 'edge')  199 us
    reduce_scatter x1, waiting for transfers between devices, body(): lax.psum_scatter(sum_recv, 'edge', scatter_dimension=0, tiled=True)  66.9 us
    reduce_scatter x1, waiting for transfers between devices, body(): lax.psum_scatter(sum_msg, 'edge', scatter_dimension=0, tiled=True)  66.9 us
    reduce_scatter x1, waiting for transfers between devices, body(): lax.psum_scatter(sum_edge, 'edge', scatter_dimension=0, tiled=True)  66.4 us
    reduce_scatter x1, waiting for transfers between devices, body(): lax.psum_scatter(sum_send, 'edge', scatter_dimension=0, tiled=True)  62.6 us
    while x310, local copies, waits for them, and re-layouts  54.1 us
    dot_general x35, matrix products, transposed_times(): lax.dot_general(left, right, (((0,), (0,)), ((), ())), preferred_element_...  38.6 us
  transfers between devices with their start and end apart: 19, of which 14 were waited for; matrix products, arithmetic and copies ran while one was open for 6% of the time, Pallas kernels for 0%

commit v1 on v0

v1 whole, which is shorter than its diff:
```python
import functools

import jax
import jax.numpy as jnp
from jax import lax
from jax.experimental import pallas as pl
from jax.experimental.pallas import tpu as pltpu
from jax.sharding import PartitionSpec as P

BLOCK = 128
PARTS = 2
PAD = 16
BF = jnp.bfloat16
F32 = jnp.float32
ANY = pl.BlockSpec(memory_space=pl.ANY)
SMEM = pl.BlockSpec(memory_space=pltpu.SMEM)
VMEM = pl.BlockSpec(memory_space=pltpu.VMEM)


def matmul(left, right):
    return jnp.dot(left, right, preferred_element_type=F32)


def times_transposed(left, right):
    return lax.dot_general(left, right, (((1,), (1,)), ((), ())), preferred_element_type=F32)


def transposed_times(left, right):
    return lax.dot_general(left, right, (((0,), (0,)), ((), ())), preferred_element_type=F32)


class Copies:
    def __init__(self, sems):
        self.sems = sems
        self.count = 0

    def start(self, source, target):
        copy = pltpu.make_async_copy(source, target, self.sems.at[self.count])
        self.count += 1
        copy.start()
        return copy


def base_of(half, span, batches):
    return jnp.where(half == 0, span - batches, 0)


def place_of(batch, half, span, batches):
    return (span - batches if half == 0 else 0) + batch


def worker_of(batch, half, span, batches):
    return half * span + place_of(batch, half, span, batches)


def own_batch(member, span, batches):
    half = lax.div(member, span)
    batch = lax.rem(member, span) - base_of(half, span, batches)
    return jnp.clip(batch, 0, batches - 1)


def pick_row(table, row, lanes):
    value = table[0:1, lanes]
    for other in range(1, table.shape[0]):
        value = jnp.where(row == other, table[other : other + 1, lanes], value)
    return value


def hot_rows(index_rows, row, nodes):
    index = index_rows[row : row + 1, :]
    rows = lax.broadcasted_iota(jnp.int32, (nodes, index_rows.shape[1]), 0)
    return jnp.where(rows == index, 1.0, 0.0).astype(BF)


def pack_kernel(span, batches, info, senders, receivers, tiles, edges, *refs):
    index_out = refs[0]
    outs = refs[1 : 1 + span - 1]
    rows, sems = refs[span:]
    copies = Copies(sems)
    member = info[1]
    half = lax.div(member, span)
    offset = lax.rem(member, span)
    count = senders.shape[1]
    tile_count = tiles.shape[1]
    tile_len = count // tile_count
    waits = []
    picks = []
    for step in range(span):
        batch = lax.rem(offset - step + span, span) - base_of(half, span, batches)
        batch = jnp.clip(batch, 0, batches - 1)
        picks.append(batch)
        if step:
            waits.append(copies.start(edges.at[0, batch], outs[step - 1].at[pl.ds(0, count)]))
    rows[...] = jnp.zeros_like(rows)
    for step in range(span):
        batch = picks[step]
        for tile in range(tile_count):
            lanes = slice(tile * tile_len, (tile + 1) * tile_len)
            send = pick_row(senders, batch, lanes) + tiles[batch, tile, 0] * BLOCK
            recv = pick_row(receivers, batch, lanes) + tiles[batch, tile, 1] * BLOCK
            which = lax.broadcasted_iota(jnp.int32, (PAD, tile_len), 0)
            block = jnp.where(which == 0, send, jnp.where(which == 1, recv, 0))
            rows[step, :, lanes] = block.astype(F32).astype(BF)
        target = index_out if step == 0 else outs[step - 1].at[pl.ds(count, PAD)]
        waits.append(copies.start(rows.at[step], target))
    for wait in waits:
        wait.wait()


def forward_kernel(span, batches, info, nodes, edges, own_index, *refs):
    others = refs[: span - 1]
    w_send, w_recv, w_edge, w_msg = refs[span - 1 : span + 3]
    act_out, slope_out, part_out, index_out = refs[span + 3 : span + 7]
    feats, pieces, weights, hidden, acts, slopes, part, sems = refs[span + 7 :]
    copies = Copies(sems)
    batch = own_batch(info[1], span, batches)
    count = edges.shape[2]
    node_count = nodes.shape[2]
    get_feats = copies.start(nodes.at[0, batch], feats)
    get_w = [copies.start(w.at[0], weights.at[k]) for k, w in enumerate((w_send, w_recv, w_edge, w_msg))]
    get_piece = [
        [
            copies.start(edges.at[0, batch], pieces.at[0, pl.ds(0, count)]),
            copies.start(own_index, pieces.at[0, pl.ds(count, PAD)]),
        ]
    ]
    for step in range(1, span):
        get_piece.append([copies.start(others[step - 1], pieces.at[step])])
    get_feats.wait()
    get_w[0].wait()
    hidden[:node_count] = matmul(feats[...], weights[0]).astype(BF)
    get_w[1].wait()
    hidden[node_count:] = matmul(feats[...], weights[1]).astype(BF)
    get_w[2].wait()
    puts = []
    total = None
    for step in range(span):
        for get in get_piece[step]:
            get.wait()
        puts.append(copies.start(pieces.at[step, pl.ds(count, PAD)], index_out.at[step]))
        index_rows = pieces[step, count : count + PAD, :count].astype(F32).astype(jnp.int32)
        send_hot = hot_rows(index_rows, 0, node_count)
        recv_hot = hot_rows(index_rows, 1, node_count)
        both = jnp.concatenate([send_hot, recv_hot], axis=0)
        pre = transposed_times(both, hidden[...]) + matmul(pieces[step, :count], weights[2])
        sigma = jax.nn.sigmoid(pre)
        act = (pre * sigma).astype(BF)
        acts[step * count : (step + 1) * count] = act
        slopes[step * count : (step + 1) * count] = (sigma * (1.0 + pre * (1.0 - sigma))).astype(BF)
        run = pl.ds(step * count, count)
        puts.append(copies.start(acts.at[run], act_out.at[run]))
        puts.append(copies.start(slopes.at[run], slope_out.at[run]))
        added = matmul(recv_hot, act)
        total = added if total is None else total + added
    get_w[3].wait()
    part[...] = matmul(total.astype(BF), weights[3]).astype(BF)
    puts.append(copies.start(part, part_out))
    for put in puts:
        put.wait()


def node_kernel(span, batches, info, nodes, part_own, part_other, w_node, w_agg, out):
    batch = own_batch(info[1], span, batches)
    count = nodes.shape[2]
    agg = (part_own[...].astype(F32) + part_other[...].astype(F32)).astype(BF)
    pre = matmul(nodes[0, batch], w_node[0]) + matmul(agg, w_agg[0])
    sigma = jax.nn.sigmoid(pre)
    out[:count] = agg
    out[count : 2 * count] = (pre * sigma).astype(BF)
    out[2 * count :] = (sigma * (1.0 + pre * (1.0 - sigma))).astype(BF)


def chain_kernel(span, batches, count, active, info, *refs):
    if active is None:
        chain_step(span, batches, count, True, info, *refs)
    else:
        refs = refs[:2] + refs[4:]

        @pl.when(info[0] == active)
        def _():
            chain_step(span, batches, count, False, info, *refs)


def chain_step(span, batches, count, first, info, *refs):
    if first:
        top_nodes, top_edges = refs[:2]
        others = refs[2 : span + 1]
        refs = refs[span + 1 :]
    else:
        came, cross = refs[:2]
        refs = refs[2:]
    index, slope, node_pack = refs[:3]
    w_out, w_agg, w_msg, w_edge, w_node, w_send, w_recv = refs[3:10]
    pay_out, part_out, keep_out = refs[10:13]
    grad_a, grad_b, pay, rows, slopes, node_slope, weights, hots, keep, sems = refs[13:]
    copies = Copies(sems)
    member = info[1]
    batch = own_batch(member, span, batches)
    half = lax.div(member, span)
    node_count = grad_a.shape[0]
    total = span * count
    if first:
        get_grad = [copies.start(top_nodes.at[batch], grad_a)]
    else:
        get_grad = [copies.start(came.at[pl.ds(total, node_count)], grad_a), copies.start(cross, grad_b)]
    get_w = {}

    def fetch(slot, ref):
        get_w[slot] = copies.start(ref.at[0], weights.at[slot])

    fetch(0, w_out)
    get_slope_n = copies.start(node_pack.at[pl.ds(2 * node_count, node_count)], node_slope)
    fetch(1, w_agg)
    get_index = copies.start(index, rows)
    fetch(2, w_msg)
    get_edge, get_slope = [], []
    for step in range(span):
        run = pl.ds(step * count, count)
        if first:
            source = top_edges.at[batch] if step == 0 else others[step - 1]
        else:
            source = came.at[run]
        get_edge.append(copies.start(source, pay.at[run]))
        get_slope.append(copies.start(slope.at[run], slopes.at[run]))
        if step == 0:
            fetch(3, w_edge)
    fetch(4, w_node)
    fetch(5, w_send)
    fetch(6, w_recv)
    puts = []

    for get in get_grad:
        get.wait()
    if first:
        grad = grad_a[...]
    else:
        grad = (grad_a[...].astype(F32) + grad_b[...].astype(F32)).astype(BF)
    node_at = 2 * total
    get_w[0].wait()
    get_slope_n.wait()
    delta = (times_transposed(grad, weights[0]) * node_slope[...].astype(F32)).astype(BF)
    get_w[1].wait()
    agg_grad = times_transposed(delta, weights[1]).astype(BF)
    keep[node_at : node_at + node_count] = delta
    keep[node_at + node_count : node_at + 2 * node_count] = grad
    get_index.wait()
    get_w[2].wait()
    for step in range(span):
        at = step * count
        run = slice(at, at + count)
        index_rows = rows[step, :, :count].astype(F32).astype(jnp.int32)
        send_hot = hot_rows(index_rows, 0, node_count)
        recv_hot = hot_rows(index_rows, 1, node_count)
        hots[:node_count, run] = send_hot
        hots[node_count:, run] = recv_hot
        get_edge[step].wait()
        incoming = pay[run].astype(F32)
        spread = transposed_times(recv_hot, agg_grad)
        message_grad = (incoming + spread).astype(BF)
        keep[run] = message_grad
        get_slope[step].wait()
        edge_delta = (times_transposed(message_grad, weights[2]) * slopes[run].astype(F32)).astype(BF)
        keep[total + at : total + at + count] = edge_delta
        if step == 0:
            get_w[3].wait()
        pay[run] = (incoming + times_transposed(edge_delta, weights[3])).astype(BF)
        piece = pl.ds(at, count)
        puts.append(copies.start(pay.at[piece], pay_out.at[piece]))
    sums = matmul(hots[...], keep[total : 2 * total]).astype(BF)
    keep[node_at + 2 * node_count :] = sums
    get_w[4].wait()
    get_w[5].wait()
    get_w[6].wait()
    own = grad.astype(F32) + times_transposed(delta, weights[4])
    own = own * jnp.where(half == 0, 1.0, 0.0)
    part = times_transposed(sums[:node_count], weights[5]) + times_transposed(sums[node_count:], weights[6])
    pay[total:] = (own + part).astype(BF)
    tail = pl.ds(total, node_count)
    puts.append(copies.start(pay.at[tail], pay_out.at[tail]))
    puts.append(copies.start(pay.at[tail], part_out))
    puts.append(copies.start(keep, keep_out))
    for put in puts:
        put.wait()


def grads_kernel(span, batches, groups, info, nodes, edges, *refs):
    others = refs[: span - 1]
    act, node_pack = refs[span - 1 : span + 1]
    kept, paid = refs[span + 1 : span + 3]
    refs = refs[span + 3 :]
    blocks = refs[:groups]
    returns = refs[groups : groups + span]
    feats, pieces, acts, packs, keep, part, sums, sems = refs[groups + span :]
    copies = Copies(sems)
    member = info[1]
    batch = own_batch(member, span, batches)
    half = lax.div(member, span)
    count = edges.shape[2]
    node_count = nodes.shape[2]
    width = nodes.shape[3]
    total = span * count
    gets = [copies.start(nodes.at[0, batch], feats), copies.start(node_pack, packs), copies.start(act, acts)]
    gets.append(copies.start(edges.at[0, batch], pieces.at[0]))
    for step in range(1, span):
        gets.append(copies.start(others[step - 1].at[pl.ds(0, count)], pieces.at[step]))
    gets.append(copies.start(kept, keep))
    gets.append(copies.start(paid.at[pl.ds(total, node_count)], part))
    puts = [copies.start(paid.at[pl.ds(step * count, count)], returns[step]) for step in range(span)]
    for get in gets:
        get.wait()
    node_at = 2 * total
    delta = keep[node_at : node_at + node_count]
    grad = keep[node_at + node_count : node_at + 2 * node_count]
    sent = keep[node_at + 2 * node_count : node_at + 3 * node_count]
    received = keep[node_at + 3 * node_count :]
    sums[0] = transposed_times(feats[...], sent).astype(BF)
    sums[1] = transposed_times(feats[...], received).astype(BF)
    edge_sum = None
    for step in range(span):
        added = transposed_times(pieces[step], keep[total + step * count : total + (step + 1) * count])
        edge_sum = added if edge_sum is None else edge_sum + added
    sums[2] = edge_sum.astype(BF)
    sums[3] = transposed_times(acts[...], keep[:total]).astype(BF)
    sums[5] = transposed_times(packs[:node_count], delta).astype(BF)

    @pl.when(half == 0)
    def _():
        sums[4] = transposed_times(feats[...], delta).astype(BF)

    @pl.when(half != 0)
    def _():
        sums[4] = transposed_times(packs[node_count : 2 * node_count], grad).astype(BF)

    share = width // groups
    node_share = node_count // groups
    for step in range(groups):
        owner = lax.rem(member + step, groups)
        at = pl.multiple_of(owner * share, share)
        for slot in range(5):
            puts.append(copies.start(sums.at[slot, pl.ds(at, share)], blocks[step].at[pl.ds(slot * share, share)]))
        at_half = pl.multiple_of(owner * share + half * (share // 2), share // 2)
        puts.append(
            copies.start(sums.at[5, pl.ds(at_half, share // 2)], blocks[step].at[pl.ds(5 * share, share // 2)])
        )
        at_node = pl.multiple_of(owner * node_share, node_share)
        puts.append(
            copies.start(
                part.at[pl.ds(at_node, node_share)], blocks[step].at[pl.ds(5 * share + share // 2, node_share)]
            )
        )
    for put in puts:
        put.wait()


def finish_kernel(span, batches, groups, info, *refs):
    blocks = refs[:groups]
    returns = refs[groups : groups + span]
    refs = refs[groups + span :]
    nodes_out, edges_out, send_out, recv_out, edge_out, msg_out, node_out, agg_out, out_out = refs[:9]
    held, sems = refs[9:]
    copies = Copies(sems)
    member = info[1]
    half = lax.div(member, span)
    offset = lax.rem(member, span)
    back_sems = copies.count
    copies.count += batches
    for batch in range(batches):
        turn = lax.rem(offset - base_of(half, span, batches) - batch + 2 * span, span)
        for step in range(span):

            @pl.when(turn == step)
            def _(batch=batch, step=step):
                pltpu.make_async_copy(returns[step], edges_out.at[0, batch], sems.at[back_sems + batch]).start()

    for batch in range(batches):
        for part in range(PARTS):
            worker = worker_of(batch, part, span, batches)
            turn = lax.rem(member - worker + groups, groups)
            slot = copies.count
            copies.count += 1
            for step in range(groups):

                @pl.when(turn == step)
                def _(batch=batch, part=part, step=step, slot=slot):
                    pltpu.make_async_copy(blocks[step], held.at[batch, part], sems.at[slot]).start()

            pltpu.make_async_copy(blocks[0], held.at[batch, part], sems.at[slot]).wait()
    share = send_out.shape[1]
    for slot, out in enumerate((send_out, recv_out, edge_out, msg_out)):
        rows = slice(slot * share, (slot + 1) * share)
        value = None
        for batch in range(batches):
            for part in range(PARTS):
                piece = held[batch, part, rows].astype(F32)
                value = piece if value is None else value + piece
        out[0] = value

    def over_batches(part, start, length):
        value = None
        for batch in range(batches):
            piece = held[batch, part, start : start + length].astype(F32)
            value = piece if value is None else value + piece
        return value

    node_out[0] = over_batches(0, 4 * share, share)
    out_out[0] = over_batches(1, 4 * share, share)
    for part in range(PARTS):
        agg_out[0, part * (share // 2) : (part + 1) * (share // 2)] = over_batches(part, 5 * share, share // 2)
    at = 5 * share + share // 2
    for batch in range(batches):
        rows = held[batch, 0, at:].astype(F32) + held[batch, 1, at:].astype(F32)
        nodes_out[0, batch] = rows.astype(BF)
    for batch in range(batches):
        pltpu.make_async_copy(returns[0], edges_out.at[0, batch], sems.at[back_sems + batch]).wait()


def call(kernel, name, in_specs, out_shapes, out_specs, scratch, flops, touched, aliases={}):
    return pl.pallas_call(
        kernel,
        name=name,
        out_shape=out_shapes,
        in_specs=in_specs,
        out_specs=out_specs,
        scratch_shapes=scratch,
        input_output_aliases=aliases,
        compiler_params=pltpu.CompilerParams(vmem_limit_bytes=48 * 1024 * 1024),
        cost_estimate=pl.CostEstimate(flops=flops, bytes_accessed=touched, transcendentals=0),
    )


def body(
    layer_nodes,
    layer_edges,
    top_nodes,
    top_edges,
    tile_blocks,
    senders,
    receivers,
    w_send,
    w_recv,
    w_edge,
    w_msg,
    w_node,
    w_agg,
    w_out,
):
    sections = lax.axis_size("section")
    groups = lax.axis_size("edge")
    section = lax.axis_index("section")
    member = lax.axis_index("edge")
    span = groups // PARTS
    _, batches, node_count, width = layer_nodes.shape
    count = layer_edges.shape[2]
    total = span * count
    share = width // groups
    node_share = node_count // groups
    info = jnp.stack([section, member]).astype(jnp.int32)
    axes = ("section", "edge")
    works = [(m, h) for h in range(PARTS) for m in range(batches)]

    def worker(m, h):
        return worker_of(m, h, span, batches)

    def source(m, h, step):
        return h * span + (place_of(m, h, span, batches) + step) % span

    def move(value, layers, links, shift=0):
        pairs = [(s * groups + a, (s + shift) * groups + b) for s in layers for a, b in links]
        return lax.ppermute(value, axes, pairs)

    every = list(range(sections))
    last = [sections - 1]
    collect = [[(source(m, h, step), worker(m, h)) for m, h in works] for step in range(span)]
    deliver = [[(b, a) for a, b in links] for links in collect]

    def like(rows, cols=width, kind=BF):
        return jax.ShapeDtypeStruct((rows, cols), kind)

    def sems(n):
        return pltpu.SemaphoreType.DMA((n,))

    packed = call(
        functools.partial(pack_kernel, span, batches),
        "pack",
        [SMEM, VMEM, VMEM, SMEM, ANY],
        [like(PAD)] + [like(count + PAD)] * (span - 1),
        [ANY] * span,
        [pltpu.VMEM((span, PAD, width), BF), sems(2 * span)],
        0,
        2**20,
    )(info, senders, receivers, tile_blocks, layer_edges)
    own_index, pieces = packed[0], packed[1:]
    pieces = [move(piece, every, collect[step + 1]) for step, piece in enumerate(pieces)]
    half = member // span
    offset = member % span
    tops = []
    for step in range(1, span):
        pick = jnp.clip((offset - step) % span - base_of(half, span, batches), 0, batches - 1)
        tops.append(
            move(lax.dynamic_index_in_dim(top_edges, pick, 0, keepdims=False), last, collect[step])
        )

    act, slope, part, index = call(
        functools.partial(forward_kernel, span, batches),
        "forward",
        [SMEM] + [ANY] * (span + 6),
        [like(total), like(total), like(node_count), jax.ShapeDtypeStruct((span, PAD, width), BF)],
        [ANY] * 4,
        [
            pltpu.VMEM((node_count, width), BF),
            pltpu.VMEM((span, count + PAD, width), BF),
            pltpu.VMEM((4, width, width), BF),
            pltpu.VMEM((2 * node_count, width), BF),
            pltpu.VMEM((total, width), BF),
            pltpu.VMEM((total, width), BF),
            pltpu.VMEM((node_count, width), BF),
            sems(8 + 5 * span),
        ],
        2 * 10**9,
        6 * 2**20,
    )(info, layer_nodes, layer_edges, own_index, *pieces, w_send, w_recv, w_edge, w_msg)

    swap = [(worker(m, h), worker(m, 1 - h)) for m, h in works]
    part_other = move(part, every, swap)
    node_pack = call(
        functools.partial(node_kernel, span, batches),
        "node_forward",
        [SMEM] + [VMEM] * 5,
        like(3 * node_count),
        VMEM,
        [],
        3 * 10**8,
        3 * 2**20,
    )(info, layer_nodes, part, part_other, w_node, w_agg)

    pay = keep = None
    incoming = None
    for moment in range(sections):
        first = moment == 0
        inputs = (top_nodes, top_edges, *tops) if first else (*incoming, pay, keep)
        pay, part, keep = call(
            functools.partial(chain_kernel, span, batches, count, None if first else sections - 1 - moment),
            "chain",
            [SMEM] + [ANY] * (len(inputs) + 10),
            [like(total + node_count), like(node_count), like(2 * total + 4 * node_count)],
            [ANY] * 3,
            [
                pltpu.VMEM((node_count, width), BF),
                pltpu.VMEM((node_count, width), BF),
                pltpu.VMEM((total + node_count, width), BF),
                pltpu.VMEM((span, PAD, width), BF),
                pltpu.VMEM((total, width), BF),
                pltpu.VMEM((node_count, width), BF),
                pltpu.VMEM((7, width, width), BF),
                pltpu.VMEM((2 * node_count, total), BF),
                pltpu.VMEM((2 * total + 4 * node_count, width), BF),
                sems(16 + 3 * span),
            ],
            3 * 10**9,
            10 * 2**20,
            {} if first else {3: 0, 4: 2},
        )(info, *inputs, index, slope, node_pack, w_out, w_agg, w_msg, w_edge, w_node, w_send, w_recv)
        if moment < sections - 1:
            here = [sections - 1 - moment]
            cross = move(part, here, swap, -1)
            came = move(pay, here, [(worker(m, h), worker(m, h)) for m, h in works], -1)
            incoming = (came, cross)

    rows = 5 * share + share // 2 + node_share
    out = call(
        functools.partial(grads_kernel, span, batches, groups),
        "weight_grads",
        [SMEM] + [ANY] * (span + 5),
        [like(rows)] * groups + [like(count)] * span,
        [ANY] * (groups + span),
        [
            pltpu.VMEM((node_count, width), BF),
            pltpu.VMEM((span, count, width), BF),
            pltpu.VMEM((total, width), BF),
            pltpu.VMEM((3 * node_count, width), BF),
            pltpu.VMEM((2 * total + 4 * node_count, width), BF),
            pltpu.VMEM((node_count, width), BF),
            pltpu.VMEM((6, width, width), BF),
            sems(5 + 2 * span + 7 * groups),
        ],
        2 * 10**9,
        10 * 2**20,
    )(info, layer_nodes, layer_edges, *pieces, act, node_pack, keep, pay)
    blocks, returns = out[:groups], out[groups:]
    blocks = [blocks[0]] + [
        move(blocks[step], every, [(worker(m, h), (worker(m, h) + step) % groups) for m, h in works])
        for step in range(1, groups)
    ]
    returns = [returns[0]] + [move(returns[step], every, deliver[step]) for step in range(1, span)]
    grad_shape = jax.ShapeDtypeStruct((1, share, width), F32)
    return call(
        functools.partial(finish_kernel, span, batches, groups),
        "finish",
        [SMEM] + [ANY] * (groups + span),
        [
            jax.ShapeDtypeStruct((1, batches, node_share, width), BF),
            jax.ShapeDtypeStruct((1, batches, count, width), BF),
        ]
        + [grad_shape] * 7,
        [VMEM, ANY] + [VMEM] * 7,
        [pltpu.VMEM((batches, PARTS, rows, width), BF), sems(batches + batches * PARTS)],
        0,
        5 * 2**20,
    )(info, *blocks, *returns)


def solution(mesh):
    in_specs = (
        P("section", None, None, None),
        P("section", None, "edge", None),
        P(),
        P(None, "edge", None),
        P(None, "edge", None),
        P(None, "edge"),
        P(None, "edge"),
        P("section", None, None),
        P("section", None, None),
        P("section", None, None),
        P("section", None, None),
        P("section", None, None),
        P("section", None, None),
        P("section", None, None),
    )
    out_specs = (
        P("section", None, "edge", None),
        P("section", None, "edge", None),
        P("section", "edge", None),
        P("section", "edge", None),
        P("section", "edge", None),
        P("section", "edge", None),
        P("section", "edge", None),
        P("section", "edge", None),
        P("section", "edge", None),
    )
    return jax.shard_map(body, mesh=mesh, in_specs=in_specs, out_specs=out_specs, check_vma=False)
```

time: 998 us -> 190 us (0.19)
  the two profiles are of different devices: /device:TPU:26 before, /device:TPU:10 now
where the time goes in v1:
time: 190 us; the launch traced here: 189 us
  waiting for transfers between devices  84.8 us (45%)
  starting transfers between devices  48.8 us (26%)
  Pallas kernels  40.3 us (21%)
  local copies, waits for them, and re-layouts  13.7 us (7%)
    ppermute x23, waiting for transfers between devices, move(): return lax.ppermute(value, axes, pairs)  84.8 us
    ppermute x23, starting transfers between devices, move(): return lax.ppermute(value, axes, pairs)  48.8 us
    pallas_call x4, Pallas kernels, body(): call(functools.partial(chain_kernel, span, batches, count, None if first...  20.1 us
    unnamed x56, local copies, waits for them, and re-layouts  13.7 us
    pallas_call x1, Pallas kernels, body(): call(functools.partial(grads_kernel, span, batches, groups), 'weight_grad...  10.4 us
    pallas_call x1, Pallas kernels, body(): call(functools.partial(forward_kernel, span, batches), 'forward', [SMEM]...  5.11 us
  transfers between devices with their start and end apart: 23, of which 10 were waited for; matrix products, arithmetic and copies ran while one was open for 0% of the time, Pallas kernels for 1%

profile of v1, /device:TPU:10, one launch (start us, length us, event | category | flops | bytes accessed | tf_op | source)
XLA Modules:
  0.0 189.1 jit_solution(16859941625232028434)
XLA Ops:
  4.7 2.4 %collective-permute-start = (bf16[272,512]{1,0:T(8,128)(2,1)S(1)}, bf16[272,512]{1,0:T(8,128)(2,1)S(1)}, u32[]{:S(2)}, u32[]{:S(2)}) collective-permute-start(bf16[272,512]{1,0:T(8,128)(2,1)S(1)} %get-tuple-element.40), channel_id=1, source_target_pairs={{3,2},{0,3},{5,4},{6,5},{11,10},{8,11},{13,12},{14,13},{19,18},{16... | collective-permute-start | bytes 835592 | tf_op jit(solution)/shard_map/ppermute | solution.py:469
  7.1 1.3 collective-permute-start.1
  8.4 1.3 collective-permute-start.2
  9.8 7.2 %collective-permute-done.refs_0_ = bf16[272,512]{1,0:T(8,128)(2,1)S(1)} collective-permute-done((bf16[272,512]{1,0:T(8,128)(2,1)S(1)}, bf16[272,512]{1,0:T(8,128)(2,1)S(1)}, u32[]{:S(2)}, u32[]{:S(2)}) %collective-permute-start) | collective-permute-done | bytes 278560 | tf_op jit(solution)/shard_map/ppermute | solution.py:469
  17.1 1.5 collective-permute-done.1.refs_1_
  18.6 3.2 %collective-permute-done.2.refs_2_ = bf16[272,512]{1,0:T(8,128)(2,1)S(1)} collective-permute-done((bf16[272,512]{1,0:T(8,128)(2,1)S(1)}, bf16[272,512]{1,0:T(8,128)(2,1)S(1)}, u32[]{:S(2)}, u32[]{:S(2)}) %collective-permute-start.2) | collective-permute-done | bytes 278560 | tf_op jit(solution)/shard_map/ppermute | solution.py:469
  28.1 5.1 %forward.1 = (bf16[1024,512]{1,0:T(8,128)(2,1)S(1)}, bf16[1024,512]{1,0:T(8,128)(2,1)}, bf16[256,512]{1,0:T(8,128)(2,1)S(1)}, bf16[4,16,512]{2,1,0:T(8,128)(2,1)S(1)}) custom-call(s32[2]{0:T(128)S(1)} %pad_add_fusion.info, bf16[1,2,256,512]{3,2,1,0:T(8,128)(2,1)S(1)} %copy-done.17, bf16[1,2,256,512]{3,2,1,0:T(8,128)(2,1)S(1)} %copy-done.15, ...), custom_call_target="tpu_custom_call" | custom-call | flops 2000000000 | bytes 6291456 | tf_op jit(solution)/shard_map/forward/pallas_call | solution.py:503
  33.3 3.8 %collective-permute-start.3 = (bf16[256,512]{1,0:T(8,128)(2,1)S(1)}, bf16[256,512]{1,0:T(8,128)(2,1)S(1)}, u32[]{:S(2)}, u32[]{:S(2)}) collective-permute-start(bf16[256,512]{1,0:T(8,128)(2,1)S(1)} %get-tuple-element.45.part_own), channel_id=1, source_target_pairs={{2,4},{3,5},{4,2},{5,3},{10,12},{11,13},{12,10},{13,11},{18,20},{1... | collective-permute-start | bytes 786440 | tf_op jit(solution)/shard_map/ppermute | solution.py:469
  39.4 4.3 %collective-permute-done.3.part_other = bf16[256,512]{1,0:T(8,128)(2,1)S(1)} collective-permute-done((bf16[256,512]{1,0:T(8,128)(2,1)S(1)}, bf16[256,512]{1,0:T(8,128)(2,1)S(1)}, u32[]{:S(2)}, u32[]{:S(2)}) %collective-permute-start.3) | collective-permute-done | bytes 262176 | tf_op jit(solution)/shard_map/ppermute | solution.py:469
  45.8 9.0 %chain.4 = (bf16[1280,512]{1,0:T(8,128)(2,1)}, bf16[256,512]{1,0:T(8,128)(2,1)S(1)}, bf16[3072,512]{1,0:T(8,128)(2,1)}) custom-call(s32[2]{0:T(128)S(1)} %pad_add_fusion.info, bf16[2,256,512]{2,1,0:T(8,128)(2,1)S(1)} %copy-done.24, bf16[2,256,512]{2,1,0:T(8,128)(2,1)S(1)} %copy-done.19, bf16[256,512]{1,0:T(8,128)(2,1)S(1)} %collective-permute-done.4.refs_2_, ...), custom_call_target="tpu_custom_call" | custom-call | flops 3000000000 | bytes 10485760 | tf_op jit(solution)/shard_map/chain/pallas_call | solution.py:541
  56.3 1.1 copy-done.26
  59.8 1.1 copy-done.27
  61.7 1.3 collective-permute-start.11
  63.0 1.3 collective-permute-start.12
  64.3 50.9 %collective-permute-done.12.refs_1_ = bf16[256,512]{1,0:T(8,128)(2,1)S(1)} collective-permute-done((bf16[256,512]{1,0:T(8,128)(2,1)S(1)}, bf16[256,512]{1,0:T(8,128)(2,1)S(1)}, u32[]{:S(2)}, u32[]{:S(2)}) %collective-permute-start.12) | collective-permute-done | bytes 262176 | tf_op jit(solution)/shard_map/ppermute | solution.py:469
  115.2 1.1 copy-done.25
  116.3 9.3 %chain.7 = (bf16[1280,512]{1,0:T(8,128)(2,1)}, bf16[256,512]{1,0:T(8,128)(2,1)}, bf16[3072,512]{1,0:T(8,128)(2,1)}) custom-call(s32[2]{0:T(128)S(1)} %pad_add_fusion.info, bf16[1280,512]{1,0:T(8,128)(2,1)} %copy-done.25, bf16[256,512]{1,0:T(8,128)(2,1)S(1)} %collective-permute-done.12.refs_1_, ...), custom_call_target="tpu_custom_call", output_to_operand_aliasing={{0}: (3, {}), {2}: (4, {})} | custom-call | flops 3000000000 | bytes 10485760 | tf_op jit(solution)/shard_map/chain/pallas_call | solution.py:541
  125.7 10.4 %weight_grads.1 = (bf16[384,512]{1,0:T(8,128)(2,1)S(1)}, bf16[384,512]{1,0:T(8,128)(2,1)S(1)}, bf16[384,512]{1,0:T(8,128)(2,1)S(1)}, bf16[384,512]{1,0:T(8,128)(...) custom-call(s32[2]{0:T(128)S(1)} %pad_add_fusion.info, ...), custom_call_target="tpu_custom_call" | custom-call | flops 2000000000 | bytes 10485760 | tf_op jit(solution)/shard_map/weight_grads/pallas_call | solution.py:570
  136.1 1.9 %collective-permute-start.13 = (bf16[384,512]{1,0:T(8,128)(2,1)S(1)}, bf16[384,512]{1,0:T(8,128)(2,1)S(1)}, u32[]{:S(2)}, u32[]{:S(2)}) collective-permute-start(bf16[384,512]{1,0:T(8,128)(2,1)S(1)} %get-tuple-element.60), channel_id=1, source_target_pairs={{2,3},{3,4},{4,5},{5,6},{10,11},{11,12},{12,13},{13,14},{18,19},{1... | collective-permute-start | bytes 1179656 | tf_op jit(solution)/shard_map/ppermute | solution.py:469
  138.0 2.4 %collective-permute-start.14 = (bf16[384,512]{1,0:T(8,128)(2,1)S(1)}, bf16[384,512]{1,0:T(8,128)(2,1)S(1)}, u32[]{:S(2)}, u32[]{:S(2)}) collective-permute-start(bf16[384,512]{1,0:T(8,128)(2,1)S(1)} %get-tuple-element.61), channel_id=1, source_target_pairs={{2,4},{3,5},{4,6},{5,7},{10,12},{11,13},{12,14},{13,15},{18,20},{1... | collective-permute-start | bytes 1179656 | tf_op jit(solution)/shard_map/ppermute | solution.py:469
  140.4 1.9 %collective-permute-start.20 = (bf16[256,512]{1,0:T(8,128)(2,1)S(1)}, bf16[256,512]{1,0:T(8,128)(2,1)S(1)}, u32[]{:S(2)}, u32[]{:S(2)}) collective-permute-start(bf16[256,512]{1,0:T(8,128)(2,1)S(1)} %get-tuple-element.68), channel_id=1, source_target_pairs={{2,3},{3,0},{4,5},{5,6},{10,11},{11,8},{12,13},{13,14},{18,19},{19... | collective-permute-start | bytes 786440 | tf_op jit(solution)/shard_map/ppermute | solution.py:469
  142.4 1.3 collective-permute-start.21
  143.7 3.9 %collective-permute-start.22 = (bf16[256,512]{1,0:T(8,128)(2,1)S(1)}, bf16[256,512]{1,0:T(8,128)(2,1)S(1)}, u32[]{:S(2)}, u32[]{:S(2)}) collective-permute-start(bf16[256,512]{1,0:T(8,128)(2,1)S(1)} %get-tuple-element.70), channel_id=1, source_target_pairs={{2,1},{3,2},{4,7},{5,4},{10,9},{11,10},{12,15},{13,12},{18,17},{19... | collective-permute-start | bytes 786440 | tf_op jit(solution)/shard_map/ppermute | solution.py:469
  147.6 8.1 %collective-permute-done.20.refs_9_ = bf16[256,512]{1,0:T(8,128)(2,1)S(1)} collective-permute-done((bf16[256,512]{1,0:T(8,128)(2,1)S(1)}, bf16[256,512]{1,0:T(8,128)(2,1)S(1)}, u32[]{:S(2)}, u32[]{:S(2)}) %collective-permute-start.20) | collective-permute-done | bytes 262176 | tf_op jit(solution)/shard_map/ppermute | solution.py:469
  155.7 12.5 %collective-permute-start.15 = (bf16[384,512]{1,0:T(8,128)(2,1)S(1)}, bf16[384,512]{1,0:T(8,128)(2,1)S(1)}, u32[]{:S(2)}, u32[]{:S(2)}) collective-permute-start(bf16[384,512]{1,0:T(8,128)(2,1)S(1)} %get-tuple-element.62), channel_id=1, source_target_pairs={{2,5},{3,6},{4,7},{5,0},{10,13},{11,14},{12,15},{13,8},{18,21},{19... | collective-permute-start | bytes 1179656 | tf_op jit(solution)/shard_map/ppermute | solution.py:469
  168.2 1.9 %collective-permute-start.16 = (bf16[384,512]{1,0:T(8,128)(2,1)S(1)}, bf16[384,512]{1,0:T(8,128)(2,1)S(1)}, u32[]{:S(2)}, u32[]{:S(2)}) collective-permute-start(bf16[384,512]{1,0:T(8,128)(2,1)S(1)} %get-tuple-element.63), channel_id=1, source_target_pairs={{2,6},{3,7},{4,0},{5,1},{10,14},{11,15},{12,8},{13,9},{18,22},{19,... | collective-permute-start | bytes 1179656 | tf_op jit(solution)/shard_map/ppermute | solution.py:469
  170.1 1.3 collective-permute-start.17
  171.5 1.9 %collective-permute-start.18 = (bf16[384,512]{1,0:T(8,128)(2,1)S(1)}, bf16[384,512]{1,0:T(8,128)(2,1)S(1)}, u32[]{:S(2)}, u32[]{:S(2)}) collective-permute-start(bf16[384,512]{1,0:T(8,128)(2,1)S(1)} %get-tuple-element.65), channel_id=1, source_target_pairs={{2,0},{3,1},{4,2},{5,3},{10,8},{11,9},{12,10},{13,11},{18,16},{19,... | collective-permute-start | bytes 1179656 | tf_op jit(solution)/shard_map/ppermute | solution.py:469
  173.4 3.3 %collective-permute-start.19 = (bf16[384,512]{1,0:T(8,128)(2,1)S(1)}, bf16[384,512]{1,0:T(8,128)(2,1)S(1)}, u32[]{:S(2)}, u32[]{:S(2)}) collective-permute-start(bf16[384,512]{1,0:T(8,128)(2,1)S(1)} %get-tuple-element.66), channel_id=1, source_target_pairs={{2,1},{3,2},{4,3},{5,4},{10,9},{11,10},{12,11},{13,12},{18,17},{19... | collective-permute-start | bytes 1179656 | tf_op jit(solution)/shard_map/ppermute | solution.py:469
  178.5 5.3 %collective-permute-done.18.refs_6_ = bf16[384,512]{1,0:T(8,128)(2,1)S(1)} collective-permute-done((bf16[384,512]{1,0:T(8,128)(2,1)S(1)}, bf16[384,512]{1,0:T(8,128)(2,1)S(1)}, u32[]{:S(2)}, u32[]{:S(2)}) %collective-permute-start.18) | collective-permute-done | bytes 393248 | tf_op jit(solution)/shard_map/ppermute | solution.py:469
  183.8 2.4 %collective-permute-done.19.refs_7_ = bf16[384,512]{1,0:T(8,128)(2,1)S(1)} collective-permute-done((bf16[384,512]{1,0:T(8,128)(2,1)S(1)}, bf16[384,512]{1,0:T(8,128)(2,1)S(1)}, u32[]{:S(2)}, u32[]{:S(2)}) %collective-permute-start.19) | collective-permute-done | bytes 393248 | tf_op jit(solution)/shard_map/ppermute | solution.py:469
  186.2 2.7 %finish.1 = (bf16[1,2,32,512]{3,2,1,0:T(8,128)(2,1)}, bf16[1,2,256,512]{3,2,1,0:T(8,128)(2,1)}, f32[1,64,512]{2,1,0:T(8,128)}, f32[1,64,512]{2,1,0:T(8,128)}, f3...) custom-call(s32[2]{0:T(128)S(1)} %pad_add_fusion.info, ...), custom_call_target="tpu_custom_call" | custom-call | bytes 5242880 | tf_op jit(solution)/shard_map/finish/pallas_call | solution.py:596
  (81 shorter events, 21.1 us)
Async XLA Ops:
  4.7 12.4 %collective-permute-start = (bf16[272,512]{1,0:T(8,128)(2,1)S(1)}, bf16[272,512]{1,0:T(8,128)(2,1)S(1)}, u32[]{:S(2)}, u32[]{:S(2)}) collective-permute-start(bf16[272,512]{1,0:T(8,128)(2,1)S(1)} %get-tuple-element.40), channel_id=1, source_target_pairs={{3,2},{0,3},{5,4},{6,5},{11,10},{8,11},{13,12},{14,13},{19,18},{16... | collective-permute-start | bytes 835592 | tf_op jit(solution)/shard_map/ppermute | solution.py:469
  7.1 11.5 %collective-permute-start.1 = (bf16[272,512]{1,0:T(8,128)(2,1)S(1)}, bf16[272,512]{1,0:T(8,128)(2,1)S(1)}, u32[]{:S(2)}, u32[]{:S(2)}) collective-permute-start(bf16[272,512]{1,0:T(8,128)(2,1)S(1)} %get-tuple-element.41), channel_id=1, source_target_pairs={{0,2},{1,3},{6,4},{7,5},{8,10},{9,11},{14,12},{15,13},{16,18},{17,... | collective-permute-start | bytes 835592 | tf_op jit(solution)/shard_map/ppermute | solution.py:469
  8.4 13.4 %collective-permute-start.2 = (bf16[272,512]{1,0:T(8,128)(2,1)S(1)}, bf16[272,512]{1,0:T(8,128)(2,1)S(1)}, u32[]{:S(2)}, u32[]{:S(2)}) collective-permute-start(bf16[272,512]{1,0:T(8,128)(2,1)S(1)} %get-tuple-element.42), channel_id=1, source_target_pairs={{1,2},{2,3},{7,4},{4,5},{9,10},{10,11},{15,12},{12,13},{17,18},{18... | collective-permute-start | bytes 835592 | tf_op jit(solution)/shard_map/ppermute | solution.py:469
  28.1 8.9 %copy-start.19 = (bf16[2,256,512]{2,1,0:T(8,128)(2,1)S(1)}, bf16[2,256,512]{2,1,0:T(8,128)(2,1)}, u32[]{:S(2)}) copy-start(bf16[2,256,512]{2,1,0:T(8,128)(2,1)} %refs_1_.1) | copy-start | bytes 1572868
  28.1 17.7 %copy-start.24 = (bf16[2,256,512]{2,1,0:T(8,128)(2,1)S(1)}, bf16[2,256,512]{2,1,0:T(8,128)(2,1)}, u32[]{:S(2)}) copy-start(bf16[2,256,512]{2,1,0:T(8,128)(2,1)} %refs_0_.1) | copy-start | bytes 1572868
  33.2 11.5 %copy-start.20 = (bf16[1024,512]{1,0:T(8,128)(2,1)}, bf16[1024,512]{1,0:T(8,128)(2,1)S(1)}, u32[]{:S(2)}) copy-start(bf16[1024,512]{1,0:T(8,128)(2,1)S(1)} %get-tuple-element.44.refs_3_) | copy-start | bytes 3145732
  33.2 10.4 %copy-start.3 = (bf16[1,512,512]{2,1,0:T(8,128)(2,1)S(1)}, bf16[1,512,512]{2,1,0:T(8,128)(2,1)}, u32[]{:S(2)}) copy-start(bf16[1,512,512]{2,1,0:T(8,128)(2,1)} %refs_11_.7) | copy-start | bytes 1572868
  33.2 10.4 %copy-start.4 = (bf16[1,512,512]{2,1,0:T(8,128)(2,1)S(1)}, bf16[1,512,512]{2,1,0:T(8,128)(2,1)}, u32[]{:S(2)}) copy-start(bf16[1,512,512]{2,1,0:T(8,128)(2,1)} %refs_8_.7) | copy-start | bytes 1572868
  33.2 10.4 %copy-start.18 = (bf16[1,2,256,512]{3,2,1,0:T(8,128)(2,1)S(1)}, bf16[1,2,256,512]{3,2,1,0:T(8,128)(2,1)}, u32[]{:S(2)}) copy-start(bf16[1,2,256,512]{3,2,1,0:T(8,128)(2,1)} %nodes.5) | copy-start | bytes 1572868
  33.3 10.4 %collective-permute-start.3 = (bf16[256,512]{1,0:T(8,128)(2,1)S(1)}, bf16[256,512]{1,0:T(8,128)(2,1)S(1)}, u32[]{:S(2)}, u32[]{:S(2)}) collective-permute-start(bf16[256,512]{1,0:T(8,128)(2,1)S(1)} %get-tuple-element.45.part_own), channel_id=1, source_target_pairs={{2,4},{3,5},{4,2},{5,3},{10,12},{11,13},{12,10},{13,11},{18,20},{1... | collective-permute-start | bytes 786440 | tf_op jit(solution)/shard_map/ppermute | solution.py:469
  37.1 8.6 %collective-permute-start.6 = (bf16[256,512]{1,0:T(8,128)(2,1)S(1)}, bf16[256,512]{1,0:T(8,128)(2,1)S(1)}, u32[]{:S(2)}, u32[]{:S(2)}) collective-permute-start(bf16[256,512]{1,0:T(8,128)(2,1)S(1)} %get-tuple-element.71), channel_id=1, source_target_pairs={{25,26},{26,27},{31,28},{28,29}} | collective-permute-start | bytes 786440 | tf_op jit(solution)/shard_map/ppermute | solution.py:469
  37.8 7.9 %collective-permute-start.5 = (bf16[256,512]{1,0:T(8,128)(2,1)S(1)}, bf16[256,512]{1,0:T(8,128)(2,1)S(1)}, u32[]{:S(2)}, u32[]{:S(2)}) collective-permute-start(bf16[256,512]{1,0:T(8,128)(2,1)S(1)} %get-tuple-element.72), channel_id=1, source_target_pairs={{24,26},{25,27},{30,28},{31,29}} | collective-permute-start | bytes 786440 | tf_op jit(solution)/shard_map/ppermute | solution.py:469
  38.5 7.2 %collective-permute-start.4 = (bf16[256,512]{1,0:T(8,128)(2,1)S(1)}, bf16[256,512]{1,0:T(8,128)(2,1)S(1)}, u32[]{:S(2)}, u32[]{:S(2)}) collective-permute-start(bf16[256,512]{1,0:T(8,128)(2,1)S(1)} %get-tuple-element.73), channel_id=1, source_target_pairs={{27,26},{24,27},{29,28},{30,29}} | collective-permute-start | bytes 786440 | tf_op jit(solution)/shard_map/ppermute | solution.py:469
  45.8 11.5 %copy-start.1 = (bf16[768,512]{1,0:T(8,128)(2,1)S(1)}, bf16[768,512]{1,0:T(8,128)(2,1)}, u32[]{:S(2)}) copy-start(bf16[768,512]{1,0:T(8,128)(2,1)} %copy-done) | copy-start | bytes 2359300
  45.8 11.5 %copy-start.2 = (bf16[1024,512]{1,0:T(8,128)(2,1)S(1)}, bf16[1024,512]{1,0:T(8,128)(2,1)}, u32[]{:S(2)}) copy-start(bf16[1024,512]{1,0:T(8,128)(2,1)} %get-tuple-element.47.refs_6_.refs_5_) | copy-start | bytes 3145732
  54.8 1.5 collective-permute-start.7
  55.5 0.7 collective-permute-start.8
  58.3 1.5 collective-permute-start.9
  59.1 0.7 collective-permute-start.10
  61.7 53.5 %collective-permute-start.11 = (bf16[1280,512]{1,0:T(8,128)(2,1)}, bf16[1280,512]{1,0:T(8,128)(2,1)S(1)}, u32[]{:S(2)}, u32[]{:S(2)}) collective-permute-start(bf16[1280,512]{1,0:T(8,128)(2,1)} %get-tuple-element.54.refs_2_), channel_id=1, source_target_pairs={{10,2},{11,3},{12,4},{13,5}} | collective-permute-start | bytes 3932168 | tf_op jit(solution)/shard_map/ppermute | solution.py:469
  63.0 52.2 %collective-permute-start.12 = (bf16[256,512]{1,0:T(8,128)(2,1)S(1)}, bf16[256,512]{1,0:T(8,128)(2,1)S(1)}, u32[]{:S(2)}, u32[]{:S(2)}) collective-permute-start(bf16[256,512]{1,0:T(8,128)(2,1)S(1)} %get-tuple-element.55), channel_id=1, source_target_pairs={{10,4},{11,5},{12,2},{13,3}} | collective-permute-start | bytes 786440 | tf_op jit(solution)/shard_map/ppermute | solution.py:469
  116.3 9.3 %copy-start.16 = (bf16[1,2,256,512]{3,2,1,0:T(8,128)(2,1)S(1)}, bf16[1,2,256,512]{3,2,1,0:T(8,128)(2,1)}, u32[]{:S(2)}) copy-start(bf16[1,2,256,512]{3,2,1,0:T(8,128)(2,1)} %edges.5) | copy-start | bytes 1572868
  136.1 35.3 %collective-permute-start.13 = (bf16[384,512]{1,0:T(8,128)(2,1)S(1)}, bf16[384,512]{1,0:T(8,128)(2,1)S(1)}, u32[]{:S(2)}, u32[]{:S(2)}) collective-permute-start(bf16[384,512]{1,0:T(8,128)(2,1)S(1)} %get-tuple-element.60), channel_id=1, source_target_pairs={{2,3},{3,4},{4,5},{5,6},{10,11},{11,12},{12,13},{13,14},{18,19},{1... | collective-permute-start | bytes 1179656 | tf_op jit(solution)/shard_map/ppermute | solution.py:469
  138.0 35.4 %collective-permute-start.14 = (bf16[384,512]{1,0:T(8,128)(2,1)S(1)}, bf16[384,512]{1,0:T(8,128)(2,1)S(1)}, u32[]{:S(2)}, u32[]{:S(2)}) collective-permute-start(bf16[384,512]{1,0:T(8,128)(2,1)S(1)} %get-tuple-element.61), channel_id=1, source_target_pairs={{2,4},{3,5},{4,6},{5,7},{10,12},{11,13},{12,14},{13,15},{18,20},{1... | collective-permute-start | bytes 1179656 | tf_op jit(solution)/shard_map/ppermute | solution.py:469
  140.4 15.3 %collective-permute-start.20 = (bf16[256,512]{1,0:T(8,128)(2,1)S(1)}, bf16[256,512]{1,0:T(8,128)(2,1)S(1)}, u32[]{:S(2)}, u32[]{:S(2)}) collective-permute-start(bf16[256,512]{1,0:T(8,128)(2,1)S(1)} %get-tuple-element.68), channel_id=1, source_target_pairs={{2,3},{3,0},{4,5},{5,6},{10,11},{11,8},{12,13},{13,14},{18,19},{19... | collective-permute-start | bytes 786440 | tf_op jit(solution)/shard_map/ppermute | solution.py:469
  142.4 25.9 %collective-permute-start.21 = (bf16[256,512]{1,0:T(8,128)(2,1)S(1)}, bf16[256,512]{1,0:T(8,128)(2,1)S(1)}, u32[]{:S(2)}, u32[]{:S(2)}) collective-permute-start(bf16[256,512]{1,0:T(8,128)(2,1)S(1)} %get-tuple-element.69), channel_id=1, source_target_pairs={{2,0},{3,1},{4,6},{5,7},{10,8},{11,9},{12,14},{13,15},{18,16},{19,... | collective-permute-start | bytes 786440 | tf_op jit(solution)/shard_map/ppermute | solution.py:469
  143.7 26.5 %collective-permute-start.22 = (bf16[256,512]{1,0:T(8,128)(2,1)S(1)}, bf16[256,512]{1,0:T(8,128)(2,1)S(1)}, u32[]{:S(2)}, u32[]{:S(2)}) collective-permute-start(bf16[256,512]{1,0:T(8,128)(2,1)S(1)} %get-tuple-element.70), channel_id=1, source_target_pairs={{2,1},{3,2},{4,7},{5,4},{10,9},{11,10},{12,15},{13,12},{18,17},{19... | collective-permute-start | bytes 786440 | tf_op jit(solution)/shard_map/ppermute | solution.py:469
  155.7 21.0 %collective-permute-start.15 = (bf16[384,512]{1,0:T(8,128)(2,1)S(1)}, bf16[384,512]{1,0:T(8,128)(2,1)S(1)}, u32[]{:S(2)}, u32[]{:S(2)}) collective-permute-start(bf16[384,512]{1,0:T(8,128)(2,1)S(1)} %get-tuple-element.62), channel_id=1, source_target_pairs={{2,5},{3,6},{4,7},{5,0},{10,13},{11,14},{12,15},{13,8},{18,21},{19... | collective-permute-start | bytes 1179656 | tf_op jit(solution)/shard_map/ppermute | solution.py:469
  168.2 9.5 %collective-permute-start.16 = (bf16[384,512]{1,0:T(8,128)(2,1)S(1)}, bf16[384,512]{1,0:T(8,128)(2,1)S(1)}, u32[]{:S(2)}, u32[]{:S(2)}) collective-permute-start(bf16[384,512]{1,0:T(8,128)(2,1)S(1)} %get-tuple-element.63), channel_id=1, source_target_pairs={{2,6},{3,7},{4,0},{5,1},{10,14},{11,15},{12,8},{13,9},{18,22},{19,... | collective-permute-start | bytes 1179656 | tf_op jit(solution)/shard_map/ppermute | solution.py:469
  170.1 8.4 %collective-permute-start.17 = (bf16[384,512]{1,0:T(8,128)(2,1)S(1)}, bf16[384,512]{1,0:T(8,128)(2,1)S(1)}, u32[]{:S(2)}, u32[]{:S(2)}) collective-permute-start(bf16[384,512]{1,0:T(8,128)(2,1)S(1)} %get-tuple-element.64), channel_id=1, source_target_pairs={{2,7},{3,0},{4,1},{5,2},{10,15},{11,8},{12,9},{13,10},{18,23},{19,... | collective-permute-start | bytes 1179656 | tf_op jit(solution)/shard_map/ppermute | solution.py:469
  171.5 12.3 %collective-permute-start.18 = (bf16[384,512]{1,0:T(8,128)(2,1)S(1)}, bf16[384,512]{1,0:T(8,128)(2,1)S(1)}, u32[]{:S(2)}, u32[]{:S(2)}) collective-permute-start(bf16[384,512]{1,0:T(8,128)(2,1)S(1)} %get-tuple-element.65), channel_id=1, source_target_pairs={{2,0},{3,1},{4,2},{5,3},{10,8},{11,9},{12,10},{13,11},{18,16},{19,... | collective-permute-start | bytes 1179656 | tf_op jit(solution)/shard_map/ppermute | solution.py:469
  173.4 12.8 %collective-permute-start.19 = (bf16[384,512]{1,0:T(8,128)(2,1)S(1)}, bf16[384,512]{1,0:T(8,128)(2,1)S(1)}, u32[]{:S(2)}, u32[]{:S(2)}) collective-permute-start(bf16[384,512]{1,0:T(8,128)(2,1)S(1)} %get-tuple-element.66), channel_id=1, source_target_pairs={{2,1},{3,2},{4,3},{5,4},{10,9},{11,10},{12,11},{13,12},{18,17},{19... | collective-permute-start | bytes 1179656 | tf_op jit(solution)/shard_map/ppermute | solution.py:469
  (19 other events, 50.0 us)

commit v2 on v1

v2 whole, which is shorter than its diff:
```python
import functools

import jax
import jax.numpy as jnp
from jax import lax
from jax.experimental import pallas as pl
from jax.experimental.pallas import tpu as pltpu
from jax.sharding import PartitionSpec as P

BLOCK = 128
PARTS = 2
PAD = 16
VMEM_MIB = 32
BF = jnp.bfloat16
F32 = jnp.float32
SMEM = pl.BlockSpec(memory_space=pltpu.SMEM)
VMEM = pl.BlockSpec(memory_space=pltpu.VMEM)


def matmul(left, right):
    return jnp.dot(left, right, preferred_element_type=F32)


def times_transposed(left, right):
    return lax.dot_general(left, right, (((1,), (1,)), ((), ())), preferred_element_type=F32)


def transposed_times(left, right):
    return lax.dot_general(left, right, (((0,), (0,)), ((), ())), preferred_element_type=F32)


def base_of(half, span, batches):
    return jnp.where(half == 0, span - batches, 0)


def place_of(batch, half, span, batches):
    return (span - batches if half == 0 else 0) + batch


def worker_of(batch, half, span, batches):
    return half * span + place_of(batch, half, span, batches)


def own_batch(member, span, batches):
    half = lax.div(member, span)
    batch = lax.rem(member, span) - base_of(half, span, batches)
    return jnp.clip(batch, 0, batches - 1)


def pick_row(table, row, lanes):
    value = table[0:1, lanes]
    for other in range(1, table.shape[0]):
        value = jnp.where(row == other, table[other : other + 1, lanes], value)
    return value


def hot_rows(index_rows, row, nodes):
    index = index_rows[row : row + 1, :].astype(F32).astype(jnp.int32)
    rows = lax.broadcasted_iota(jnp.int32, (nodes, index_rows.shape[1]), 0)
    return jnp.where(rows == index, 1.0, 0.0).astype(BF)


def hot_columns(index_rows, row, nodes):
    pick = lax.broadcasted_iota(jnp.int32, (index_rows.shape[0], nodes), 0) == row
    index = transposed_times(index_rows, jnp.where(pick, 1.0, 0.0).astype(BF))
    columns = lax.broadcasted_iota(jnp.int32, index.shape, 1).astype(F32)
    return jnp.where(columns == index, 1.0, 0.0).astype(BF)


def slope_of(pre, sigma):
    return (sigma * (1.0 + pre * (1.0 - sigma))).astype(BF)


def pack_kernel(span, batches, info, senders, receivers, tiles, edges, *refs):
    index_out = refs[0]
    outs = refs[1:]
    member = info[1]
    half = lax.div(member, span)
    offset = lax.rem(member, span)
    count = senders.shape[1]
    tile_count = tiles.shape[1]
    tile_len = count // tile_count
    for step in range(span):
        batch = lax.rem(offset - step + span, span) - base_of(half, span, batches)
        batch = jnp.clip(batch, 0, batches - 1)
        if step:
            out, start = outs[step - 1], count
            out[:count] = edges[0, batch]
        else:
            out, start = index_out, 0
        out[start : start + PAD] = jnp.zeros((PAD, out.shape[1]), BF)
        for tile in range(tile_count):
            lanes = slice(tile * tile_len, (tile + 1) * tile_len)
            send = pick_row(senders, batch, lanes) + tiles[batch, tile, 0] * BLOCK
            recv = pick_row(receivers, batch, lanes) + tiles[batch, tile, 1] * BLOCK
            which = lax.broadcasted_iota(jnp.int32, (PAD, tile_len), 0)
            block = jnp.where(which == 0, send, jnp.where(which == 1, recv, 0))
            out[start : start + PAD, lanes] = block.astype(F32).astype(BF)


def ready_kernel(span, batches, info, nodes, w_send, w_recv, w_node, *refs):
    w_edge, w_msg, w_agg, w_out = refs[:4]
    turned, plain, hidden, node_pre, feats_turned = refs[4:]
    batch = own_batch(info[1], span, batches)
    node_count = nodes.shape[2]
    feats = nodes[0, batch]
    hidden[:node_count] = matmul(feats, w_send[0]).astype(BF)
    hidden[node_count:] = matmul(feats, w_recv[0]).astype(BF)
    node_pre[...] = matmul(feats, w_node[0])
    feats_turned[...] = feats.T
    for slot, weight in enumerate((w_edge, w_msg, w_agg)):
        plain[slot] = weight[0]
    for slot, weight in enumerate((w_out, w_agg, w_msg, w_edge, w_node, w_send, w_recv)):
        turned[slot] = weight[0].T


def forward_kernel(span, batches, chunk, info, edges, own_index, *refs):
    others = refs[: span - 1]
    hidden, plain = refs[span - 1 : span + 1]
    act_out, slope_out, part_out, hot_out, hots_out, pieces, both = refs[span + 1 :]
    batch = own_batch(info[1], span, batches)
    count = edges.shape[2]
    node_count = part_out.shape[0]
    for step in range(span):
        run = slice(step * count, (step + 1) * count)
        if step:
            pieces[run] = others[step - 1][:count]
            index_rows = others[step - 1][count : count + PAD, :count]
        else:
            pieces[run] = edges[0, batch]
            index_rows = own_index[:, :count]
        hots_out[:node_count, run] = hot_rows(index_rows, 0, node_count)
        hots_out[node_count:, run] = hot_rows(index_rows, 1, node_count)
        both[run, :node_count] = hot_columns(index_rows, 0, node_count)
        recv_hot = hot_columns(index_rows, 1, node_count)
        both[run, node_count:] = recv_hot
        hot_out[run] = recv_hot
    for at in range(0, span * count, chunk):
        run = slice(at, at + chunk)
        pre = matmul(both[run], hidden[...]) + matmul(pieces[run], plain[0])
        sigma = jax.nn.sigmoid(pre)
        act_out[run] = (pre * sigma).astype(BF)
        slope_out[run] = slope_of(pre, sigma)
    total = matmul(hots_out[node_count:], act_out[...])
    part_out[...] = matmul(total.astype(BF), plain[1]).astype(BF)


def turn_kernel(span, batches, info, edges, act, *refs):
    others = refs[: span - 1]
    edges_turned, act_turned = refs[span - 1 :]
    batch = own_batch(info[1], span, batches)
    count = edges.shape[2]
    for step in range(span):
        run = slice(step * count, (step + 1) * count)
        piece = others[step - 1][:count] if step else edges[0, batch]
        edges_turned[:, run] = piece.T
        act_turned[:, run] = act[run].T


def node_kernel(node_pre, part_own, part_other, plain, turned_first, out):
    count = part_own.shape[0]
    agg = (part_own[...].astype(F32) + part_other[...].astype(F32)).astype(BF)
    pre = node_pre[...] + matmul(agg, plain[2])
    sigma = jax.nn.sigmoid(pre)
    out[:count] = agg
    out[count : 2 * count] = (pre * sigma).astype(BF)
    out[2 * count :] = slope_of(pre, sigma)


def chain_kernel(span, batches, chunk, first, active, info, *refs):
    if active is None:
        chain_step(span, batches, chunk, first, info, *refs)
        return
    kept = None
    if len(refs) == 12:
        kept = refs[2:4]
        refs = refs[:2] + refs[4:]

    @pl.when(info[0] == active)
    def _():
        chain_step(span, batches, chunk, first, info, *refs)

    if kept is not None:

        @pl.when(info[0] != active)
        def _():
            refs[-3][...] = kept[0][...]
            refs[-1][...] = kept[1][...]


def chain_step(span, batches, chunk, first, info, *refs):
    member = info[1]
    batch = own_batch(member, span, batches)
    half = lax.div(member, span)
    if first:
        top_nodes, top_edges = refs[:2]
        others = refs[2 : span + 1]
        hot, hots, slope, node_pack, turned, pay, part_out, keep, came = refs[span + 1 :]
        count = top_edges.shape[1]
        for step in range(span):
            came[step * count : (step + 1) * count] = others[step - 1][...] if step else top_edges[batch]
        grad = top_nodes[batch]
    else:
        came, cross = refs[:2]
        hot, hots, slope, node_pack, turned, pay, part_out, keep = refs[2:]
        total = slope.shape[0]
        grad = (came[total:].astype(F32) + cross[...].astype(F32)).astype(BF)
    total = slope.shape[0]
    node_count = part_out.shape[0]
    node_at = 2 * total
    delta = (matmul(grad, turned[0]) * node_pack[2 * node_count :].astype(F32)).astype(BF)
    agg_grad = matmul(delta, turned[1]).astype(BF)
    keep[node_at : node_at + node_count] = delta
    keep[node_at + node_count : node_at + 2 * node_count] = grad
    for at in range(0, total, chunk):
        run = slice(at, at + chunk)
        incoming = came[run].astype(F32)
        message_grad = (incoming + matmul(hot[run], agg_grad)).astype(BF)
        keep[run] = message_grad
        edge_delta = (matmul(message_grad, turned[2]) * slope[run].astype(F32)).astype(BF)
        keep[total + at : total + at + chunk] = edge_delta
        pay[run] = (incoming + matmul(edge_delta, turned[3])).astype(BF)
    sums = matmul(hots[...], keep[total : 2 * total]).astype(BF)
    keep[node_at + 2 * node_count :] = sums
    own = grad.astype(F32) + matmul(delta, turned[4])
    own = own * jnp.where(half == 0, 1.0, 0.0)
    part = matmul(sums[:node_count], turned[5]) + matmul(sums[node_count:], turned[6])
    part = (own + part).astype(BF)
    pay[total:] = part
    part_out[...] = part


def grads_kernel(span, groups, low, high, info, *refs):
    section = info[0]

    @pl.when((section >= low) & (section < high))
    def _():
        grads_step(span, groups, info, *refs)


def grads_step(span, groups, info, edges_turned, act_turned, feats_turned, node_pack, keep, pay, *refs):
    blocks = refs[:groups]
    returns = refs[groups : groups + span]
    sums = refs[groups + span]
    member = info[1]
    half = lax.div(member, span)
    total = edges_turned.shape[1]
    node_count = feats_turned.shape[1]
    width = feats_turned.shape[0]
    count = total // span
    node_at = 2 * total
    delta = keep[node_at : node_at + node_count]
    grad = keep[node_at + node_count : node_at + 2 * node_count]
    sums[0] = matmul(feats_turned[...], keep[node_at + 2 * node_count : node_at + 3 * node_count]).astype(BF)
    sums[1] = matmul(feats_turned[...], keep[node_at + 3 * node_count :]).astype(BF)
    sums[2] = matmul(edges_turned[...], keep[total : 2 * total]).astype(BF)
    sums[3] = matmul(act_turned[...], keep[:total]).astype(BF)
    sums[5] = transposed_times(node_pack[:node_count], delta).astype(BF)

    @pl.when(half == 0)
    def _():
        sums[4] = matmul(feats_turned[...], delta).astype(BF)

    @pl.when(half != 0)
    def _():
        sums[4] = transposed_times(node_pack[node_count : 2 * node_count], grad).astype(BF)

    for step in range(span):
        returns[step][...] = pay[step * count : (step + 1) * count]
    share = width // groups
    node_share = node_count // groups
    for step in range(groups):
        owner = lax.rem(member + step, groups)
        at = pl.multiple_of(owner * share, share)
        block = blocks[step]
        for slot in range(5):
            block[slot * share : (slot + 1) * share] = sums[slot, pl.ds(at, share)]
        at_half = pl.multiple_of(owner * share + half * (share // 2), share // 2)
        block[5 * share : 5 * share + share // 2] = sums[5, pl.ds(at_half, share // 2)]
        at_node = pl.multiple_of(total + owner * node_share, node_share)
        block[5 * share + share // 2 :] = pay[pl.ds(at_node, node_share)]


def finish_kernel(span, batches, groups, info, *refs):
    per_set = groups + span
    sets = (refs[:per_set], refs[per_set : 2 * per_set])
    refs = refs[2 * per_set :]
    nodes_out, edges_out, send_out, recv_out, edge_out, msg_out, node_out, agg_out, out_out = refs[:9]
    held = refs[9]
    section = info[0]
    member = info[1]
    half = lax.div(member, span)
    offset = lax.rem(member, span)
    for which in range(2):

        @pl.when((section == 0) == (which == 1))
        def _(which=which):
            blocks, returns = sets[which][:groups], sets[which][groups:]
            for batch in range(batches):
                turn = lax.rem(offset - base_of(half, span, batches) - batch + 2 * span, span)
                for step in range(span):

                    @pl.when(turn == step)
                    def _(step=step):
                        edges_out[0, batch] = returns[step][...]

                for part in range(PARTS):
                    turn_b = lax.rem(member - worker_of(batch, part, span, batches) + groups, groups)
                    for step in range(groups):

                        @pl.when(turn_b == step)
                        def _(step=step, part=part):
                            held[batch, part] = blocks[step][...]

    share = send_out.shape[1]
    for slot, out in enumerate((send_out, recv_out, edge_out, msg_out)):
        rows = slice(slot * share, (slot + 1) * share)
        value = None
        for batch in range(batches):
            for part in range(PARTS):
                piece = held[batch, part, rows].astype(F32)
                value = piece if value is None else value + piece
        out[0] = value

    def over_batches(part, start, length):
        value = None
        for batch in range(batches):
            piece = held[batch, part, start : start + length].astype(F32)
            value = piece if value is None else value + piece
        return value

    node_out[0] = over_batches(0, 4 * share, share)
    out_out[0] = over_batches(1, 4 * share, share)
    for part in range(PARTS):
        agg_out[0, part * (share // 2) : (part + 1) * (share // 2)] = over_batches(part, 5 * share, share // 2)
    at = 5 * share + share // 2
    for batch in range(batches):
        rows = held[batch, 0, at:].astype(F32) + held[batch, 1, at:].astype(F32)
        nodes_out[0, batch] = rows.astype(BF)


def call(kernel, name, in_specs, out_shapes, scratch, flops, touched, aliases={}):
    many = isinstance(out_shapes, list)
    return pl.pallas_call(
        kernel,
        name=name,
        out_shape=out_shapes,
        in_specs=in_specs,
        out_specs=[VMEM] * len(out_shapes) if many else VMEM,
        scratch_shapes=scratch,
        input_output_aliases=aliases,
        compiler_params=pltpu.CompilerParams(vmem_limit_bytes=VMEM_MIB * 1024 * 1024),
        cost_estimate=pl.CostEstimate(flops=flops, bytes_accessed=touched, transcendentals=0),
    )


def body(
    layer_nodes,
    layer_edges,
    top_nodes,
    top_edges,
    tile_blocks,
    senders,
    receivers,
    w_send,
    w_recv,
    w_edge,
    w_msg,
    w_node,
    w_agg,
    w_out,
):
    sections = lax.axis_size("section")
    groups = lax.axis_size("edge")
    section = lax.axis_index("section")
    member = lax.axis_index("edge")
    span = groups // PARTS
    _, batches, node_count, width = layer_nodes.shape
    count = layer_edges.shape[2]
    total = span * count
    chunk = 2 * count
    share = width // groups
    node_share = node_count // groups
    info = jnp.stack([section, member]).astype(jnp.int32)
    axes = ("section", "edge")
    works = [(m, h) for h in range(PARTS) for m in range(batches)]

    def worker(m, h):
        return worker_of(m, h, span, batches)

    def source(m, h, step):
        return h * span + (place_of(m, h, span, batches) + step) % span

    def move(value, layers, links, shift=0):
        pairs = [(s * groups + a, (s + shift) * groups + b) for s in layers for a, b in links]
        return lax.ppermute(value, axes, pairs)

    every = list(range(sections))
    last = [sections - 1]
    collect = [[(source(m, h, step), worker(m, h)) for m, h in works] for step in range(span)]
    deliver = [[(b, a) for a, b in links] for links in collect]

    def like(rows, cols=width, kind=BF):
        return jax.ShapeDtypeStruct((rows, cols), kind)

    packed = call(
        functools.partial(pack_kernel, span, batches),
        "pack",
        [SMEM, VMEM, VMEM, SMEM, VMEM],
        [like(PAD)] + [like(count + PAD)] * (span - 1),
        [],
        0,
        2**20,
    )(info, senders, receivers, tile_blocks, layer_edges)
    own_index, pieces = packed[0], packed[1:]
    pieces = [move(piece, every, collect[step + 1]) for step, piece in enumerate(pieces)]
    half = member // span
    offset = member % span
    tops = []
    for step in range(1, span):
        pick = jnp.clip((offset - step) % span - base_of(half, span, batches), 0, batches - 1)
        tops.append(move(lax.dynamic_index_in_dim(top_edges, pick, 0, keepdims=False), last, collect[step]))

    turned, plain, hidden, node_pre, feats_turned = call(
        functools.partial(ready_kernel, span, batches),
        "ready",
        [SMEM] + [VMEM] * 8,
        [
            jax.ShapeDtypeStruct((7, width, width), BF),
            jax.ShapeDtypeStruct((3, width, width), BF),
            like(2 * node_count),
            like(node_count, kind=F32),
            like(width, node_count),
        ],
        [],
        4 * 10**8,
        10 * 2**20,
    )(info, layer_nodes, w_send, w_recv, w_node, w_edge, w_msg, w_agg, w_out)

    act, slope, part, hot, hots = call(
        functools.partial(forward_kernel, span, batches, chunk),
        "forward",
        [SMEM] + [VMEM] * (span + 3),
        [like(total), like(total), like(node_count), like(total, node_count), like(2 * node_count, total)],
        [pltpu.VMEM((total, width), BF), pltpu.VMEM((total, 2 * node_count), BF)],
        2 * 10**9,
        6 * 2**20,
    )(info, layer_edges, own_index, *pieces, hidden, plain)

    swap = [(worker(m, h), worker(m, 1 - h)) for m, h in works]
    part_other = move(part, every, swap)
    edges_turned, act_turned = call(
        functools.partial(turn_kernel, span, batches),
        "turn",
        [SMEM] + [VMEM] * (span + 1),
        [like(width, total), like(width, total)],
        [],
        0,
        4 * 2**20,
    )(info, layer_edges, act, *pieces)
    node_pack = call(
        node_kernel,
        "node_forward",
        [VMEM] * 4 + [pl.BlockSpec(memory_space=pl.ANY)],
        like(3 * node_count),
        [],
        10**5,
        2**10,
    )(node_pre, part, part_other, plain, edges_turned)

    kept = [like(total + node_count), like(node_count), like(2 * total + 4 * node_count)]
    both_ways = [(worker(m, h), worker(m, h)) for m, h in works]
    rows = 5 * share + share // 2 + node_share
    pay = keep = None
    incoming = None
    sets = []

    def weight_grads(low, high, keep, pay):
        out = call(
            functools.partial(grads_kernel, span, groups, low, high),
            "weight_grads",
            [SMEM] + [VMEM] * 6,
            [like(rows)] * groups + [like(count)] * span,
            [pltpu.VMEM((6, width, width), BF)],
            2 * 10**9,
            10 * 2**20,
        )(info, edges_turned, act_turned, feats_turned, node_pack, keep, pay)
        blocks, returns = out[:groups], out[groups:]
        layers = list(range(low, high))
        blocks = [blocks[0]] + [
            move(blocks[step], layers, [(worker(m, h), (worker(m, h) + step) % groups) for m, h in works])
            for step in range(1, groups)
        ]
        returns = [returns[0]] + [move(returns[step], layers, deliver[step]) for step in range(1, span)]
        return blocks + returns

    for moment in range(sections):
        first = moment == 0
        layer = sections - 1 - moment
        in_place = 0 < moment < sections - 1
        if first:
            inputs = (top_nodes, top_edges, *tops)
        elif in_place:
            inputs = (*incoming, pay, keep)
        else:
            inputs = incoming
        pay, part, keep = call(
            functools.partial(chain_kernel, span, batches, chunk, first, None if first else layer),
            "chain",
            [SMEM] + [VMEM] * (len(inputs) + 5),
            kept,
            [pltpu.VMEM((total, width), BF)] if first else [],
            3 * 10**9,
            10 * 2**20,
            {3: 0, 4: 2} if in_place else {},
        )(info, *inputs, hot, hots, slope, node_pack, turned)
        if layer > 0:
            cross = move(part, [layer], swap, -1)
            came = move(pay, [layer], both_ways, -1)
            incoming = (came, cross)
        if layer <= 1:
            sets.append(weight_grads(layer, sections if layer == 1 else 1, keep, pay))

    grad_shape = jax.ShapeDtypeStruct((1, share, width), F32)
    return call(
        functools.partial(finish_kernel, span, batches, groups),
        "finish",
        [SMEM] + [VMEM] * (2 * (groups + span)),
        [
            jax.ShapeDtypeStruct((1, batches, node_share, width), BF),
            jax.ShapeDtypeStruct((1, batches, count, width), BF),
        ]
        + [grad_shape] * 7,
        [pltpu.VMEM((batches, PARTS, rows, width), BF)],
        0,
        5 * 2**20,
    )(info, *sets[0], *sets[1])


def solution(mesh):
    in_specs = (
        P("section", None, None, None),
        P("section", None, "edge", None),
        P(),
        P(None, "edge", None),
        P(None, "edge", None),
        P(None, "edge"),
        P(None, "edge"),
        P("section", None, None),
        P("section", None, None),
        P("section", None, None),
        P("section", None, None),
        P("section", None, None),
        P("section", None, None),
        P("section", None, None),
    )
    out_specs = (
        P("section", None, "edge", None),
        P("section", None, "edge", None),
        P("section", "edge", None),
        P("section", "edge", None),
        P("section", "edge", None),
        P("section", "edge", None),
        P("section", "edge", None),
        P("section", "edge", None),
        P("section", "edge", None),
    )
    return jax.shard_map(body, mesh=mesh, in_specs=in_specs, out_specs=out_specs, check_vma=False)
```

time: 190 us -> 154 us (0.81)
  the two profiles are of different devices: /device:TPU:10 before, /device:TPU:2 now
where the time goes in v2:
time: 154 us; the launch traced here: 153 us
  waiting for transfers between devices  84.1 us (55%)
  starting transfers between devices  31.5 us (20%)
  Pallas kernels  22.6 us (15%)
  local copies, waits for them, and re-layouts  13 us (8%)
    ppermute x33, waiting for transfers between devices, move(): return lax.ppermute(value, axes, pairs)  84.1 us
    ppermute x33, starting transfers between devices, move(): return lax.ppermute(value, axes, pairs)  31.5 us
    unnamed x30, local copies, waits for them, and re-layouts  12.9 us
    pallas_call x4, Pallas kernels, body(): call(functools.partial(chain_kernel, span, batches, chunk, first, None if...  10.2 us
    pallas_call x2, Pallas kernels, weight_grads(): call(functools.partial(grads_kernel, span, groups, low, high), 'weight_gr...  3.3 us
    pallas_call x1, Pallas kernels, body(): call(functools.partial(forward_kernel, span, batches, chunk), 'forward',...  3.11 us
  transfers between devices with their start and end apart: 33, of which 6 were waited for; matrix products, arithmetic and copies ran while one was open for 0% of the time, Pallas kernels for 7%

profile of v2, /device:TPU:2, one launch (start us, length us, event | category | flops | bytes accessed | tf_op | source)
XLA Modules:
  0.0 152.6 jit_solution(13419936939233696120)
XLA Ops:
  0.7 1.0 copy-done
  5.1 5.3 %collective-permute-start.1 = (bf16[272,512]{1,0:T(8,128)(2,1)S(1)}, bf16[272,512]{1,0:T(8,128)(2,1)S(1)}, u32[]{:S(2)}, u32[]{:S(2)}) collective-permute-start(bf16[272,512]{1,0:T(8,128)(2,1)S(1)} %get-tuple-element.62), channel_id=1, source_target_pairs={{0,2},{1,3},{6,4},{7,5},{8,10},{9,11},{14,12},{15,13},{16,18},{17,... | collective-permute-start | bytes 835592 | tf_op jit(solution)/shard_map/ppermute | solution.py:396
  10.4 1.3 collective-permute-start.2
  11.8 1.0 copy-done.3
  12.9 1.0 copy-done.4
  13.9 1.0 copy-done.5
  14.9 1.0 copy-done.6
  16.0 1.0 copy-done.7
  17.0 1.0 copy-done.8
  18.1 1.0 copy-done.9
  19.1 1.0 copy-done.10
  20.2 1.7 %ready.1 = (bf16[7,512,512]{2,1,0:T(8,128)(2,1)S(1)}, bf16[3,512,512]{2,1,0:T(8,128)(2,1)S(1)}, bf16[512,512]{1,0:T(8,128)(2,1)S(1)}, f32[256,512]{1,0:T(8,128)S(1)}, bf16[512,256]{1,0:T(8,128)(2,1)S(1)}) custom-call(s32[2]{0:T(128)S(1)} %pad_add_fusion.info, bf16[1,2,256,512]{3,2,1,0:T(8,128)(2,1)S(1)} %copy-done.3, bf16[1,512,512]{2,1,0:T(8,128)(2,1)S(1)} %copy-done.4, ...), custom_call_target="tpu_custom_call" | custom-call | flops 400000000 | bytes 10485760 | tf_op jit(solution)/shard_map/ready/pallas_call | solution.py:424
  22.9 3.1 %forward.1 = (bf16[1024,512]{1,0:T(8,128)(2,1)S(1)}, bf16[1024,512]{1,0:T(8,128)(2,1)S(1)}, bf16[256,512]{1,0:T(8,128)(2,1)S(1)}, bf16[1024,256]{1,0:T(8,128)(2,1)S(1)}, bf16[512,1024]{1,0:T(8,128)(2,1)S(1)}) custom-call(s32[2]{0:T(128)S(1)} %pad_add_fusion.info, bf16[1,2,256,512]{3,2,1,0:T(8,128)(2,1)S(1)} %copy-done.1, ...), custom_call_target="tpu_custom_call" | custom-call | flops 2000000000 | bytes 6291456 | tf_op jit(solution)/shard_map/forward/pallas_call | solution.py:440
  28.8 1.2 turn.1
  31.0 3.5 %chain.4 = (bf16[1280,512]{1,0:T(8,128)(2,1)S(1)}, bf16[256,512]{1,0:T(8,128)(2,1)S(1)}, bf16[3072,512]{1,0:T(8,128)(2,1)S(1)}) custom-call(s32[2]{0:T(128)S(1)} %pad_add_fusion.info, bf16[2,256,512]{2,1,0:T(8,128)(2,1)S(1)} %copy-done.14, bf16[2,256,512]{2,1,0:T(8,128)(2,1)S(1)} %copy-done.2, bf16[256,512]{1,0:T(8,128)(2,1)S(1)} %collective-permute-done.4.refs_2_, ...), custom_call_target="tpu_custom_call" | custom-call | flops 3000000000 | bytes 10485760 | tf_op jit(solution)/shard_map/chain/pallas_call | solution.py:507
  36.0 1.1 chain.5
  38.6 1.3 chain.6
  48.9 4.3 %chain.7 = (bf16[1280,512]{1,0:T(8,128)(2,1)S(1)}, bf16[256,512]{1,0:T(8,128)(2,1)}, bf16[3072,512]{1,0:T(8,128)(2,1)S(1)}) custom-call(s32[2]{0:T(128)S(1)} %pad_add_fusion.info, bf16[1280,512]{1,0:T(8,128)(2,1)S(1)} %collective-permute-done.21.refs_0_, bf16[256,512]{1,0:T(8,128)(2,1)S(1)} %collective-permute-done.22.refs_1_, ...), custom_call_target="tpu_custom_call" | custom-call | flops 3000000000 | bytes 10485760 | tf_op jit(solution)/shard_map/chain/pallas_call | solution.py:507
  53.1 2.7 %weight_grads.3 = (bf16[384,512]{1,0:T(8,128)(2,1)S(1)}, bf16[384,512]{1,0:T(8,128)(2,1)S(1)}, bf16[384,512]{1,0:T(8,128)(2,1)S(1)}, bf16[384,512]{1,0:T(8,128)(...) custom-call(s32[2]{0:T(128)S(1)} %pad_add_fusion.info, ...), custom_call_target="tpu_custom_call" | custom-call | flops 2000000000 | bytes 10485760 | tf_op jit(solution)/shard_map/weight_grads/pallas_call | solution.py:479
  58.0 1.3 collective-permute-start.31
  59.3 1.3 collective-permute-start.32
  61.3 65.2 %collective-permute-done.31.refs_22_ = bf16[256,512]{1,0:T(8,128)(2,1)S(1)} collective-permute-done((bf16[256,512]{1,0:T(8,128)(2,1)S(1)}, bf16[256,512]{1,0:T(8,128)(2,1)S(1)}, u32[]{:S(2)}, u32[]{:S(2)}) %collective-permute-start.31) | collective-permute-done | bytes 262176 | tf_op jit(solution)/shard_map/ppermute | solution.py:396
  126.5 1.3 collective-permute-start.26
  127.8 2.9 %collective-permute-done.32.refs_23_ = bf16[256,512]{1,0:T(8,128)(2,1)S(1)} collective-permute-done((bf16[256,512]{1,0:T(8,128)(2,1)S(1)}, bf16[256,512]{1,0:T(8,128)(2,1)S(1)}, u32[]{:S(2)}, u32[]{:S(2)}) %collective-permute-start.32) | collective-permute-done | bytes 262176 | tf_op jit(solution)/shard_map/ppermute | solution.py:396
  130.7 1.3 collective-permute-start.27
  132.0 1.3 collective-permute-start.28
  133.3 1.3 collective-permute-start.29
  134.6 2.5 %collective-permute-done.26.refs_16_ = bf16[384,512]{1,0:T(8,128)(2,1)S(1)} collective-permute-done((bf16[384,512]{1,0:T(8,128)(2,1)S(1)}, bf16[384,512]{1,0:T(8,128)(2,1)S(1)}, u32[]{:S(2)}, u32[]{:S(2)}) %collective-permute-start.26) | collective-permute-done | bytes 393248 | tf_op jit(solution)/shard_map/ppermute | solution.py:396
  137.1 5.1 %collective-permute-done.27.refs_17_ = bf16[384,512]{1,0:T(8,128)(2,1)S(1)} collective-permute-done((bf16[384,512]{1,0:T(8,128)(2,1)S(1)}, bf16[384,512]{1,0:T(8,128)(2,1)S(1)}, u32[]{:S(2)}, u32[]{:S(2)}) %collective-permute-start.27) | collective-permute-done | bytes 393248 | tf_op jit(solution)/shard_map/ppermute | solution.py:396
  142.2 4.0 %collective-permute-done.28.refs_18_ = bf16[384,512]{1,0:T(8,128)(2,1)S(1)} collective-permute-done((bf16[384,512]{1,0:T(8,128)(2,1)S(1)}, bf16[384,512]{1,0:T(8,128)(2,1)S(1)}, u32[]{:S(2)}, u32[]{:S(2)}) %collective-permute-start.28) | collective-permute-done | bytes 393248 | tf_op jit(solution)/shard_map/ppermute | solution.py:396
  146.3 4.3 %collective-permute-done.29.refs_19_ = bf16[384,512]{1,0:T(8,128)(2,1)S(1)} collective-permute-done((bf16[384,512]{1,0:T(8,128)(2,1)S(1)}, bf16[384,512]{1,0:T(8,128)(2,1)S(1)}, u32[]{:S(2)}, u32[]{:S(2)}) %collective-permute-start.29) | collective-permute-done | bytes 393248 | tf_op jit(solution)/shard_map/ppermute | solution.py:396
  150.6 2.0 %finish.1 = (bf16[1,2,32,512]{3,2,1,0:T(8,128)(2,1)}, bf16[1,2,256,512]{3,2,1,0:T(8,128)(2,1)}, f32[1,64,512]{2,1,0:T(8,128)}, f32[1,64,512]{2,1,0:T(8,128)}, f3...) custom-call(s32[2]{0:T(128)S(1)} %pad_add_fusion.info, ...), custom_call_target="tpu_custom_call" | custom-call | bytes 5242880 | tf_op jit(solution)/shard_map/finish/pallas_call | solution.py:525
  (78 shorter events, 22.6 us)
Async XLA Ops:
  4.5 17.5 %collective-permute-start = (bf16[272,512]{1,0:T(8,128)(2,1)S(1)}, bf16[272,512]{1,0:T(8,128)(2,1)S(1)}, u32[]{:S(2)}, u32[]{:S(2)}) collective-permute-start(bf16[272,512]{1,0:T(8,128)(2,1)S(1)} %get-tuple-element.61), channel_id=1, source_target_pairs={{3,2},{0,3},{5,4},{6,5},{11,10},{8,11},{13,12},{14,13},{19,18},{16... | collective-permute-start | bytes 835592 | tf_op jit(solution)/shard_map/ppermute | solution.py:396
  5.1 16.8 %collective-permute-start.1 = (bf16[272,512]{1,0:T(8,128)(2,1)S(1)}, bf16[272,512]{1,0:T(8,128)(2,1)S(1)}, u32[]{:S(2)}, u32[]{:S(2)}) collective-permute-start(bf16[272,512]{1,0:T(8,128)(2,1)S(1)} %get-tuple-element.62), channel_id=1, source_target_pairs={{0,2},{1,3},{6,4},{7,5},{8,10},{9,11},{14,12},{15,13},{16,18},{17,... | collective-permute-start | bytes 835592 | tf_op jit(solution)/shard_map/ppermute | solution.py:396
  10.4 11.6 %collective-permute-start.2 = (bf16[272,512]{1,0:T(8,128)(2,1)S(1)}, bf16[272,512]{1,0:T(8,128)(2,1)S(1)}, u32[]{:S(2)}, u32[]{:S(2)}) collective-permute-start(bf16[272,512]{1,0:T(8,128)(2,1)S(1)} %get-tuple-element.63), channel_id=1, source_target_pairs={{1,2},{2,3},{7,4},{4,5},{9,10},{10,11},{15,12},{12,13},{17,18},{18... | collective-permute-start | bytes 835592 | tf_op jit(solution)/shard_map/ppermute | solution.py:396
  26.0 3.9 %collective-permute-start.3 = (bf16[256,512]{1,0:T(8,128)(2,1)S(1)}, bf16[256,512]{1,0:T(8,128)(2,1)S(1)}, u32[]{:S(2)}, u32[]{:S(2)}) collective-permute-start(bf16[256,512]{1,0:T(8,128)(2,1)S(1)} %get-tuple-element.71.part_own), channel_id=1, source_target_pairs={{2,4},{3,5},{4,2},{5,3},{10,12},{11,13},{12,10},{13,11},{18,20},{1... | collective-permute-start | bytes 786440 | tf_op jit(solution)/shard_map/ppermute | solution.py:396
  26.7 3.7 %collective-permute-start.6 = (bf16[256,512]{1,0:T(8,128)(2,1)S(1)}, bf16[256,512]{1,0:T(8,128)(2,1)S(1)}, u32[]{:S(2)}, u32[]{:S(2)}) collective-permute-start(bf16[256,512]{1,0:T(8,128)(2,1)S(1)} %get-tuple-element.111), channel_id=1, source_target_pairs={{25,26},{26,27},{31,28},{28,29}} | collective-permute-start | bytes 786440 | tf_op jit(solution)/shard_map/ppermute | solution.py:396
  27.4 3.0 %collective-permute-start.5 = (bf16[256,512]{1,0:T(8,128)(2,1)S(1)}, bf16[256,512]{1,0:T(8,128)(2,1)S(1)}, u32[]{:S(2)}, u32[]{:S(2)}) collective-permute-start(bf16[256,512]{1,0:T(8,128)(2,1)S(1)} %get-tuple-element.112), channel_id=1, source_target_pairs={{24,26},{25,27},{30,28},{31,29}} | collective-permute-start | bytes 786440 | tf_op jit(solution)/shard_map/ppermute | solution.py:396
  28.1 2.4 %collective-permute-start.4 = (bf16[256,512]{1,0:T(8,128)(2,1)S(1)}, bf16[256,512]{1,0:T(8,128)(2,1)S(1)}, u32[]{:S(2)}, u32[]{:S(2)}) collective-permute-start(bf16[256,512]{1,0:T(8,128)(2,1)S(1)} %get-tuple-element.113), channel_id=1, source_target_pairs={{27,26},{24,27},{29,28},{30,29}} | collective-permute-start | bytes 786440 | tf_op jit(solution)/shard_map/ppermute | solution.py:396
  34.5 1.5 collective-permute-start.7
  35.3 0.7 collective-permute-start.8
  37.1 1.5 collective-permute-start.9
  39.9 8.3 %collective-permute-start.21 = (bf16[1280,512]{1,0:T(8,128)(2,1)S(1)}, bf16[1280,512]{1,0:T(8,128)(2,1)S(1)}, u32[]{:S(2)}, u32[]{:S(2)}) collective-permute-start(bf16[1280,512]{1,0:T(8,128)(2,1)S(1)} %get-tuple-element.83.refs_5_), channel_id=1, source_target_pairs={{10,2},{11,3},{12,4},{13,5}} | collective-permute-start | bytes 3932168 | tf_op jit(solution)/shard_map/ppermute | solution.py:396
  40.7 3.3 %collective-permute-start.22 = (bf16[256,512]{1,0:T(8,128)(2,1)S(1)}, bf16[256,512]{1,0:T(8,128)(2,1)S(1)}, u32[]{:S(2)}, u32[]{:S(2)}) collective-permute-start(bf16[256,512]{1,0:T(8,128)(2,1)S(1)} %get-tuple-element.96), channel_id=1, source_target_pairs={{10,4},{11,5},{12,2},{13,3}} | collective-permute-start | bytes 786440 | tf_op jit(solution)/shard_map/ppermute | solution.py:396
  41.9 2.8 %collective-permute-start.18 = (bf16[256,512]{1,0:T(8,128)(2,1)S(1)}, bf16[256,512]{1,0:T(8,128)(2,1)S(1)}, u32[]{:S(2)}, u32[]{:S(2)}) collective-permute-start(bf16[256,512]{1,0:T(8,128)(2,1)S(1)} %get-tuple-element.93), channel_id=1, source_target_pairs={{10,11},{11,8},{12,13},{13,14},{18,19},{19,16},{20,21},{21,22},{26... | collective-permute-start | bytes 786440 | tf_op jit(solution)/shard_map/ppermute | solution.py:396
  42.6 4.2 %collective-permute-start.11 = (bf16[384,512]{1,0:T(8,128)(2,1)S(1)}, bf16[384,512]{1,0:T(8,128)(2,1)S(1)}, u32[]{:S(2)}, u32[]{:S(2)}) collective-permute-start(bf16[384,512]{1,0:T(8,128)(2,1)S(1)} %get-tuple-element.85), channel_id=1, source_target_pairs={{10,11},{11,12},{12,13},{13,14},{18,19},{19,20},{20,21},{21,22},{2... | collective-permute-start | bytes 1179656 | tf_op jit(solution)/shard_map/ppermute | solution.py:396
  43.3 4.2 %collective-permute-start.12 = (bf16[384,512]{1,0:T(8,128)(2,1)S(1)}, bf16[384,512]{1,0:T(8,128)(2,1)S(1)}, u32[]{:S(2)}, u32[]{:S(2)}) collective-permute-start(bf16[384,512]{1,0:T(8,128)(2,1)S(1)} %get-tuple-element.86), channel_id=1, source_target_pairs={{10,12},{11,13},{12,14},{13,15},{18,20},{19,21},{20,22},{21,23},{2... | collective-permute-start | bytes 1179656 | tf_op jit(solution)/shard_map/ppermute | solution.py:396
  44.0 1.4 collective-permute-start.19
  44.7 1.4 collective-permute-start.20
  45.4 10.5 %collective-permute-start.13 = (bf16[384,512]{1,0:T(8,128)(2,1)S(1)}, bf16[384,512]{1,0:T(8,128)(2,1)S(1)}, u32[]{:S(2)}, u32[]{:S(2)}) collective-permute-start(bf16[384,512]{1,0:T(8,128)(2,1)S(1)} %get-tuple-element.87), channel_id=1, source_target_pairs={{10,13},{11,14},{12,15},{13,8},{18,21},{19,22},{20,23},{21,16},{26... | collective-permute-start | bytes 1179656 | tf_op jit(solution)/shard_map/ppermute | solution.py:396
  46.1 10.5 %collective-permute-start.14 = (bf16[384,512]{1,0:T(8,128)(2,1)S(1)}, bf16[384,512]{1,0:T(8,128)(2,1)S(1)}, u32[]{:S(2)}, u32[]{:S(2)}) collective-permute-start(bf16[384,512]{1,0:T(8,128)(2,1)S(1)} %get-tuple-element.88), channel_id=1, source_target_pairs={{10,14},{11,15},{12,8},{13,9},{18,22},{19,23},{20,16},{21,17},{26,... | collective-permute-start | bytes 1179656 | tf_op jit(solution)/shard_map/ppermute | solution.py:396
  46.8 10.5 %collective-permute-start.15 = (bf16[384,512]{1,0:T(8,128)(2,1)S(1)}, bf16[384,512]{1,0:T(8,128)(2,1)S(1)}, u32[]{:S(2)}, u32[]{:S(2)}) collective-permute-start(bf16[384,512]{1,0:T(8,128)(2,1)S(1)} %get-tuple-element.89), channel_id=1, source_target_pairs={{10,15},{11,8},{12,9},{13,10},{18,23},{19,16},{20,17},{21,18},{26,... | collective-permute-start | bytes 1179656 | tf_op jit(solution)/shard_map/ppermute | solution.py:396
  47.5 10.5 %collective-permute-start.16 = (bf16[384,512]{1,0:T(8,128)(2,1)S(1)}, bf16[384,512]{1,0:T(8,128)(2,1)S(1)}, u32[]{:S(2)}, u32[]{:S(2)}) collective-permute-start(bf16[384,512]{1,0:T(8,128)(2,1)S(1)} %get-tuple-element.90), channel_id=1, source_target_pairs={{10,8},{11,9},{12,10},{13,11},{18,16},{19,17},{20,18},{21,19},{26,... | collective-permute-start | bytes 1179656 | tf_op jit(solution)/shard_map/ppermute | solution.py:396
  48.2 11.1 %collective-permute-start.17 = (bf16[384,512]{1,0:T(8,128)(2,1)S(1)}, bf16[384,512]{1,0:T(8,128)(2,1)S(1)}, u32[]{:S(2)}, u32[]{:S(2)}) collective-permute-start(bf16[384,512]{1,0:T(8,128)(2,1)S(1)} %get-tuple-element.91), channel_id=1, source_target_pairs={{10,9},{11,10},{12,11},{13,12},{18,17},{19,18},{20,19},{21,20},{26... | collective-permute-start | bytes 1179656 | tf_op jit(solution)/shard_map/ppermute | solution.py:396
  55.9 76.1 %collective-permute-start.23 = (bf16[384,512]{1,0:T(8,128)(2,1)S(1)}, bf16[384,512]{1,0:T(8,128)(2,1)S(1)}, u32[]{:S(2)}, u32[]{:S(2)}) collective-permute-start(bf16[384,512]{1,0:T(8,128)(2,1)S(1)} %get-tuple-element.100), channel_id=1, source_target_pairs={{2,3},{3,4},{4,5},{5,6}} | collective-permute-start | bytes 1179656 | tf_op jit(solution)/shard_map/ppermute | solution.py:396
  56.6 76.7 %collective-permute-start.24 = (bf16[384,512]{1,0:T(8,128)(2,1)S(1)}, bf16[384,512]{1,0:T(8,128)(2,1)S(1)}, u32[]{:S(2)}, u32[]{:S(2)}) collective-permute-start(bf16[384,512]{1,0:T(8,128)(2,1)S(1)} %get-tuple-element.101), channel_id=1, source_target_pairs={{2,4},{3,5},{4,6},{5,7}} | collective-permute-start | bytes 1179656 | tf_op jit(solution)/shard_map/ppermute | solution.py:396
  57.3 3.3 %collective-permute-start.30 = (bf16[256,512]{1,0:T(8,128)(2,1)S(1)}, bf16[256,512]{1,0:T(8,128)(2,1)S(1)}, u32[]{:S(2)}, u32[]{:S(2)}) collective-permute-start(bf16[256,512]{1,0:T(8,128)(2,1)S(1)} %get-tuple-element.108), channel_id=1, source_target_pairs={{2,3},{3,0},{4,5},{5,6}} | collective-permute-start | bytes 786440 | tf_op jit(solution)/shard_map/ppermute | solution.py:396
  58.0 68.5 %collective-permute-start.31 = (bf16[256,512]{1,0:T(8,128)(2,1)S(1)}, bf16[256,512]{1,0:T(8,128)(2,1)S(1)}, u32[]{:S(2)}, u32[]{:S(2)}) collective-permute-start(bf16[256,512]{1,0:T(8,128)(2,1)S(1)} %get-tuple-element.109), channel_id=1, source_target_pairs={{2,0},{3,1},{4,6},{5,7}} | collective-permute-start | bytes 786440 | tf_op jit(solution)/shard_map/ppermute | solution.py:396
  59.3 71.4 %collective-permute-start.32 = (bf16[256,512]{1,0:T(8,128)(2,1)S(1)}, bf16[256,512]{1,0:T(8,128)(2,1)S(1)}, u32[]{:S(2)}, u32[]{:S(2)}) collective-permute-start(bf16[256,512]{1,0:T(8,128)(2,1)S(1)} %get-tuple-element.110), channel_id=1, source_target_pairs={{2,1},{3,2},{4,7},{5,4}} | collective-permute-start | bytes 786440 | tf_op jit(solution)/shard_map/ppermute | solution.py:396
  60.6 74.0 %collective-permute-start.25 = (bf16[384,512]{1,0:T(8,128)(2,1)S(1)}, bf16[384,512]{1,0:T(8,128)(2,1)S(1)}, u32[]{:S(2)}, u32[]{:S(2)}) collective-permute-start(bf16[384,512]{1,0:T(8,128)(2,1)S(1)} %get-tuple-element.102), channel_id=1, source_target_pairs={{2,5},{3,6},{4,7},{5,0}} | collective-permute-start | bytes 1179656 | tf_op jit(solution)/shard_map/ppermute | solution.py:396
  126.5 10.6 %collective-permute-start.26 = (bf16[384,512]{1,0:T(8,128)(2,1)S(1)}, bf16[384,512]{1,0:T(8,128)(2,1)S(1)}, u32[]{:S(2)}, u32[]{:S(2)}) collective-permute-start(bf16[384,512]{1,0:T(8,128)(2,1)S(1)} %get-tuple-element.103), channel_id=1, source_target_pairs={{2,6},{3,7},{4,0},{5,1}} | collective-permute-start | bytes 1179656 | tf_op jit(solution)/shard_map/ppermute | solution.py:396
  130.7 11.6 %collective-permute-start.27 = (bf16[384,512]{1,0:T(8,128)(2,1)S(1)}, bf16[384,512]{1,0:T(8,128)(2,1)S(1)}, u32[]{:S(2)}, u32[]{:S(2)}) collective-permute-start(bf16[384,512]{1,0:T(8,128)(2,1)S(1)} %get-tuple-element.104), channel_id=1, source_target_pairs={{2,7},{3,0},{4,1},{5,2}} | collective-permute-start | bytes 1179656 | tf_op jit(solution)/shard_map/ppermute | solution.py:396
  132.0 14.3 %collective-permute-start.28 = (bf16[384,512]{1,0:T(8,128)(2,1)S(1)}, bf16[384,512]{1,0:T(8,128)(2,1)S(1)}, u32[]{:S(2)}, u32[]{:S(2)}) collective-permute-start(bf16[384,512]{1,0:T(8,128)(2,1)S(1)} %get-tuple-element.105), channel_id=1, source_target_pairs={{2,0},{3,1},{4,2},{5,3}} | collective-permute-start | bytes 1179656 | tf_op jit(solution)/shard_map/ppermute | solution.py:396
  133.3 17.3 %collective-permute-start.29 = (bf16[384,512]{1,0:T(8,128)(2,1)S(1)}, bf16[384,512]{1,0:T(8,128)(2,1)S(1)}, u32[]{:S(2)}, u32[]{:S(2)}) collective-permute-start(bf16[384,512]{1,0:T(8,128)(2,1)S(1)} %get-tuple-element.106), channel_id=1, source_target_pairs={{2,1},{3,2},{4,3},{5,4}} | collective-permute-start | bytes 1179656 | tf_op jit(solution)/shard_map/ppermute | solution.py:396
  (16 other events, 15.9 us)

commit v3 on v2

--- a/solution.py
+++ b/solution.py
@@ -10,9 +10,10 @@
 BLOCK = 128
 PARTS = 2
 PAD = 16
-VMEM_MIB = 32
+GRANT = 32
 BF = jnp.bfloat16
 F32 = jnp.float32
+ANY = pl.BlockSpec(memory_space=pl.ANY)
 SMEM = pl.BlockSpec(memory_space=pltpu.SMEM)
 VMEM = pl.BlockSpec(memory_space=pltpu.VMEM)
 
@@ -73,29 +74,48 @@
 
 def pack_kernel(span, batches, info, senders, receivers, tiles, edges, *refs):
     index_out = refs[0]
-    outs = refs[1:]
+    outs = refs[1:span]
+    send_in, recv_in, rows, sems = refs[span:]
     member = info[1]
     half = lax.div(member, span)
     offset = lax.rem(member, span)
     count = senders.shape[1]
     tile_count = tiles.shape[1]
     tile_len = count // tile_count
+    gets = [
+        pltpu.make_async_copy(senders, send_in, sems.at[0]),
+        pltpu.make_async_copy(receivers, recv_in, sems.at[1]),
+    ]
+    picks, puts = [], []
     for step in range(span):
         batch = lax.rem(offset - step + span, span) - base_of(half, span, batches)
-        batch = jnp.clip(batch, 0, batches - 1)
+        picks.append(jnp.clip(batch, 0, batches - 1))
         if step:
-            out, start = outs[step - 1], count
-            out[:count] = edges[0, batch]
-        else:
-            out, start = index_out, 0
-        out[start : start + PAD] = jnp.zeros((PAD, out.shape[1]), BF)
+            puts.append(
+                pltpu.make_async_copy(
+                    edges.at[0, picks[step]], outs[step - 1].at[pl.ds(0, count)], sems.at[1 + step]
+                )
+            )
+    for copy in gets + puts:
+        copy.start()
+    for copy in gets:
+        copy.wait()
+    rows[...] = jnp.zeros_like(rows)
+    for step in range(span):
+        batch = picks[step]
         for tile in range(tile_count):
             lanes = slice(tile * tile_len, (tile + 1) * tile_len)
-            send = pick_row(senders, batch, lanes) + tiles[batch, tile, 0] * BLOCK
-            recv = pick_row(receivers, batch, lanes) + tiles[batch, tile, 1] * BLOCK
+            send = pick_row(send_in, batch, lanes) + tiles[batch, tile, 0] * BLOCK
+            recv = pick_row(recv_in, batch, lanes) + tiles[batch, tile, 1] * BLOCK
             which = lax.broadcasted_iota(jnp.int32, (PAD, tile_len), 0)
             block = jnp.where(which == 0, send, jnp.where(which == 1, recv, 0))
-            out[start : start + PAD, lanes] = block.astype(F32).astype(BF)
+            rows[step, :, lanes] = block.astype(F32).astype(BF)
+        target = outs[step - 1].at[pl.ds(count, PAD)] if step else index_out
+        copy = pltpu.make_async_copy(rows.at[step], target, sems.at[1 + span + step])
+        copy.start()
+        puts.append(copy)
+    for copy in puts:
+        copy.wait()
 
 
 def ready_kernel(span, batches, info, nodes, w_send, w_recv, w_node, *refs):
@@ -168,11 +188,8 @@
 
 
 def chain_kernel(span, batches, chunk, first, active, info, *refs):
-    if active is None:
-        chain_step(span, batches, chunk, first, info, *refs)
-        return
     kept = None
-    if len(refs) == 12:
+    if not first and len(refs) == 12:
         kept = refs[2:4]
         refs = refs[:2] + refs[4:]
 
@@ -230,20 +247,13 @@
     part_out[...] = part
 
 
-def grads_kernel(span, groups, low, high, info, *refs):
-    section = info[0]
-
-    @pl.when((section >= low) & (section < high))
-    def _():
-        grads_step(span, groups, info, *refs)
-
-
-def grads_step(span, groups, info, edges_turned, act_turned, feats_turned, node_pack, keep, pay, *refs):
-    blocks = refs[:groups]
-    returns = refs[groups : groups + span]
-    sums = refs[groups + span]
+def grads_kernel(span, batches, groups, info, edges_turned, act_turned, feats_turned, node_pack, keep, pay, *refs):
+    near, far = refs[:span], refs[span : 2 * span]
+    sums = refs[2 * span]
     member = info[1]
     half = lax.div(member, span)
+    offset = lax.rem(member, span)
+    batch = own_batch(member, span, batches)
     total = edges_turned.shape[1]
     node_count = feats_turned.shape[1]
     width = feats_turned.shape[0]
@@ -265,52 +275,46 @@
     def _():
         sums[4] = transposed_times(node_pack[node_count : 2 * node_count], grad).astype(BF)
 
-    for step in range(span):
-        returns[step][...] = pay[step * count : (step + 1) * count]
     share = width // groups
     node_share = node_count // groups
-    for step in range(groups):
-        owner = lax.rem(member + step, groups)
+
+    def fill(block, start, owner):
         at = pl.multiple_of(owner * share, share)
-        block = blocks[step]
         for slot in range(5):
-            block[slot * share : (slot + 1) * share] = sums[slot, pl.ds(at, share)]
+            block[start + slot * share : start + (slot + 1) * share] = sums[slot, pl.ds(at, share)]
         at_half = pl.multiple_of(owner * share + half * (share // 2), share // 2)
-        block[5 * share : 5 * share + share // 2] = sums[5, pl.ds(at_half, share // 2)]
+        block[start + 5 * share : start + 5 * share + share // 2] = sums[5, pl.ds(at_half, share // 2)]
         at_node = pl.multiple_of(total + owner * node_share, node_share)
-        block[5 * share + share // 2 :] = pay[pl.ds(at_node, node_share)]
+        block[start + 5 * share + share // 2 :] = pay[pl.ds(at_node, node_share)]
+
+    for step in range(span):
+        near[step][:count] = pay[step * count : (step + 1) * count]
+        fill(near[step], count, half * span + lax.rem(offset + step, span))
+        fill(far[step], 0, (1 - half) * span + lax.rem(batch + step, span))
 
 
 def finish_kernel(span, batches, groups, info, *refs):
-    per_set = groups + span
-    sets = (refs[:per_set], refs[per_set : 2 * per_set])
-    refs = refs[2 * per_set :]
+    near, far = refs[:span], refs[span : 2 * span]
+    refs = refs[2 * span :]
     nodes_out, edges_out, send_out, recv_out, edge_out, msg_out, node_out, agg_out, out_out = refs[:9]
     held = refs[9]
-    section = info[0]
     member = info[1]
     half = lax.div(member, span)
     offset = lax.rem(member, span)
-    for which in range(2):
-
-        @pl.when((section == 0) == (which == 1))
-        def _(which=which):
-            blocks, returns = sets[which][:groups], sets[which][groups:]
-            for batch in range(batches):
-                turn = lax.rem(offset - base_of(half, span, batches) - batch + 2 * span, span)
-                for step in range(span):
-
-                    @pl.when(turn == step)
-                    def _(step=step):
-                        edges_out[0, batch] = returns[step][...]
-
-                for part in range(PARTS):
-                    turn_b = lax.rem(member - worker_of(batch, part, span, batches) + groups, groups)
-                    for step in range(groups):
-
-                        @pl.when(turn_b == step)
-                        def _(step=step, part=part):
-                            held[batch, part] = blocks[step][...]
+    count = edges_out.shape[2]
+    for batch in range(batches):
+        turn = lax.rem(offset - base_of(half, span, batches) - batch + 2 * span, span)
+        turn_far = lax.rem(offset - batch + span, span)
+        for step in range(span):
+
+            @pl.when(turn == step)
+            def _(step=step, batch=batch):
+                edges_out[0, batch] = near[step][:count]
+                held[batch, half] = near[step][count:]
+
+            @pl.when(turn_far == step)
+            def _(step=step, batch=batch):
+                held[batch, 1 - half] = far[step][...]
 
     share = send_out.shape[1]
     for slot, out in enumerate((send_out, recv_out, edge_out, msg_out)):
@@ -339,17 +343,17 @@
         nodes_out[0, batch] = rows.astype(BF)
 
 
-def call(kernel, name, in_specs, out_shapes, scratch, flops, touched, aliases={}):
+def call(kernel, name, in_specs, out_shapes, scratch, flops, touched, aliases={}, grant=GRANT, out_spec=VMEM):
     many = isinstance(out_shapes, list)
     return pl.pallas_call(
         kernel,
         name=name,
         out_shape=out_shapes,
         in_specs=in_specs,
-        out_specs=[VMEM] * len(out_shapes) if many else VMEM,
+        out_specs=[out_spec] * len(out_shapes) if many else out_spec,
         scratch_shapes=scratch,
         input_output_aliases=aliases,
-        compiler_params=pltpu.CompilerParams(vmem_limit_bytes=VMEM_MIB * 1024 * 1024),
+        compiler_params=pltpu.CompilerParams(vmem_limit_bytes=grant * 2**20),
         cost_estimate=pl.CostEstimate(flops=flops, bytes_accessed=touched, transcendentals=0),
     )
 
@@ -406,11 +410,18 @@
     packed = call(
         functools.partial(pack_kernel, span, batches),
         "pack",
-        [SMEM, VMEM, VMEM, SMEM, VMEM],
+        [SMEM, ANY, ANY, SMEM, ANY],
         [like(PAD)] + [like(count + PAD)] * (span - 1),
-        [],
+        [
+            pltpu.VMEM((batches, count), jnp.int32),
+            pltpu.VMEM((batches, count), jnp.int32),
+            pltpu.VMEM((span, PAD, width), BF),
+            pltpu.SemaphoreType.DMA((2 + 2 * span,)),
+        ],
         0,
         2**20,
+        grant=62,
+        out_spec=ANY,
     )(info, senders, receivers, tile_blocks, layer_edges)
     own_index, pieces = packed[0], packed[1:]
     pieces = [move(piece, every, collect[step + 1]) for step, piece in enumerate(pieces)]
@@ -461,7 +472,7 @@
     node_pack = call(
         node_kernel,
         "node_forward",
-        [VMEM] * 4 + [pl.BlockSpec(memory_space=pl.ANY)],
+        [VMEM] * 4 + [ANY],
         like(3 * node_count),
         [],
         10**5,
@@ -473,39 +484,16 @@
     rows = 5 * share + share // 2 + node_share
     pay = keep = None
     incoming = None
-    sets = []
-
-    def weight_grads(low, high, keep, pay):
-        out = call(
-            functools.partial(grads_kernel, span, groups, low, high),
-            "weight_grads",
-            [SMEM] + [VMEM] * 6,
-            [like(rows)] * groups + [like(count)] * span,
-            [pltpu.VMEM((6, width, width), BF)],
-            2 * 10**9,
-            10 * 2**20,
-        )(info, edges_turned, act_turned, feats_turned, node_pack, keep, pay)
-        blocks, returns = out[:groups], out[groups:]
-        layers = list(range(low, high))
-        blocks = [blocks[0]] + [
-            move(blocks[step], layers, [(worker(m, h), (worker(m, h) + step) % groups) for m, h in works])
-            for step in range(1, groups)
-        ]
-        returns = [returns[0]] + [move(returns[step], layers, deliver[step]) for step in range(1, span)]
-        return blocks + returns
-
     for moment in range(sections):
         first = moment == 0
         layer = sections - 1 - moment
-        in_place = 0 < moment < sections - 1
+        in_place = not first
         if first:
             inputs = (top_nodes, top_edges, *tops)
-        elif in_place:
+        else:
             inputs = (*incoming, pay, keep)
-        else:
-            inputs = incoming
         pay, part, keep = call(
-            functools.partial(chain_kernel, span, batches, chunk, first, None if first else layer),
+            functools.partial(chain_kernel, span, batches, chunk, first, layer),
             "chain",
             [SMEM] + [VMEM] * (len(inputs) + 5),
             kept,
@@ -518,14 +506,24 @@
             cross = move(part, [layer], swap, -1)
             came = move(pay, [layer], both_ways, -1)
             incoming = (came, cross)
-        if layer <= 1:
-            sets.append(weight_grads(layer, sections if layer == 1 else 1, keep, pay))
-
+
+    out = call(
+        functools.partial(grads_kernel, span, batches, groups),
+        "weight_grads",
+        [SMEM] + [VMEM] * 6,
+        [like(count + rows)] * span + [like(rows)] * span,
+        [pltpu.VMEM((6, width, width), BF)],
+        2 * 10**9,
+        10 * 2**20,
+    )(info, edges_turned, act_turned, feats_turned, node_pack, keep, pay)
+    across = [[(worker(m, h), (1 - h) * span + (m + step) % span) for m, h in works] for step in range(span)]
+    far = [move(block, every, across[step]) for step, block in enumerate(out[span:])]
+    near = [out[0]] + [move(out[step], every, deliver[step]) for step in range(1, span)]
     grad_shape = jax.ShapeDtypeStruct((1, share, width), F32)
     return call(
         functools.partial(finish_kernel, span, batches, groups),
         "finish",
-        [SMEM] + [VMEM] * (2 * (groups + span)),
+        [SMEM] + [VMEM] * (2 * span),
         [
             jax.ShapeDtypeStruct((1, batches, node_share, width), BF),
             jax.ShapeDtypeStruct((1, batches, count, width), BF),
@@ -534,7 +532,7 @@
         [pltpu.VMEM((batches, PARTS, rows, width), BF)],
         0,
         5 * 2**20,
-    )(info, *sets[0], *sets[1])
+    )(info, *near, *far)
 
 
 def solution(mesh):

time: 154 us -> 170 us (1.10)
  the two profiles are of different devices: /device:TPU:2 before, /device:TPU:26 now
where the time goes in v3:
time: 170 us
  waiting for transfers between devices  92.8 us (55%)
  Pallas kernels  44.1 us (26%)
  starting transfers between devices  20.3 us (12%)
  local copies, waits for them, and re-layouts  10.6 us (6%)
    ppermute x20, waiting for transfers between devices, move(): return lax.ppermute(value, axes, pairs)  92.8 us
    pallas_call x1, Pallas kernels, body(): call(functools.partial(pack_kernel, span, batches), 'pack', [SMEM, ANY, A...  25.7 us
    ppermute x20, starting transfers between devices, move(): return lax.ppermute(value, axes, pairs)  20.3 us
    unnamed x26, local copies, waits for them, and re-layouts  10.5 us
    pallas_call x4, Pallas kernels, body(): call(functools.partial(chain_kernel, span, batches, chunk, first, layer),...  7.23 us
  transfers between devices with their start and end apart: 20, of which 4 were waited for; matrix products, arithmetic and copies ran while one was open for 0% of the time, Pallas kernels for 2%

profile of v3, /device:TPU:26, one launch (start us, length us, event | category | flops | bytes accessed | tf_op | source)
XLA Modules:
  0.0 169.5 jit_solution(3339517362422127037)
XLA Ops:
  1.2 25.7 %pack.1 = (bf16[16,512]{1,0:T(8,128)(2,1)}, bf16[272,512]{1,0:T(8,128)(2,1)}, bf16[272,512]{1,0:T(8,128)(2,1)}, bf16[272,512]{1,0:T(8,128)(2,1)}) custom-call(s32[2]{0:T(128)} %pad_add_fusion.info, s32[2,256]{1,0:T(2,128)} %senders.1, s32[2,256]{1,0:T(2,128)} %receivers.1, s32[2,2,2]{2,1,0:T(2,128)} %tiles.1, bf16[1,2,256,512]{3,2,1,0:T(8,128)(2,1)} %edges.5), custom_call_target="tpu_custom_call" | custom-call | bytes 1048576 | tf_op jit(solution)/shard_map/pack/pallas_call | solution.py:410
  27.7 4.1 %collective-permute-start.1 = (bf16[272,512]{1,0:T(8,128)(2,1)}, bf16[272,512]{1,0:T(8,128)(2,1)S(1)}, u32[]{:S(2)}, u32[]{:S(2)}) collective-permute-start(bf16[272,512]{1,0:T(8,128)(2,1)} %get-tuple-element.46), channel_id=1, source_target_pairs={{0,2},{1,3},{6,4},{7,5},{8,10},{9,11},{14,12},{15,13},{16,18},{17,... | collective-permute-start | bytes 835592 | tf_op jit(solution)/shard_map/ppermute | solution.py:400
  31.8 1.3 collective-permute-start.2
  33.2 1.0 copy-done.2
  34.2 1.0 copy-done.3
  35.3 1.0 copy-done.4
  36.3 1.0 copy-done.5
  37.4 1.0 copy-done.6
  38.4 1.0 copy-done.7
  39.5 1.0 copy-done.8
  40.5 1.0 copy-done.9
  42.2 1.7 ready.1
  44.0 0.9 copy-done
  44.9 3.1 %forward.1 = (bf16[1024,512]{1,0:T(8,128)(2,1)S(1)}, bf16[1024,512]{1,0:T(8,128)(2,1)S(1)}, bf16[256,512]{1,0:T(8,128)(2,1)S(1)}, bf16[1024,256]{1,0:T(8,128)(2,1)S(1)}, bf16[512,1024]{1,0:T(8,128)(2,1)S(1)}) custom-call(s32[2]{0:T(128)S(1)} %copy-done.10, bf16[1,2,256,512]{3,2,1,0:T(8,128)(2,1)S(1)} %copy-done, bf16[16,512]{1,0:T(8,128)(2,1)S(1)} %copy-done.12, ...), custom_call_target="tpu_custom_call" | custom-call | flops 2000000000 | bytes 6291456 | tf_op jit(solution)/shard_map/forward/pallas_call | solution.py:451
  50.8 1.2 turn.1
  53.6 0.7 collective-permute-start.7
  55.1 1.1 chain.5
  56.2 0.7 collective-permute-start.9
  57.6 1.3 chain.6
  59.0 0.7 collective-permute-start.11
  60.4 4.3 %chain.7 = (bf16[1280,512]{1,0:T(8,128)(2,1)S(1)}, bf16[256,512]{1,0:T(8,128)(2,1)}, bf16[3072,512]{1,0:T(8,128)(2,1)S(1)}) custom-call(s32[2]{0:T(128)S(1)} %copy-done.10, bf16[1280,512]{1,0:T(8,128)(2,1)S(1)} %collective-permute-done.11.refs_0_, ...), custom_call_target="tpu_custom_call", output_to_operand_aliasing={{0}: (3, {}), {2}: (4, {})} | custom-call | flops 3000000000 | bytes 10485760 | tf_op jit(solution)/shard_map/chain/pallas_call | solution.py:495
  64.7 2.8 %weight_grads.1 = (bf16[640,512]{1,0:T(8,128)(2,1)S(1)}, bf16[640,512]{1,0:T(8,128)(2,1)S(1)}, bf16[640,512]{1,0:T(8,128)(2,1)S(1)}, bf16[640,512]{1,0:T(8,128)(...) custom-call(s32[2]{0:T(128)S(1)} %copy-done.10, ...), custom_call_target="tpu_custom_call" | custom-call | flops 2000000000 | bytes 10485760 | tf_op jit(solution)/shard_map/weight_grads/pallas_call | solution.py:510
  68.9 0.7 collective-permute-start.13
  69.6 1.3 collective-permute-start.14
  70.9 1.3 collective-permute-start.15
  72.2 1.3 collective-permute-start.18
  73.5 1.3 collective-permute-start.19
  74.8 72.0 %collective-permute-done.18.refs_6_ = bf16[384,512]{1,0:T(8,128)(2,1)S(1)} collective-permute-done((bf16[384,512]{1,0:T(8,128)(2,1)S(1)}, bf16[384,512]{1,0:T(8,128)(2,1)S(1)}, u32[]{:S(2)}, u32[]{:S(2)}) %collective-permute-start.18) | collective-permute-done | bytes 393248 | tf_op jit(solution)/shard_map/ppermute | solution.py:400
  146.9 3.0 %collective-permute-done.19.refs_7_ = bf16[384,512]{1,0:T(8,128)(2,1)S(1)} collective-permute-done((bf16[384,512]{1,0:T(8,128)(2,1)S(1)}, bf16[384,512]{1,0:T(8,128)(2,1)S(1)}, u32[]{:S(2)}, u32[]{:S(2)}) %collective-permute-start.19) | collective-permute-done | bytes 393248 | tf_op jit(solution)/shard_map/ppermute | solution.py:400
  149.9 15.3 %collective-permute-done.14.refs_2_ = bf16[640,512]{1,0:T(8,128)(2,1)S(1)} collective-permute-done((bf16[640,512]{1,0:T(8,128)(2,1)S(1)}, bf16[640,512]{1,0:T(8,128)(2,1)S(1)}, u32[]{:S(2)}, u32[]{:S(2)}) %collective-permute-start.14) | collective-permute-done | bytes 655392 | tf_op jit(solution)/shard_map/ppermute | solution.py:400
  165.1 2.5 %collective-permute-done.15.refs_3_ = bf16[640,512]{1,0:T(8,128)(2,1)S(1)} collective-permute-done((bf16[640,512]{1,0:T(8,128)(2,1)S(1)}, bf16[640,512]{1,0:T(8,128)(2,1)S(1)}, u32[]{:S(2)}, u32[]{:S(2)}) %collective-permute-start.15) | collective-permute-done | bytes 655392 | tf_op jit(solution)/shard_map/ppermute | solution.py:400
  167.6 1.9 %finish.1 = (bf16[1,2,32,512]{3,2,1,0:T(8,128)(2,1)}, bf16[1,2,256,512]{3,2,1,0:T(8,128)(2,1)}, f32[1,64,512]{2,1,0:T(8,128)}, f32[1,64,512]{2,1,0:T(8,128)}, f3...) custom-call(s32[2]{0:T(128)S(1)} %copy-done.10, ...), custom_call_target="tpu_custom_call" | custom-call | bytes 5242880 | tf_op jit(solution)/shard_map/finish/pallas_call | solution.py:523
  (47 shorter events, 9.7 us)
Async XLA Ops:
  27.0 17.0 %collective-permute-start = (bf16[272,512]{1,0:T(8,128)(2,1)}, bf16[272,512]{1,0:T(8,128)(2,1)S(1)}, u32[]{:S(2)}, u32[]{:S(2)}) collective-permute-start(bf16[272,512]{1,0:T(8,128)(2,1)} %get-tuple-element.45), channel_id=1, source_target_pairs={{3,2},{0,3},{5,4},{6,5},{11,10},{8,11},{13,12},{14,13},{19,18},{16... | collective-permute-start | bytes 835592 | tf_op jit(solution)/shard_map/ppermute | solution.py:400
  27.7 16.3 %collective-permute-start.1 = (bf16[272,512]{1,0:T(8,128)(2,1)}, bf16[272,512]{1,0:T(8,128)(2,1)S(1)}, u32[]{:S(2)}, u32[]{:S(2)}) collective-permute-start(bf16[272,512]{1,0:T(8,128)(2,1)} %get-tuple-element.46), channel_id=1, source_target_pairs={{0,2},{1,3},{6,4},{7,5},{8,10},{9,11},{14,12},{15,13},{16,18},{17,... | collective-permute-start | bytes 835592 | tf_op jit(solution)/shard_map/ppermute | solution.py:400
  31.8 12.2 %collective-permute-start.2 = (bf16[272,512]{1,0:T(8,128)(2,1)}, bf16[272,512]{1,0:T(8,128)(2,1)S(1)}, u32[]{:S(2)}, u32[]{:S(2)}) collective-permute-start(bf16[272,512]{1,0:T(8,128)(2,1)} %get-tuple-element.47), channel_id=1, source_target_pairs={{1,2},{2,3},{7,4},{4,5},{9,10},{10,11},{15,12},{12,13},{17,18},{18... | collective-permute-start | bytes 835592 | tf_op jit(solution)/shard_map/ppermute | solution.py:400
  33.2 1.0 copy-start.2
  34.2 1.0 copy-start.3
  35.3 1.0 copy-start.4
  36.3 1.0 copy-start.5
  37.4 1.0 copy-start.6
  38.4 1.0 copy-start.7
  39.5 1.0 copy-start.8
  40.5 1.0 copy-start.9
  42.2 1.7 %copy-start.1 = (bf16[2,256,512]{2,1,0:T(8,128)(2,1)S(1)}, bf16[2,256,512]{2,1,0:T(8,128)(2,1)}, u32[]{:S(2)}) copy-start(bf16[2,256,512]{2,1,0:T(8,128)(2,1)} %refs_1_.3) | copy-start | bytes 1572868
  43.9 1.0 copy-start
  43.9 1.0 copy-start.12
  48.1 3.9 %collective-permute-start.3 = (bf16[256,512]{1,0:T(8,128)(2,1)S(1)}, bf16[256,512]{1,0:T(8,128)(2,1)S(1)}, u32[]{:S(2)}, u32[]{:S(2)}) collective-permute-start(bf16[256,512]{1,0:T(8,128)(2,1)S(1)} %get-tuple-element.55.part_own), channel_id=1, source_target_pairs={{2,4},{3,5},{4,2},{5,3},{10,12},{11,13},{12,10},{13,11},{18,20},{1... | collective-permute-start | bytes 786440 | tf_op jit(solution)/shard_map/ppermute | solution.py:400
  48.7 3.7 %collective-permute-start.6 = (bf16[256,512]{1,0:T(8,128)(2,1)S(1)}, bf16[256,512]{1,0:T(8,128)(2,1)S(1)}, u32[]{:S(2)}, u32[]{:S(2)}) collective-permute-start(bf16[256,512]{1,0:T(8,128)(2,1)S(1)} %get-tuple-element.79), channel_id=1, source_target_pairs={{25,26},{26,27},{31,28},{28,29}} | collective-permute-start | bytes 786440 | tf_op jit(solution)/shard_map/ppermute | solution.py:400
  49.4 3.0 %collective-permute-start.5 = (bf16[256,512]{1,0:T(8,128)(2,1)S(1)}, bf16[256,512]{1,0:T(8,128)(2,1)S(1)}, u32[]{:S(2)}, u32[]{:S(2)}) collective-permute-start(bf16[256,512]{1,0:T(8,128)(2,1)S(1)} %get-tuple-element.80), channel_id=1, source_target_pairs={{24,26},{25,27},{30,28},{31,29}} | collective-permute-start | bytes 786440 | tf_op jit(solution)/shard_map/ppermute | solution.py:400
  50.1 2.3 %collective-permute-start.4 = (bf16[256,512]{1,0:T(8,128)(2,1)S(1)}, bf16[256,512]{1,0:T(8,128)(2,1)S(1)}, u32[]{:S(2)}, u32[]{:S(2)}) collective-permute-start(bf16[256,512]{1,0:T(8,128)(2,1)S(1)} %get-tuple-element.81), channel_id=1, source_target_pairs={{27,26},{24,27},{29,28},{30,29}} | collective-permute-start | bytes 786440 | tf_op jit(solution)/shard_map/ppermute | solution.py:400
  52.0 1.0 copy-start.11
  53.6 1.5 collective-permute-start.7
  54.4 0.7 collective-permute-start.8
  56.2 1.5 collective-permute-start.9
  56.9 0.7 collective-permute-start.10
  59.0 1.5 collective-permute-start.11
  59.7 0.7 collective-permute-start.12
  67.5 4.7 %collective-permute-start.16 = (bf16[384,512]{1,0:T(8,128)(2,1)S(1)}, bf16[384,512]{1,0:T(8,128)(2,1)S(1)}, u32[]{:S(2)}, u32[]{:S(2)}) collective-permute-start(bf16[384,512]{1,0:T(8,128)(2,1)S(1)} %get-tuple-element.75), channel_id=1, source_target_pairs={{2,4},{3,5},{4,0},{5,1},{10,12},{11,13},{12,8},{13,9},{18,20},{19,... | collective-permute-start | bytes 1179656 | tf_op jit(solution)/shard_map/ppermute | solution.py:400
  68.2 5.3 %collective-permute-start.17 = (bf16[384,512]{1,0:T(8,128)(2,1)S(1)}, bf16[384,512]{1,0:T(8,128)(2,1)S(1)}, u32[]{:S(2)}, u32[]{:S(2)}) collective-permute-start(bf16[384,512]{1,0:T(8,128)(2,1)S(1)} %get-tuple-element.76), channel_id=1, source_target_pairs={{2,5},{3,6},{4,1},{5,2},{10,13},{11,14},{12,9},{13,10},{18,21},{19... | collective-permute-start | bytes 1179656 | tf_op jit(solution)/shard_map/ppermute | solution.py:400
  68.9 80.9 %collective-permute-start.13 = (bf16[640,512]{1,0:T(8,128)(2,1)S(1)}, bf16[640,512]{1,0:T(8,128)(2,1)S(1)}, u32[]{:S(2)}, u32[]{:S(2)}) collective-permute-start(bf16[640,512]{1,0:T(8,128)(2,1)S(1)} %get-tuple-element.72), channel_id=1, source_target_pairs={{2,3},{3,0},{4,5},{5,6},{10,11},{11,8},{12,13},{13,14},{18,19},{19... | collective-permute-start | bytes 1966088 | tf_op jit(solution)/shard_map/ppermute | solution.py:400
  69.6 95.5 %collective-permute-start.14 = (bf16[640,512]{1,0:T(8,128)(2,1)S(1)}, bf16[640,512]{1,0:T(8,128)(2,1)S(1)}, u32[]{:S(2)}, u32[]{:S(2)}) collective-permute-start(bf16[640,512]{1,0:T(8,128)(2,1)S(1)} %get-tuple-element.73), channel_id=1, source_target_pairs={{2,0},{3,1},{4,6},{5,7},{10,8},{11,9},{12,14},{13,15},{18,16},{19,... | collective-permute-start | bytes 1966088 | tf_op jit(solution)/shard_map/ppermute | solution.py:400
  70.9 96.7 %collective-permute-start.15 = (bf16[640,512]{1,0:T(8,128)(2,1)S(1)}, bf16[640,512]{1,0:T(8,128)(2,1)S(1)}, u32[]{:S(2)}, u32[]{:S(2)}) collective-permute-start(bf16[640,512]{1,0:T(8,128)(2,1)S(1)} %get-tuple-element.74), channel_id=1, source_target_pairs={{2,1},{3,2},{4,7},{5,4},{10,9},{11,10},{12,15},{13,12},{18,17},{19... | collective-permute-start | bytes 1966088 | tf_op jit(solution)/shard_map/ppermute | solution.py:400
  72.2 74.7 %collective-permute-start.18 = (bf16[384,512]{1,0:T(8,128)(2,1)S(1)}, bf16[384,512]{1,0:T(8,128)(2,1)S(1)}, u32[]{:S(2)}, u32[]{:S(2)}) collective-permute-start(bf16[384,512]{1,0:T(8,128)(2,1)S(1)} %get-tuple-element.77), channel_id=1, source_target_pairs={{2,6},{3,7},{4,2},{5,3},{10,14},{11,15},{12,10},{13,11},{18,22},{1... | collective-permute-start | bytes 1179656 | tf_op jit(solution)/shard_map/ppermute | solution.py:400
  73.5 76.3 %collective-permute-start.19 = (bf16[384,512]{1,0:T(8,128)(2,1)S(1)}, bf16[384,512]{1,0:T(8,128)(2,1)S(1)}, u32[]{:S(2)}, u32[]{:S(2)}) collective-permute-start(bf16[384,512]{1,0:T(8,128)(2,1)S(1)} %get-tuple-element.78), channel_id=1, source_target_pairs={{2,7},{3,4},{4,3},{5,0},{10,15},{11,12},{12,11},{13,8},{18,23},{19... | collective-permute-start | bytes 1179656 | tf_op jit(solution)/shard_map/ppermute | solution.py:400
  (1 other events, 0.7 us)

commit v4 on v3

--- a/solution.py
+++ b/solution.py
@@ -10,6 +10,7 @@
 BLOCK = 128
 PARTS = 2
 PAD = 16
+SEND, RECV, EDGE, MSG, NODE, AGG, OUT = range(7)
 GRANT = 32
 BF = jnp.bfloat16
 F32 = jnp.float32
@@ -73,9 +74,8 @@
 
 
 def pack_kernel(span, batches, info, senders, receivers, tiles, edges, *refs):
-    index_out = refs[0]
-    outs = refs[1:span]
-    send_in, recv_in, rows, sems = refs[span:]
+    outs, seconds = refs[:span], refs[span : 2 * span - 1]
+    send_in, recv_in, sems = refs[2 * span - 1 :]
     member = info[1]
     half = lax.div(member, span)
     offset = lax.rem(member, span)
@@ -86,69 +86,66 @@
         pltpu.make_async_copy(senders, send_in, sems.at[0]),
         pltpu.make_async_copy(receivers, recv_in, sems.at[1]),
     ]
-    picks, puts = [], []
+    picks, loads = [], []
     for step in range(span):
         batch = lax.rem(offset - step + span, span) - base_of(half, span, batches)
         picks.append(jnp.clip(batch, 0, batches - 1))
-        if step:
-            puts.append(
-                pltpu.make_async_copy(
-                    edges.at[0, picks[step]], outs[step - 1].at[pl.ds(0, count)], sems.at[1 + step]
-                )
-            )
-    for copy in gets + puts:
+        loads.append(
+            pltpu.make_async_copy(edges.at[0, picks[step]], outs[step].at[pl.ds(0, count)], sems.at[2 + step])
+        )
+    for copy in gets + loads:
         copy.start()
     for copy in gets:
         copy.wait()
-    rows[...] = jnp.zeros_like(rows)
     for step in range(span):
         batch = picks[step]
+        out = outs[step]
+        out[count:] = jnp.zeros((PAD, out.shape[1]), BF)
         for tile in range(tile_count):
             lanes = slice(tile * tile_len, (tile + 1) * tile_len)
             send = pick_row(send_in, batch, lanes) + tiles[batch, tile, 0] * BLOCK
             recv = pick_row(recv_in, batch, lanes) + tiles[batch, tile, 1] * BLOCK
             which = lax.broadcasted_iota(jnp.int32, (PAD, tile_len), 0)
             block = jnp.where(which == 0, send, jnp.where(which == 1, recv, 0))
-            rows[step, :, lanes] = block.astype(F32).astype(BF)
-        target = outs[step - 1].at[pl.ds(count, PAD)] if step else index_out
-        copy = pltpu.make_async_copy(rows.at[step], target, sems.at[1 + span + step])
-        copy.start()
-        puts.append(copy)
-    for copy in puts:
-        copy.wait()
-
-
-def ready_kernel(span, batches, info, nodes, w_send, w_recv, w_node, *refs):
-    w_edge, w_msg, w_agg, w_out = refs[:4]
-    turned, plain, hidden, node_pre, feats_turned = refs[4:]
+            out[count:, lanes] = block.astype(F32).astype(BF)
+    for step in range(span):
+        loads[step].wait()
+        if step:
+            seconds[step - 1][...] = outs[step][...]
+
+
+def ready_kernel(span, batches, info, nodes, weights, *refs):
+    turned, hidden, node_pre, feats_turned = refs[span - 1 : span + 3]
     batch = own_batch(info[1], span, batches)
     node_count = nodes.shape[2]
     feats = nodes[0, batch]
-    hidden[:node_count] = matmul(feats, w_send[0]).astype(BF)
-    hidden[node_count:] = matmul(feats, w_recv[0]).astype(BF)
-    node_pre[...] = matmul(feats, w_node[0])
+    hidden[:node_count] = matmul(feats, weights[SEND]).astype(BF)
+    hidden[node_count:] = matmul(feats, weights[RECV]).astype(BF)
+    node_pre[...] = matmul(feats, weights[NODE])
     feats_turned[...] = feats.T
-    for slot, weight in enumerate((w_edge, w_msg, w_agg)):
-        plain[slot] = weight[0]
-    for slot, weight in enumerate((w_out, w_agg, w_msg, w_edge, w_node, w_send, w_recv)):
-        turned[slot] = weight[0].T
-
-
-def forward_kernel(span, batches, chunk, info, edges, own_index, *refs):
-    others = refs[: span - 1]
-    hidden, plain = refs[span - 1 : span + 1]
-    act_out, slope_out, part_out, hot_out, hots_out, pieces, both = refs[span + 1 :]
-    batch = own_batch(info[1], span, batches)
-    count = edges.shape[2]
+    for slot in range(weights.shape[0]):
+        turned[slot] = weights[slot].T
+
+
+def forward_kernel(span, batches, chunk, sections, info, own, *refs):
+    groups = (refs[: span - 1], refs[span - 1 : 2 * span - 2])
+    hidden, weights = refs[2 * span - 2 : 2 * span]
+    act_out, slope_out, part_out, hot_out, hots_out, pieces, both, index = refs[2 * span :]
+    count = own.shape[0] - PAD
     node_count = part_out.shape[0]
+    for which, others in enumerate(groups):
+
+        @pl.when(lax.rem(sections - 1 - info[0], 2) == which)
+        def _(others=others):
+            for step in range(1, span):
+                pieces[step * count : (step + 1) * count] = others[step - 1][:count]
+                index[step] = others[step - 1][count:, :count]
+
+    pieces[:count] = own[:count]
+    index[0] = own[count:, :count]
     for step in range(span):
         run = slice(step * count, (step + 1) * count)
-        if step:
-            pieces[run] = others[step - 1][:count]
-            index_rows = others[step - 1][count : count + PAD, :count]
-        else:
-            pieces[run] = edges[0, batch]
-            index_rows = own_index[:, :count]
+        index_rows = index[step]
         hots_out[:node_count, run] = hot_rows(index_rows, 0, node_count)
         hots_out[node_count:, run] = hot_rows(index_rows, 1, node_count)
         both[run, :node_count] = hot_columns(index_rows, 0, node_count)
@@ -157,30 +154,26 @@
         hot_out[run] = recv_hot
     for at in range(0, span * count, chunk):
         run = slice(at, at + chunk)
-        pre = matmul(both[run], hidden[...]) + matmul(pieces[run], plain[0])
+        pre = matmul(both[run], hidden[...]) + matmul(pieces[run], weights[EDGE])
         sigma = jax.nn.sigmoid(pre)
         act_out[run] = (pre * sigma).astype(BF)
         slope_out[run] = slope_of(pre, sigma)
     total = matmul(hots_out[node_count:], act_out[...])
-    part_out[...] = matmul(total.astype(BF), plain[1]).astype(BF)
-
-
-def turn_kernel(span, batches, info, edges, act, *refs):
-    others = refs[: span - 1]
-    edges_turned, act_turned = refs[span - 1 :]
-    batch = own_batch(info[1], span, batches)
-    count = edges.shape[2]
-    for step in range(span):
-        run = slice(step * count, (step + 1) * count)
-        piece = others[step - 1][:count] if step else edges[0, batch]
-        edges_turned[:, run] = piece.T
+    part_out[...] = matmul(total.astype(BF), weights[MSG]).astype(BF)
+
+
+def turn_kernel(pieces, act, edges_turned, act_turned):
+    rows = 2 * BLOCK
+    for at in range(0, act.shape[0], rows):
+        run = slice(at, at + rows)
+        edges_turned[:, run] = pieces[run].T
         act_turned[:, run] = act[run].T
 
 
-def node_kernel(node_pre, part_own, part_other, plain, turned_first, out):
+def node_kernel(node_pre, part_own, part_other, weights, turned_first, out):
     count = part_own.shape[0]
     agg = (part_own[...].astype(F32) + part_other[...].astype(F32)).astype(BF)
-    pre = node_pre[...] + matmul(agg, plain[2])
+    pre = node_pre[...] + matmul(agg, weights[AGG])
     sigma = jax.nn.sigmoid(pre)
     out[:count] = agg
     out[count : 2 * count] = (pre * sigma).astype(BF)
@@ -225,8 +218,8 @@
     total = slope.shape[0]
     node_count = part_out.shape[0]
     node_at = 2 * total
-    delta = (matmul(grad, turned[0]) * node_pack[2 * node_count :].astype(F32)).astype(BF)
-    agg_grad = matmul(delta, turned[1]).astype(BF)
+    delta = (matmul(grad, turned[OUT]) * node_pack[2 * node_count :].astype(F32)).astype(BF)
+    agg_grad = matmul(delta, turned[AGG]).astype(BF)
     keep[node_at : node_at + node_count] = delta
     keep[node_at + node_count : node_at + 2 * node_count] = grad
     for at in range(0, total, chunk):
@@ -234,14 +227,14 @@
         incoming = came[run].astype(F32)
         message_grad = (incoming + matmul(hot[run], agg_grad)).astype(BF)
         keep[run] = message_grad
-        edge_delta = (matmul(message_grad, turned[2]) * slope[run].astype(F32)).astype(BF)
+        edge_delta = (matmul(message_grad, turned[MSG]) * slope[run].astype(F32)).astype(BF)
         keep[total + at : total + at + chunk] = edge_delta
-        pay[run] = (incoming + matmul(edge_delta, turned[3])).astype(BF)
+        pay[run] = (incoming + matmul(edge_delta, turned[EDGE])).astype(BF)
     sums = matmul(hots[...], keep[total : 2 * total]).astype(BF)
     keep[node_at + 2 * node_count :] = sums
-    own = grad.astype(F32) + matmul(delta, turned[4])
+    own = grad.astype(F32) + matmul(delta, turned[NODE])
     own = own * jnp.where(half == 0, 1.0, 0.0)
-    part = matmul(sums[:node_count], turned[5]) + matmul(sums[node_count:], turned[6])
+    part = matmul(sums[:node_count], turned[SEND]) + matmul(sums[node_count:], turned[RECV])
     part = (own + part).astype(BF)
     pay[total:] = part
     part_out[...] = part
@@ -343,14 +336,14 @@
         nodes_out[0, batch] = rows.astype(BF)
 
 
-def call(kernel, name, in_specs, out_shapes, scratch, flops, touched, aliases={}, grant=GRANT, out_spec=VMEM):
+def call(kernel, name, in_specs, out_shapes, scratch, flops, touched, aliases={}, grant=GRANT, passed=0):
     many = isinstance(out_shapes, list)
     return pl.pallas_call(
         kernel,
         name=name,
         out_shape=out_shapes,
         in_specs=in_specs,
-        out_specs=[out_spec] * len(out_shapes) if many else out_spec,
+        out_specs=[VMEM] * (len(out_shapes) - passed) + [ANY] * passed if many else VMEM,
         scratch_shapes=scratch,
         input_output_aliases=aliases,
         compiler_params=pltpu.CompilerParams(vmem_limit_bytes=grant * 2**20),
@@ -411,20 +404,20 @@
         functools.partial(pack_kernel, span, batches),
         "pack",
         [SMEM, ANY, ANY, SMEM, ANY],
-        [like(PAD)] + [like(count + PAD)] * (span - 1),
+        [like(count + PAD)] * (2 * span - 1),
         [
             pltpu.VMEM((batches, count), jnp.int32),
             pltpu.VMEM((batches, count), jnp.int32),
-            pltpu.VMEM((span, PAD, width), BF),
-            pltpu.SemaphoreType.DMA((2 + 2 * span,)),
+            pltpu.SemaphoreType.DMA((2 + span,)),
         ],
         0,
         2**20,
         grant=62,
-        out_spec=ANY,
     )(info, senders, receivers, tile_blocks, layer_edges)
-    own_index, pieces = packed[0], packed[1:]
-    pieces = [move(piece, every, collect[step + 1]) for step, piece in enumerate(pieces)]
+    own, first_out, second_out = packed[0], packed[1:span], packed[span:]
+    groups_of = [list(range(sections - 1 - group, -1, -2)) for group in range(2)]
+    first_in = [move(piece, groups_of[0], collect[step + 1]) for step, piece in enumerate(first_out)]
+    weights = jnp.concatenate([w_send, w_recv, w_edge, w_msg, w_node, w_agg, w_out], axis=0)
     half = member // span
     offset = member % span
     tops = []
@@ -432,43 +425,47 @@
         pick = jnp.clip((offset - step) % span - base_of(half, span, batches), 0, batches - 1)
         tops.append(move(lax.dynamic_index_in_dim(top_edges, pick, 0, keepdims=False), last, collect[step]))
 
-    turned, plain, hidden, node_pre, feats_turned = call(
+    ready = call(
         functools.partial(ready_kernel, span, batches),
         "ready",
-        [SMEM] + [VMEM] * 8,
+        [SMEM, VMEM, VMEM] + [ANY] * (span - 1),
         [
             jax.ShapeDtypeStruct((7, width, width), BF),
-            jax.ShapeDtypeStruct((3, width, width), BF),
             like(2 * node_count),
             like(node_count, kind=F32),
             like(width, node_count),
-        ],
+        ]
+        + [like(count + PAD)] * (span - 1),
         [],
         4 * 10**8,
         10 * 2**20,
-    )(info, layer_nodes, w_send, w_recv, w_node, w_edge, w_msg, w_agg, w_out)
-
-    act, slope, part, hot, hots = call(
-        functools.partial(forward_kernel, span, batches, chunk),
+        {3 + step: 4 + step for step in range(span - 1)},
+        passed=span - 1,
+    )(info, layer_nodes, weights, *second_out)
+    turned, hidden, node_pre, feats_turned = ready[:4]
+    second_in = [move(piece, groups_of[1], collect[step + 1]) for step, piece in enumerate(ready[4:])]
+
+    act, slope, part, hot, hots, pieces = call(
+        functools.partial(forward_kernel, span, batches, chunk, sections),
         "forward",
-        [SMEM] + [VMEM] * (span + 3),
-        [like(total), like(total), like(node_count), like(total, node_count), like(2 * node_count, total)],
-        [pltpu.VMEM((total, width), BF), pltpu.VMEM((total, 2 * node_count), BF)],
+        [SMEM] + [VMEM] * (2 * span + 1),
+        [like(total), like(total), like(node_count), like(total, node_count), like(2 * node_count, total), like(total)],
+        [pltpu.VMEM((total, 2 * node_count), BF), pltpu.VMEM((span, PAD, count), BF)],
         2 * 10**9,
         6 * 2**20,
-    )(info, layer_edges, own_index, *pieces, hidden, plain)
+    )(info, own, *first_in, *second_in, hidden, weights)
 
     swap = [(worker(m, h), worker(m, 1 - h)) for m, h in works]
     part_other = move(part, every, swap)
     edges_turned, act_turned = call(
-        functools.partial(turn_kernel, span, batches),
+        turn_kernel,
         "turn",
-        [SMEM] + [VMEM] * (span + 1),
+        [VMEM] * 2,
         [like(width, total), like(width, total)],
         [],
         0,
         4 * 2**20,
-    )(info, layer_edges, act, *pieces)
+    )(pieces, act)
     node_pack = call(
         node_kernel,
         "node_forward",
@@ -477,7 +474,7 @@
         [],
         10**5,
         2**10,
-    )(node_pre, part, part_other, plain, edges_turned)
+    )(node_pre, part, part_other, weights, edges_turned)
 
     kept = [like(total + node_count), like(node_count), like(2 * total + 4 * node_count)]
     both_ways = [(worker(m, h), worker(m, h)) for m, h in works]

time: 170 us -> 151 us (0.89)
  Pallas kernels: 44.1 us -> 21.9 us
  starting transfers between devices: 20.3 us -> 24.7 us
    pallas_call x1, Pallas kernels: 25.7 us -> 3.3 us  [body(): call(functools.partial(pack_kernel, span, batches), 'pack', [SMEM, ANY, A...]
    ppermute x20 -> x23, starting transfers between devices: 20.3 us -> 24.7 us  [move(): return lax.ppermute(value, axes, pairs)]
    unnamed x26 -> x40, local copies, waits for them, and re-layouts: 10.5 us -> 8.97 us
    ppermute x20 -> x23, waiting for transfers between devices: 92.8 us -> 93.2 us  [move(): return lax.ppermute(value, axes, pairs)]
  transfers between devices with their start and end apart: 20 -> 23, of which waited for: 4 -> 6; matrix products, arithmetic and copies ran while one was open for 0% -> 2% of each run, Pallas kernels for 2% -> 2%
where the time goes in v4:
time: 151 us
  waiting for transfers between devices  93.2 us (62%)
  starting transfers between devices  24.7 us (16%)
  Pallas kernels  21.9 us (15%)
  local copies, waits for them, and re-layouts  9.06 us (6%)
    ppermute x23, waiting for transfers between devices, move(): return lax.ppermute(value, axes, pairs)  93.2 us
    ppermute x23, starting transfers between devices, move(): return lax.ppermute(value, axes, pairs)  24.7 us
    unnamed x40, local copies, waits for them, and re-layouts  8.97 us
    pallas_call x4, Pallas kernels, body(): call(functools.partial(chain_kernel, span, batches, chunk, first, layer),...  7.23 us
    pallas_call x1, Pallas kernels, body(): call(functools.partial(forward_kernel, span, batches, chunk, sections), '...  3.99 us
    pallas_call x1, Pallas kernels, body(): call(functools.partial(pack_kernel, span, batches), 'pack', [SMEM, ANY, A...  3.3 us
  transfers between devices with their start and end apart: 23, of which 6 were waited for; matrix products, arithmetic and copies ran while one was open for 2% of the time, Pallas kernels for 2%

profile of v4, /device:TPU:26, one launch (start us, length us, event | category | flops | bytes accessed | tf_op | source)
XLA Modules:
  0.0 150.7 jit_solution(4290971996388523637)
XLA Ops:
  1.2 3.3 %pack.1 = (bf16[272,512]{1,0:T(8,128)(2,1)}, bf16[272,512]{1,0:T(8,128)(2,1)}, bf16[272,512]{1,0:T(8,128)(2,1)}, bf16[272,512]{1,0:T(8,128)(2,1)}, bf16[272,512]...) custom-call(s32[2]{0:T(128)} %pad_add_fusion.info, s32[2,256]{1,0:T(2,128)} %senders.1, ...), custom_call_target="tpu_custom_call" | custom-call | bytes 1048576 | tf_op jit(solution)/shard_map/pack/pallas_call | solution.py:403
  4.6 0.8 collective-permute-start
  6.1 1.5 %collective-permute-start.2 = (bf16[272,512]{1,0:T(8,128)(2,1)}, bf16[272,512]{1,0:T(8,128)(2,1)}, u32[]{:S(2)}, u32[]{:S(2)}) collective-permute-start(bf16[272,512]{1,0:T(8,128)(2,1)} %get-tuple-element.53), channel_id=1, source_target_pairs={{25,26},{26,27},{31,28},{28,29},{9,10},{10,11},{15,12},{12,13}} | collective-permute-start | bytes 835592 | tf_op jit(solution)/shard_map/ppermute | solution.py:393
  7.7 1.1 constant_dynamic-update-slice_fusion.6
  8.8 1.1 constant_dynamic-update-slice_fusion.5
  9.8 1.1 constant_dynamic-update-slice_fusion.4
  11.2 1.6 %ready.1 = (bf16[7,512,512]{2,1,0:T(8,128)(2,1)S(1)}, bf16[512,512]{1,0:T(8,128)(2,1)S(1)}, f32[256,512]{1,0:T(8,128)S(1)}, bf16[512,256]{1,0:T(8,128)(2,1)S(1)}...) custom-call(s32[2]{0:T(128)S(1)} %copy-done.10, ...), custom_call_target="tpu_custom_call", output_to_operand_aliasing={{4}: (3, {}), {5}: (4, {}), {6}: (5, {})} | custom-call | flops 400000000 | bytes 10485760 | tf_op jit(solution)/shard_map/ready/pallas_call | solution.py:428
  13.0 1.8 %copy-done = bf16[7,512,512]{2,1,0:T(8,128)(2,1)} copy-done((bf16[7,512,512]{2,1,0:T(8,128)(2,1)}, bf16[7,512,512]{2,1,0:T(8,128)(2,1)S(1)}, u32[]{:S(2)}) %copy-start) | copy-done | bytes 3670040
  14.7 1.4 collective-permute-start.3
  16.1 4.0 %collective-permute-start.4 = (bf16[272,512]{1,0:T(8,128)(2,1)S(1)}, bf16[272,512]{1,0:T(8,128)(2,1)}, u32[]{:S(2)}, u32[]{:S(2)}) collective-permute-start(bf16[272,512]{1,0:T(8,128)(2,1)S(1)} %get-tuple-element.58), channel_id=1, source_target_pairs={{16,18},{17,19},{22,20},{23,21},{0,2},{1,3},{6,4},{7,5}} | collective-permute-start | bytes 835592 | tf_op jit(solution)/shard_map/ppermute | solution.py:393
  20.2 2.0 %collective-permute-start.5 = (bf16[272,512]{1,0:T(8,128)(2,1)S(1)}, bf16[272,512]{1,0:T(8,128)(2,1)}, u32[]{:S(2)}, u32[]{:S(2)}) collective-permute-start(bf16[272,512]{1,0:T(8,128)(2,1)S(1)} %get-tuple-element.59), channel_id=1, source_target_pairs={{17,18},{18,19},{23,20},{20,21},{1,2},{2,3},{7,4},{4,5}} | collective-permute-start | bytes 835592 | tf_op jit(solution)/shard_map/ppermute | solution.py:393
  22.3 1.2 collective-permute-done.4.refs_4_
  23.6 3.0 %collective-permute-done.5.refs_5_ = bf16[272,512]{1,0:T(8,128)(2,1)} collective-permute-done((bf16[272,512]{1,0:T(8,128)(2,1)S(1)}, bf16[272,512]{1,0:T(8,128)(2,1)}, u32[]{:S(2)}, u32[]{:S(2)}) %collective-permute-start.5) | collective-permute-done | bytes 278560 | tf_op jit(solution)/shard_map/ppermute | solution.py:393
  26.5 2.0 %copy-done.3 = bf16[7,512,512]{2,1,0:T(8,128)(2,1)S(1)} copy-done((bf16[7,512,512]{2,1,0:T(8,128)(2,1)S(1)}, bf16[7,512,512]{2,1,0:T(8,128)(2,1)}, u32[]{:S(2)}) %copy-start.3) | copy-done | bytes 3670040
  28.6 4.0 %forward.1 = (bf16[1024,512]{1,0:T(8,128)(2,1)S(1)}, bf16[1024,512]{1,0:T(8,128)(2,1)S(1)}, bf16[256,512]{1,0:T(8,128)(2,1)S(1)}, bf16[1024,256]{1,0:T(8,128)(2,...) custom-call(s32[2]{0:T(128)S(1)} %copy-done.10, bf16[272,512]{1,0:T(8,128)(2,1)S(1)} %copy-done.12, ...), custom_call_target="tpu_custom_call" | custom-call | flops 2000000000 | bytes 6291456 | tf_op jit(solution)/shard_map/forward/pallas_call | solution.py:448
  36.5 1.5 %copy-done.1 = bf16[7,512,512]{2,1,0:T(8,128)(2,1)S(1)} copy-done((bf16[7,512,512]{2,1,0:T(8,128)(2,1)S(1)}, bf16[7,512,512]{2,1,0:T(8,128)(2,1)}, u32[]{:S(2)}) %copy-start.1) | copy-done | bytes 3670040
  38.7 0.7 collective-permute-start.10
  40.1 1.1 chain.5
  41.3 0.7 collective-permute-start.12
  42.7 1.3 chain.6
  44.0 0.7 collective-permute-start.14
  45.5 4.3 %chain.7 = (bf16[1280,512]{1,0:T(8,128)(2,1)S(1)}, bf16[256,512]{1,0:T(8,128)(2,1)}, bf16[3072,512]{1,0:T(8,128)(2,1)S(1)}) custom-call(s32[2]{0:T(128)S(1)} %copy-done.10, bf16[1280,512]{1,0:T(8,128)(2,1)S(1)} %collective-permute-done.14.refs_0_, ...), custom_call_target="tpu_custom_call", output_to_operand_aliasing={{0}: (3, {}), {2}: (4, {})} | custom-call | flops 3000000000 | bytes 10485760 | tf_op jit(solution)/shard_map/chain/pallas_call | solution.py:492
  49.7 2.8 %weight_grads.1 = (bf16[640,512]{1,0:T(8,128)(2,1)S(1)}, bf16[640,512]{1,0:T(8,128)(2,1)S(1)}, bf16[640,512]{1,0:T(8,128)(2,1)S(1)}, bf16[640,512]{1,0:T(8,128)(...) custom-call(s32[2]{0:T(128)S(1)} %copy-done.10, ...), custom_call_target="tpu_custom_call" | custom-call | flops 2000000000 | bytes 10485760 | tf_op jit(solution)/shard_map/weight_grads/pallas_call | solution.py:507
  54.7 1.3 collective-permute-start.17
  56.0 1.3 collective-permute-start.18
  57.3 1.3 collective-permute-start.21
  58.6 1.3 collective-permute-start.22
  59.9 67.0 %collective-permute-done.21.refs_6_ = bf16[384,512]{1,0:T(8,128)(2,1)S(1)} collective-permute-done((bf16[384,512]{1,0:T(8,128)(2,1)S(1)}, bf16[384,512]{1,0:T(8,128)(2,1)S(1)}, u32[]{:S(2)}, u32[]{:S(2)}) %collective-permute-start.21) | collective-permute-done | bytes 393248 | tf_op jit(solution)/shard_map/ppermute | solution.py:393
  126.9 4.2 %collective-permute-done.22.refs_7_ = bf16[384,512]{1,0:T(8,128)(2,1)S(1)} collective-permute-done((bf16[384,512]{1,0:T(8,128)(2,1)S(1)}, bf16[384,512]{1,0:T(8,128)(2,1)S(1)}, u32[]{:S(2)}, u32[]{:S(2)}) %collective-permute-start.22) | collective-permute-done | bytes 393248 | tf_op jit(solution)/shard_map/ppermute | solution.py:393
  131.1 15.3 %collective-permute-done.17.refs_2_ = bf16[640,512]{1,0:T(8,128)(2,1)S(1)} collective-permute-done((bf16[640,512]{1,0:T(8,128)(2,1)S(1)}, bf16[640,512]{1,0:T(8,128)(2,1)S(1)}, u32[]{:S(2)}, u32[]{:S(2)}) %collective-permute-start.17) | collective-permute-done | bytes 655392 | tf_op jit(solution)/shard_map/ppermute | solution.py:393
  146.4 2.5 %collective-permute-done.18.refs_3_ = bf16[640,512]{1,0:T(8,128)(2,1)S(1)} collective-permute-done((bf16[640,512]{1,0:T(8,128)(2,1)S(1)}, bf16[640,512]{1,0:T(8,128)(2,1)S(1)}, u32[]{:S(2)}, u32[]{:S(2)}) %collective-permute-start.18) | collective-permute-done | bytes 655392 | tf_op jit(solution)/shard_map/ppermute | solution.py:393
  148.9 1.9 %finish.1 = (bf16[1,2,32,512]{3,2,1,0:T(8,128)(2,1)}, bf16[1,2,256,512]{3,2,1,0:T(8,128)(2,1)}, f32[1,64,512]{2,1,0:T(8,128)}, f32[1,64,512]{2,1,0:T(8,128)}, f3...) custom-call(s32[2]{0:T(128)S(1)} %copy-done.10, ...), custom_call_target="tpu_custom_call" | custom-call | bytes 5242880 | tf_op jit(solution)/shard_map/finish/pallas_call | solution.py:520
  (68 shorter events, 10.2 us)
Async XLA Ops:
  0.6 10.3 %copy-start.13 = (bf16[1,512,512]{2,1,0:T(8,128)(2,1)S(1)}, bf16[1,512,512]{2,1,0:T(8,128)(2,1)}, u32[]{:S(2)}) copy-start(bf16[1,512,512]{2,1,0:T(8,128)(2,1)} %param.24) | copy-start | bytes 1572868
  4.6 6.4 %copy-start.14 = (bf16[1,512,512]{2,1,0:T(8,128)(2,1)S(1)}, bf16[1,512,512]{2,1,0:T(8,128)(2,1)}, u32[]{:S(2)}) copy-start(bf16[1,512,512]{2,1,0:T(8,128)(2,1)} %param.25) | copy-start | bytes 1572868
  4.6 6.5 %copy-start.15 = (bf16[1,512,512]{2,1,0:T(8,128)(2,1)S(1)}, bf16[1,512,512]{2,1,0:T(8,128)(2,1)}, u32[]{:S(2)}) copy-start(bf16[1,512,512]{2,1,0:T(8,128)(2,1)} %param.26) | copy-start | bytes 1572868
  4.6 6.5 %copy-start.16 = (bf16[1,512,512]{2,1,0:T(8,128)(2,1)S(1)}, bf16[1,512,512]{2,1,0:T(8,128)(2,1)}, u32[]{:S(2)}) copy-start(bf16[1,512,512]{2,1,0:T(8,128)(2,1)} %param.27) | copy-start | bytes 1572868
  4.6 15.6 %collective-permute-start = (bf16[272,512]{1,0:T(8,128)(2,1)}, bf16[272,512]{1,0:T(8,128)(2,1)S(1)}, u32[]{:S(2)}, u32[]{:S(2)}) collective-permute-start(bf16[272,512]{1,0:T(8,128)(2,1)} %get-tuple-element.51), channel_id=1, source_target_pairs={{27,26},{24,27},{29,28},{30,29},{11,10},{8,11},{13,12},{14,13}} | collective-permute-start | bytes 835592 | tf_op jit(solution)/shard_map/ppermute | solution.py:393
  5.4 16.9 %collective-permute-start.1 = (bf16[272,512]{1,0:T(8,128)(2,1)}, bf16[272,512]{1,0:T(8,128)(2,1)S(1)}, u32[]{:S(2)}, u32[]{:S(2)}) collective-permute-start(bf16[272,512]{1,0:T(8,128)(2,1)} %get-tuple-element.52), channel_id=1, source_target_pairs={{24,26},{25,27},{30,28},{31,29},{8,10},{9,11},{14,12},{15,13}} | collective-permute-start | bytes 835592 | tf_op jit(solution)/shard_map/ppermute | solution.py:393
  6.1 5.1 %copy-start.6 = (bf16[1,2,256,512]{3,2,1,0:T(8,128)(2,1)S(1)}, bf16[1,2,256,512]{3,2,1,0:T(8,128)(2,1)}, u32[]{:S(2)}) copy-start(bf16[1,2,256,512]{3,2,1,0:T(8,128)(2,1)} %nodes.1) | copy-start | bytes 1572868
  6.1 5.1 %copy-start.7 = (bf16[272,512]{1,0:T(8,128)(2,1)S(1)}, bf16[272,512]{1,0:T(8,128)(2,1)}, u32[]{:S(2)}) copy-start(bf16[272,512]{1,0:T(8,128)(2,1)} %get-tuple-element.54.refs_0_) | copy-start | bytes 835588
  6.1 16.1 %collective-permute-start.2 = (bf16[272,512]{1,0:T(8,128)(2,1)}, bf16[272,512]{1,0:T(8,128)(2,1)}, u32[]{:S(2)}, u32[]{:S(2)}) collective-permute-start(bf16[272,512]{1,0:T(8,128)(2,1)} %get-tuple-element.53), channel_id=1, source_target_pairs={{25,26},{26,27},{31,28},{28,29},{9,10},{10,11},{15,12},{12,13}} | collective-permute-start | bytes 835592 | tf_op jit(solution)/shard_map/ppermute | solution.py:393
  11.0 11.2 %copy-start.5 = (bf16[2,256,512]{2,1,0:T(8,128)(2,1)S(1)}, bf16[2,256,512]{2,1,0:T(8,128)(2,1)}, u32[]{:S(2)}) copy-start(bf16[2,256,512]{2,1,0:T(8,128)(2,1)} %refs_1_.1) | copy-start | bytes 1572868
  11.1 15.4 %copy-start.12 = (bf16[272,512]{1,0:T(8,128)(2,1)S(1)}, bf16[272,512]{1,0:T(8,128)(2,1)}, u32[]{:S(2)}) copy-start(bf16[272,512]{1,0:T(8,128)(2,1)} %get-tuple-element.50.own) | copy-start | bytes 835588
  14.7 7.6 %collective-permute-start.3 = (bf16[272,512]{1,0:T(8,128)(2,1)S(1)}, bf16[272,512]{1,0:T(8,128)(2,1)}, u32[]{:S(2)}, u32[]{:S(2)}) collective-permute-start(bf16[272,512]{1,0:T(8,128)(2,1)S(1)} %get-tuple-element.57), channel_id=1, source_target_pairs={{19,18},{16,19},{21,20},{22,21},{3,2},{0,3},{5,4},{6,5}} | collective-permute-start | bytes 835592 | tf_op jit(solution)/shard_map/ppermute | solution.py:393
  16.1 7.4 %collective-permute-start.4 = (bf16[272,512]{1,0:T(8,128)(2,1)S(1)}, bf16[272,512]{1,0:T(8,128)(2,1)}, u32[]{:S(2)}, u32[]{:S(2)}) collective-permute-start(bf16[272,512]{1,0:T(8,128)(2,1)S(1)} %get-tuple-element.58), channel_id=1, source_target_pairs={{16,18},{17,19},{22,20},{23,21},{0,2},{1,3},{6,4},{7,5}} | collective-permute-start | bytes 835592 | tf_op jit(solution)/shard_map/ppermute | solution.py:393
  20.2 6.3 %collective-permute-start.5 = (bf16[272,512]{1,0:T(8,128)(2,1)S(1)}, bf16[272,512]{1,0:T(8,128)(2,1)}, u32[]{:S(2)}, u32[]{:S(2)}) collective-permute-start(bf16[272,512]{1,0:T(8,128)(2,1)S(1)} %get-tuple-element.59), channel_id=1, source_target_pairs={{17,18},{18,19},{23,20},{20,21},{1,2},{2,3},{7,4},{4,5}} | collective-permute-start | bytes 835592 | tf_op jit(solution)/shard_map/ppermute | solution.py:393
  28.6 7.4 %copy-start.4 = (bf16[7,512,512]{2,1,0:T(8,128)(2,1)S(1)}, bf16[7,512,512]{2,1,0:T(8,128)(2,1)}, u32[]{:S(2)}) copy-start(bf16[7,512,512]{2,1,0:T(8,128)(2,1)} %copy-done.2) | copy-start | bytes 11010052
  32.6 3.4 %collective-permute-start.6 = (bf16[256,512]{1,0:T(8,128)(2,1)S(1)}, bf16[256,512]{1,0:T(8,128)(2,1)S(1)}, u32[]{:S(2)}, u32[]{:S(2)}) collective-permute-start(bf16[256,512]{1,0:T(8,128)(2,1)S(1)} %get-tuple-element.67.part_own), channel_id=1, source_target_pairs={{2,4},{3,5},{4,2},{5,3},{10,12},{11,13},{12,10},{13,11},{18,20},{1... | collective-permute-start | bytes 786440 | tf_op jit(solution)/shard_map/ppermute | solution.py:393
  33.3 3.2 %collective-permute-start.9 = (bf16[256,512]{1,0:T(8,128)(2,1)S(1)}, bf16[256,512]{1,0:T(8,128)(2,1)S(1)}, u32[]{:S(2)}, u32[]{:S(2)}) collective-permute-start(bf16[256,512]{1,0:T(8,128)(2,1)S(1)} %get-tuple-element.91), channel_id=1, source_target_pairs={{25,26},{26,27},{31,28},{28,29}} | collective-permute-start | bytes 786440 | tf_op jit(solution)/shard_map/ppermute | solution.py:393
  34.0 2.5 %collective-permute-start.8 = (bf16[256,512]{1,0:T(8,128)(2,1)S(1)}, bf16[256,512]{1,0:T(8,128)(2,1)S(1)}, u32[]{:S(2)}, u32[]{:S(2)}) collective-permute-start(bf16[256,512]{1,0:T(8,128)(2,1)S(1)} %get-tuple-element.92), channel_id=1, source_target_pairs={{24,26},{25,27},{30,28},{31,29}} | collective-permute-start | bytes 786440 | tf_op jit(solution)/shard_map/ppermute | solution.py:393
  34.6 1.8 %collective-permute-start.7 = (bf16[256,512]{1,0:T(8,128)(2,1)S(1)}, bf16[256,512]{1,0:T(8,128)(2,1)S(1)}, u32[]{:S(2)}, u32[]{:S(2)}) collective-permute-start(bf16[256,512]{1,0:T(8,128)(2,1)S(1)} %get-tuple-element.93), channel_id=1, source_target_pairs={{27,26},{24,27},{29,28},{30,29}} | collective-permute-start | bytes 786440 | tf_op jit(solution)/shard_map/ppermute | solution.py:393
  38.7 1.5 collective-permute-start.10
  39.4 0.7 collective-permute-start.11
  41.3 1.5 collective-permute-start.12
  42.0 0.7 collective-permute-start.13
  44.0 1.5 collective-permute-start.14
  44.8 0.7 collective-permute-start.15
  52.6 4.7 %collective-permute-start.19 = (bf16[384,512]{1,0:T(8,128)(2,1)S(1)}, bf16[384,512]{1,0:T(8,128)(2,1)S(1)}, u32[]{:S(2)}, u32[]{:S(2)}) collective-permute-start(bf16[384,512]{1,0:T(8,128)(2,1)S(1)} %get-tuple-element.87), channel_id=1, source_target_pairs={{2,4},{3,5},{4,0},{5,1},{10,12},{11,13},{12,8},{13,9},{18,20},{19,... | collective-permute-start | bytes 1179656 | tf_op jit(solution)/shard_map/ppermute | solution.py:393
  53.3 5.3 %collective-permute-start.20 = (bf16[384,512]{1,0:T(8,128)(2,1)S(1)}, bf16[384,512]{1,0:T(8,128)(2,1)S(1)}, u32[]{:S(2)}, u32[]{:S(2)}) collective-permute-start(bf16[384,512]{1,0:T(8,128)(2,1)S(1)} %get-tuple-element.88), channel_id=1, source_target_pairs={{2,5},{3,6},{4,1},{5,2},{10,13},{11,14},{12,9},{13,10},{18,21},{19... | collective-permute-start | bytes 1179656 | tf_op jit(solution)/shard_map/ppermute | solution.py:393
  54.0 77.1 %collective-permute-start.16 = (bf16[640,512]{1,0:T(8,128)(2,1)S(1)}, bf16[640,512]{1,0:T(8,128)(2,1)S(1)}, u32[]{:S(2)}, u32[]{:S(2)}) collective-permute-start(bf16[640,512]{1,0:T(8,128)(2,1)S(1)} %get-tuple-element.84), channel_id=1, source_target_pairs={{2,3},{3,0},{4,5},{5,6},{10,11},{11,8},{12,13},{13,14},{18,19},{19... | collective-permute-start | bytes 1966088 | tf_op jit(solution)/shard_map/ppermute | solution.py:393
  54.7 91.7 %collective-permute-start.17 = (bf16[640,512]{1,0:T(8,128)(2,1)S(1)}, bf16[640,512]{1,0:T(8,128)(2,1)S(1)}, u32[]{:S(2)}, u32[]{:S(2)}) collective-permute-start(bf16[640,512]{1,0:T(8,128)(2,1)S(1)} %get-tuple-element.85), channel_id=1, source_target_pairs={{2,0},{3,1},{4,6},{5,7},{10,8},{11,9},{12,14},{13,15},{18,16},{19,... | collective-permute-start | bytes 1966088 | tf_op jit(solution)/shard_map/ppermute | solution.py:393
  56.0 92.9 %collective-permute-start.18 = (bf16[640,512]{1,0:T(8,128)(2,1)S(1)}, bf16[640,512]{1,0:T(8,128)(2,1)S(1)}, u32[]{:S(2)}, u32[]{:S(2)}) collective-permute-start(bf16[640,512]{1,0:T(8,128)(2,1)S(1)} %get-tuple-element.86), channel_id=1, source_target_pairs={{2,1},{3,2},{4,7},{5,4},{10,9},{11,10},{12,15},{13,12},{18,17},{19... | collective-permute-start | bytes 1966088 | tf_op jit(solution)/shard_map/ppermute | solution.py:393
  57.3 69.6 %collective-permute-start.21 = (bf16[384,512]{1,0:T(8,128)(2,1)S(1)}, bf16[384,512]{1,0:T(8,128)(2,1)S(1)}, u32[]{:S(2)}, u32[]{:S(2)}) collective-permute-start(bf16[384,512]{1,0:T(8,128)(2,1)S(1)} %get-tuple-element.89), channel_id=1, source_target_pairs={{2,6},{3,7},{4,2},{5,3},{10,14},{11,15},{12,10},{13,11},{18,22},{1... | collective-permute-start | bytes 1179656 | tf_op jit(solution)/shard_map/ppermute | solution.py:393
  58.6 72.5 %collective-permute-start.22 = (bf16[384,512]{1,0:T(8,128)(2,1)S(1)}, bf16[384,512]{1,0:T(8,128)(2,1)S(1)}, u32[]{:S(2)}, u32[]{:S(2)}) collective-permute-start(bf16[384,512]{1,0:T(8,128)(2,1)S(1)} %get-tuple-element.90), channel_id=1, source_target_pairs={{2,7},{3,4},{4,3},{5,0},{10,15},{11,12},{12,11},{13,8},{18,23},{19... | collective-permute-start | bytes 1179656 | tf_op jit(solution)/shard_map/ppermute | solution.py:393
  (8 other events, 25.0 us)

commit v5 on v4

--- a/solution.py
+++ b/solution.py
@@ -73,7 +73,7 @@
     return (sigma * (1.0 + pre * (1.0 - sigma))).astype(BF)
 
 
-def pack_kernel(span, batches, info, senders, receivers, tiles, edges, *refs):
+def pack_kernel(span, batches, info, senders, receivers, tiles, edges, tops, *refs):
     outs, seconds = refs[:span], refs[span : 2 * span - 1]
     send_in, recv_in, sems = refs[2 * span - 1 :]
     member = info[1]
@@ -86,36 +86,41 @@
         pltpu.make_async_copy(senders, send_in, sems.at[0]),
         pltpu.make_async_copy(receivers, recv_in, sems.at[1]),
     ]
-    picks, loads = [], []
+    picks, loads, puts = [], [], []
     for step in range(span):
         batch = lax.rem(offset - step + span, span) - base_of(half, span, batches)
         picks.append(jnp.clip(batch, 0, batches - 1))
-        loads.append(
-            pltpu.make_async_copy(edges.at[0, picks[step]], outs[step].at[pl.ds(0, count)], sems.at[2 + step])
-        )
-    for copy in gets + loads:
+        latents = outs[step].at[pl.ds(0, count)]
+        grads = outs[step].at[pl.ds(count + PAD, count)]
+        loads.append(pltpu.make_async_copy(edges.at[0, picks[step]], latents, sems.at[2 + step]))
+        puts.append(pltpu.make_async_copy(tops.at[picks[step]], grads, sems.at[2 + span + step]))
+    for copy in gets + loads + puts:
         copy.start()
     for copy in gets:
         copy.wait()
     for step in range(span):
         batch = picks[step]
         out = outs[step]
-        out[count:] = jnp.zeros((PAD, out.shape[1]), BF)
+        out[count : count + PAD] = jnp.zeros((PAD, out.shape[1]), BF)
         for tile in range(tile_count):
             lanes = slice(tile * tile_len, (tile + 1) * tile_len)
             send = pick_row(send_in, batch, lanes) + tiles[batch, tile, 0] * BLOCK
             recv = pick_row(recv_in, batch, lanes) + tiles[batch, tile, 1] * BLOCK
             which = lax.broadcasted_iota(jnp.int32, (PAD, tile_len), 0)
             block = jnp.where(which == 0, send, jnp.where(which == 1, recv, 0))
-            out[count:, lanes] = block.astype(F32).astype(BF)
-    for step in range(span):
+            out[count : count + PAD, lanes] = block.astype(F32).astype(BF)
         loads[step].wait()
         if step:
-            seconds[step - 1][...] = outs[step][...]
-
-
-def ready_kernel(span, batches, info, nodes, weights, *refs):
-    turned, hidden, node_pre, feats_turned = refs[span - 1 : span + 3]
+            copy = pltpu.make_async_copy(
+                out.at[pl.ds(0, count + PAD)], seconds[step - 1], sems.at[1 + 2 * span + step]
+            )
+            copy.start()
+            puts.append(copy)
+    for copy in puts:
+        copy.wait()
+
+
+def ready_kernel(span, batches, info, nodes, weights, turned, hidden, node_pre, feats_turned):
     batch = own_batch(info[1], span, batches)
     node_count = nodes.shape[2]
     feats = nodes[0, batch]
@@ -130,19 +135,22 @@
 def forward_kernel(span, batches, chunk, sections, info, own, *refs):
     groups = (refs[: span - 1], refs[span - 1 : 2 * span - 2])
     hidden, weights = refs[2 * span - 2 : 2 * span]
-    act_out, slope_out, part_out, hot_out, hots_out, pieces, both, index = refs[2 * span :]
-    count = own.shape[0] - PAD
+    act_out, slope_out, part_out, hot_out, hots_out, pieces, tops, both, index = refs[2 * span :]
+    count = (own.shape[0] - PAD) // 2
     node_count = part_out.shape[0]
     for which, others in enumerate(groups):
 
         @pl.when(lax.rem(sections - 1 - info[0], 2) == which)
-        def _(others=others):
+        def _(others=others, which=which):
             for step in range(1, span):
                 pieces[step * count : (step + 1) * count] = others[step - 1][:count]
-                index[step] = others[step - 1][count:, :count]
+                index[step] = others[step - 1][count : count + PAD, :count]
+                if which == 0:
+                    tops[step * count : (step + 1) * count] = others[step - 1][count + PAD :]
 
     pieces[:count] = own[:count]
-    index[0] = own[count:, :count]
+    tops[:count] = own[count + PAD :]
+    index[0] = own[count : count + PAD, :count]
     for step in range(span):
         run = slice(step * count, (step + 1) * count)
         index_rows = index[step]
@@ -180,42 +188,40 @@
     out[2 * count :] = slope_of(pre, sigma)
 
 
-def chain_kernel(span, batches, chunk, first, active, info, *refs):
-    kept = None
-    if not first and len(refs) == 12:
-        kept = refs[2:4]
-        refs = refs[:2] + refs[4:]
+def chain_kernel(span, batches, chunk, first, split, active, info, *refs):
+    incoming = refs[:2] if first else refs[:3]
+    refs = refs[len(incoming) :]
+    kept = ()
+    if not first:
+        kept, refs = refs[:2], refs[2:]
+    common, refs = refs[:5], refs[5:]
 
     @pl.when(info[0] == active)
     def _():
-        chain_step(span, batches, chunk, first, info, *refs)
-
-    if kept is not None:
+        chain_step(span, batches, chunk, first, split, info, incoming, *common, *refs)
+
+    if kept:
 
         @pl.when(info[0] != active)
         def _():
-            refs[-3][...] = kept[0][...]
-            refs[-1][...] = kept[1][...]
-
-
-def chain_step(span, batches, chunk, first, info, *refs):
+            refs[0][...] = kept[0][...]
+            refs[1][...] = kept[1][...]
+
+
+def chain_step(
+    span, batches, chunk, first, split, info, incoming, hot, hots, slope, node_pack, turned, pay, keep, part_out, *rest
+):
     member = info[1]
     batch = own_batch(member, span, batches)
     half = lax.div(member, span)
+    total = slope.shape[0]
     if first:
-        top_nodes, top_edges = refs[:2]
-        others = refs[2 : span + 1]
-        hot, hots, slope, node_pack, turned, pay, part_out, keep, came = refs[span + 1 :]
-        count = top_edges.shape[1]
-        for step in range(span):
-            came[step * count : (step + 1) * count] = others[step - 1][...] if step else top_edges[batch]
+        top_nodes, came = incoming
         grad = top_nodes[batch]
     else:
-        came, cross = refs[:2]
-        hot, hots, slope, node_pack, turned, pay, part_out, keep = refs[2:]
-        total = slope.shape[0]
-        grad = (came[total:].astype(F32) + cross[...].astype(F32)).astype(BF)
-    total = slope.shape[0]
+        came, part_own, cross = incoming
+        mine = part_own[...] if part_own.shape[0] == cross.shape[0] else came[total:]
+        grad = (mine.astype(F32) + cross[...].astype(F32)).astype(BF)
     node_count = part_out.shape[0]
     node_at = 2 * total
     delta = (matmul(grad, turned[OUT]) * node_pack[2 * node_count :].astype(F32)).astype(BF)
@@ -224,12 +230,15 @@
     keep[node_at + node_count : node_at + 2 * node_count] = grad
     for at in range(0, total, chunk):
         run = slice(at, at + chunk)
-        incoming = came[run].astype(F32)
-        message_grad = (incoming + matmul(hot[run], agg_grad)).astype(BF)
+        before = came[run].astype(F32)
+        message_grad = (before + matmul(hot[run], agg_grad)).astype(BF)
         keep[run] = message_grad
         edge_delta = (matmul(message_grad, turned[MSG]) * slope[run].astype(F32)).astype(BF)
         keep[total + at : total + at + chunk] = edge_delta
-        pay[run] = (incoming + matmul(edge_delta, turned[EDGE])).astype(BF)
+        below = (before + matmul(edge_delta, turned[EDGE])).astype(BF)
+        pay[run] = below
+        if split:
+            rest[0][run] = below
     sums = matmul(hots[...], keep[total : 2 * total]).astype(BF)
     keep[node_at + 2 * node_count :] = sums
     own = grad.astype(F32) + matmul(delta, turned[NODE])
@@ -403,53 +412,48 @@
     packed = call(
         functools.partial(pack_kernel, span, batches),
         "pack",
-        [SMEM, ANY, ANY, SMEM, ANY],
-        [like(count + PAD)] * (2 * span - 1),
+        [SMEM, ANY, ANY, SMEM, ANY, ANY],
+        [like(2 * count + PAD)] * span + [like(count + PAD)] * (span - 1),
         [
             pltpu.VMEM((batches, count), jnp.int32),
             pltpu.VMEM((batches, count), jnp.int32),
-            pltpu.SemaphoreType.DMA((2 + span,)),
+            pltpu.SemaphoreType.DMA((2 + 3 * span,)),
         ],
         0,
         2**20,
-        grant=62,
-    )(info, senders, receivers, tile_blocks, layer_edges)
+        passed=span - 1,
+    )(info, senders, receivers, tile_blocks, layer_edges, top_edges)
     own, first_out, second_out = packed[0], packed[1:span], packed[span:]
     groups_of = [list(range(sections - 1 - group, -1, -2)) for group in range(2)]
     first_in = [move(piece, groups_of[0], collect[step + 1]) for step, piece in enumerate(first_out)]
+    own, w_send, w_recv, w_edge, w_msg, w_node, w_agg, w_out = lax.optimization_barrier(
+        (own, w_send, w_recv, w_edge, w_msg, w_node, w_agg, w_out)
+    )
     weights = jnp.concatenate([w_send, w_recv, w_edge, w_msg, w_node, w_agg, w_out], axis=0)
-    half = member // span
-    offset = member % span
-    tops = []
-    for step in range(1, span):
-        pick = jnp.clip((offset - step) % span - base_of(half, span, batches), 0, batches - 1)
-        tops.append(move(lax.dynamic_index_in_dim(top_edges, pick, 0, keepdims=False), last, collect[step]))
-
     ready = call(
         functools.partial(ready_kernel, span, batches),
         "ready",
-        [SMEM, VMEM, VMEM] + [ANY] * (span - 1),
+        [SMEM, VMEM, VMEM],
         [
             jax.ShapeDtypeStruct((7, width, width), BF),
             like(2 * node_count),
             like(node_count, kind=F32),
             like(width, node_count),
-        ]
-        + [like(count + PAD)] * (span - 1),
+        ],
         [],
         4 * 10**8,
         10 * 2**20,
-        {3 + step: 4 + step for step in range(span - 1)},
-        passed=span - 1,
-    )(info, layer_nodes, weights, *second_out)
-    turned, hidden, node_pre, feats_turned = ready[:4]
-    second_in = [move(piece, groups_of[1], collect[step + 1]) for step, piece in enumerate(ready[4:])]
-
-    act, slope, part, hot, hots, pieces = call(
+    )(info, layer_nodes, weights)
+    turned, hidden, node_pre, feats_turned = ready
+    first_in[0], second_out = lax.optimization_barrier((first_in[0], second_out))
+    second_in = [move(piece, groups_of[1], collect[step + 1]) for step, piece in enumerate(second_out)]
+
+    act, slope, part, hot, hots, pieces, tops = call(
         functools.partial(forward_kernel, span, batches, chunk, sections),
         "forward",
         [SMEM] + [VMEM] * (2 * span + 1),
-        [like(total), like(total), like(node_count), like(total, node_count), like(2 * node_count, total), like(total)],
+        [like(total), like(total), like(node_count), like(total, node_count), like(2 * node_count, total)]
+        + [like(total)] * 2,
         [pltpu.VMEM((total, 2 * node_count), BF), pltpu.VMEM((span, PAD, count), BF)],
         2 * 10**9,
         6 * 2**20,
@@ -476,7 +480,6 @@
         2**10,
     )(node_pre, part, part_other, weights, edges_turned)
 
-    kept = [like(total + node_count), like(node_count), like(2 * total + 4 * node_count)]
     both_ways = [(worker(m, h), worker(m, h)) for m, h in works]
     rows = 5 * share + share // 2 + node_share
     pay = keep = None
@@ -484,25 +487,28 @@
     for moment in range(sections):
         first = moment == 0
         layer = sections - 1 - moment
-        in_place = not first
-        if first:
-            inputs = (top_nodes, top_edges, *tops)
-        else:
-            inputs = (*incoming, pay, keep)
-        pay, part, keep = call(
-            functools.partial(chain_kernel, span, batches, chunk, first, layer),
+        split = layer > 0 and layer % 2 == 0
+        inputs = (top_nodes, tops) if first else (*incoming, pay, keep)
+        made = call(
+            functools.partial(chain_kernel, span, batches, chunk, first, split, layer),
             "chain",
             [SMEM] + [VMEM] * (len(inputs) + 5),
-            kept,
-            [pltpu.VMEM((total, width), BF)] if first else [],
+            [like(total + node_count), like(2 * total + 4 * node_count), like(node_count)]
+            + [like(total)] * split,
+            [],
             3 * 10**9,
             10 * 2**20,
-            {3: 0, 4: 2} if in_place else {},
+            {} if first else {4: 0, 5: 1},
         )(info, *inputs, hot, hots, slope, node_pack, turned)
-        if layer > 0:
+        pay, keep, part = made[:3]
+        if split:
+            mine = move(part, [layer], both_ways, -1)
+            came = move(made[3], [layer], both_ways, -1)
+            incoming = (came, mine, move(mine, [layer - 1], swap))
+        elif layer > 0:
             cross = move(part, [layer], swap, -1)
             came = move(pay, [layer], both_ways, -1)
-            incoming = (came, cross)
+            incoming = (came, info, cross)
 
     out = call(
         functools.partial(grads_kernel, span, batches, groups),

time: 151 us -> 155 us (1.026)
  waiting for transfers between devices: 93.2 us -> 105 us
  starting transfers between devices: 24.7 us -> 21.1 us
  Pallas kernels: 21.9 us -> 18.9 us
    ppermute x23 -> x21, waiting for transfers between devices: 93.2 us -> 105 us  [move(): return lax.ppermute(value, axes, pairs)]
    ppermute x23 -> x21, starting transfers between devices: 24.7 us -> 21.1 us  [move(): return lax.ppermute(value, axes, pairs)]
    pallas_call x1, Pallas kernels: 3.3 us -> 1.05 us  [body(): call(functools.partial(pack_kernel, span, batches), 'pack', [SMEM, ANY, A...]
    unnamed x40 -> x28, local copies, waits for them, and re-layouts: 8.97 us -> 8.14 us
  transfers between devices with their start and end apart: 23 -> 21, of which waited for: 6 -> 6; matrix products, arithmetic and copies ran while one was open for 2% -> 2% of each run, Pallas kernels for 2% -> 1%
where the time goes in v5:
time: 155 us; the launch traced here: 154 us
  waiting for transfers between devices  105 us (68%)
  starting transfers between devices  21.1 us (14%)
  Pallas kernels  18.9 us (12%)
  local copies, waits for them, and re-layouts  8.18 us (5%)
    ppermute x21, waiting for transfers between devices, move(): return lax.ppermute(value, axes, pairs)  105 us
    ppermute x21, starting transfers between devices, move(): return lax.ppermute(value, axes, pairs)  21.1 us
    unnamed x28, local copies, waits for them, and re-layouts  8.14 us
    pallas_call x4, Pallas kernels, body(): call(functools.partial(chain_kernel, span, batches, chunk, first, split,...  7.24 us
    pallas_call x1, Pallas kernels, body(): call(functools.partial(forward_kernel, span, batches, chunk, sections), '...  3.16 us
  transfers between devices with their start and end apart: 21, of which 6 were waited for; matrix products, arithmetic and copies ran while one was open for 2% of the time, Pallas kernels for 1%

profile of v5, /device:TPU:26, one launch (start us, length us, event | category | flops | bytes accessed | tf_op | source)
XLA Modules:
  0.0 154.1 jit_solution(10201854292879700920)
XLA Ops:
  0.7 1.0 copy-done.1
  1.8 1.0 copy-done.2
  4.9 1.1 pack.1
  5.9 0.7 collective-permute-start
  6.6 0.7 collective-permute-start.1
  7.3 0.7 collective-permute-start.2
  8.0 1.1 constant_dynamic-update-slice_fusion.6
  9.2 1.1 constant_dynamic-update-slice_fusion.5
  10.3 1.1 constant_dynamic-update-slice_fusion.4
  12.2 4.1 %collective-permute-start.4 = (bf16[272,512]{1,0:T(8,128)(2,1)S(1)}, bf16[272,512]{1,0:T(8,128)(2,1)S(1)}, u32[]{:S(2)}, u32[]{:S(2)}) collective-permute-start(bf16[272,512]{1,0:T(8,128)(2,1)S(1)} %get-tuple-element.71), channel_id=1, source_target_pairs={{16,18},{17,19},{22,20},{23,21},{0,2},{1,3},{6,4},{7,5}} | collective-permute-start | bytes 835592 | tf_op jit(solution)/shard_map/ppermute | solution.py:402
  16.3 1.3 collective-permute-start.5
  17.7 1.6 %ready.1 = (bf16[7,512,512]{2,1,0:T(8,128)(2,1)S(1)}, bf16[512,512]{1,0:T(8,128)(2,1)S(1)}, f32[256,512]{1,0:T(8,128)S(1)}, bf16[512,256]{1,0:T(8,128)(2,1)S(1)}) custom-call(s32[2]{0:T(128)S(1)} %pad_add_fusion.info.refs_1_, bf16[1,2,256,512]{3,2,1,0:T(8,128)(2,1)S(1)} %copy-done, bf16[7,512,512]{2,1,0:T(8,128)(2,1)S(1)} %constant_dynamic-update-slice_fusion.weights.refs_7_), custom_call_target="tpu_custom_call" | custom-call | flops 400000000 | bytes 10485760 | tf_op jit(solution)/shard_map/ready/pallas_call | solution.py:433
  19.4 4.0 %collective-permute-done.4.refs_4_ = bf16[272,512]{1,0:T(8,128)(2,1)S(1)} collective-permute-done((bf16[272,512]{1,0:T(8,128)(2,1)S(1)}, bf16[272,512]{1,0:T(8,128)(2,1)S(1)}, u32[]{:S(2)}, u32[]{:S(2)}) %collective-permute-start.4) | collective-permute-done | bytes 278560 | tf_op jit(solution)/shard_map/ppermute | solution.py:402
  23.4 4.6 %collective-permute-done.5.refs_5_ = bf16[272,512]{1,0:T(8,128)(2,1)S(1)} collective-permute-done((bf16[272,512]{1,0:T(8,128)(2,1)S(1)}, bf16[272,512]{1,0:T(8,128)(2,1)S(1)}, u32[]{:S(2)}, u32[]{:S(2)}) %collective-permute-start.5) | collective-permute-done | bytes 278560 | tf_op jit(solution)/shard_map/ppermute | solution.py:402
  28.0 3.2 %forward.1 = (bf16[1024,512]{1,0:T(8,128)(2,1)S(1)}, bf16[1024,512]{1,0:T(8,128)(2,1)S(1)}, bf16[256,512]{1,0:T(8,128)(2,1)S(1)}, bf16[1024,256]{1,0:T(8,128)(2,...) custom-call(s32[2]{0:T(128)S(1)} %pad_add_fusion.info.refs_1_, ...), custom_call_target="tpu_custom_call" | custom-call | flops 2000000000 | bytes 6291456 | tf_op jit(solution)/shard_map/forward/pallas_call | solution.py:451
  34.1 0.7 collective-permute-start.7
  35.5 1.1 chain.5
  36.7 0.7 collective-permute-start.9
  38.8 1.3 chain.6
  40.1 0.7 collective-permute-start.12
  41.6 4.3 %chain.7 = (bf16[1280,512]{1,0:T(8,128)(2,1)S(1)}, bf16[3072,512]{1,0:T(8,128)(2,1)S(1)}, bf16[256,512]{1,0:T(8,128)(2,1)}) custom-call(s32[2]{0:T(128)S(1)} %pad_add_fusion.info.refs_1_, bf16[1280,512]{1,0:T(8,128)(2,1)S(1)} %collective-permute-done.12.refs_0_, s32[2]{0:T(128)S(1)} %pad_add_fusion.info.refs_1_, ...), custom_call_target="tpu_custom_call", output_to_operand_aliasing={{0}: (4, {}), {1}: (5, {})} | custom-call | flops 3000000000 | bytes 10485760 | tf_op jit(solution)/shard_map/chain/pallas_call | solution.py:492
  45.8 2.8 %weight_grads.1 = (bf16[640,512]{1,0:T(8,128)(2,1)S(1)}, bf16[640,512]{1,0:T(8,128)(2,1)S(1)}, bf16[640,512]{1,0:T(8,128)(2,1)S(1)}, bf16[640,512]{1,0:T(8,128)(...) custom-call(s32[2]{0:T(128)S(1)} %pad_add_fusion.info.refs_1_, ...), custom_call_target="tpu_custom_call" | custom-call | flops 2000000000 | bytes 10485760 | tf_op jit(solution)/shard_map/weight_grads/pallas_call | solution.py:513
  50.1 0.7 collective-permute-start.14
  50.8 1.3 collective-permute-start.15
  52.1 1.3 collective-permute-start.16
  53.4 1.3 collective-permute-start.19
  54.7 1.3 collective-permute-start.20
  56.0 73.3 %collective-permute-done.19.refs_6_ = bf16[384,512]{1,0:T(8,128)(2,1)S(1)} collective-permute-done((bf16[384,512]{1,0:T(8,128)(2,1)S(1)}, bf16[384,512]{1,0:T(8,128)(2,1)S(1)}, u32[]{:S(2)}, u32[]{:S(2)}) %collective-permute-start.19) | collective-permute-done | bytes 393248 | tf_op jit(solution)/shard_map/ppermute | solution.py:402
  129.3 5.2 %collective-permute-done.20.refs_7_ = bf16[384,512]{1,0:T(8,128)(2,1)S(1)} collective-permute-done((bf16[384,512]{1,0:T(8,128)(2,1)S(1)}, bf16[384,512]{1,0:T(8,128)(2,1)S(1)}, u32[]{:S(2)}, u32[]{:S(2)}) %collective-permute-start.20) | collective-permute-done | bytes 393248 | tf_op jit(solution)/shard_map/ppermute | solution.py:402
  134.5 14.5 %collective-permute-done.15.refs_2_ = bf16[640,512]{1,0:T(8,128)(2,1)S(1)} collective-permute-done((bf16[640,512]{1,0:T(8,128)(2,1)S(1)}, bf16[640,512]{1,0:T(8,128)(2,1)S(1)}, u32[]{:S(2)}, u32[]{:S(2)}) %collective-permute-start.15) | collective-permute-done | bytes 655392 | tf_op jit(solution)/shard_map/ppermute | solution.py:402
  148.9 3.3 %collective-permute-done.16.refs_3_ = bf16[640,512]{1,0:T(8,128)(2,1)S(1)} collective-permute-done((bf16[640,512]{1,0:T(8,128)(2,1)S(1)}, bf16[640,512]{1,0:T(8,128)(2,1)S(1)}, u32[]{:S(2)}, u32[]{:S(2)}) %collective-permute-start.16) | collective-permute-done | bytes 655392 | tf_op jit(solution)/shard_map/ppermute | solution.py:402
  152.3 1.9 %finish.1 = (bf16[1,2,32,512]{3,2,1,0:T(8,128)(2,1)}, bf16[1,2,256,512]{3,2,1,0:T(8,128)(2,1)}, f32[1,64,512]{2,1,0:T(8,128)}, f32[1,64,512]{2,1,0:T(8,128)}, f3...) custom-call(s32[2]{0:T(128)S(1)} %pad_add_fusion.info.refs_1_, ...), custom_call_target="tpu_custom_call" | custom-call | bytes 5242880 | tf_op jit(solution)/shard_map/finish/pallas_call | solution.py:526
  (51 shorter events, 10.0 us)
Async XLA Ops:
  0.7 1.0 copy-start.1
  1.8 1.0 copy-start.2
  2.8 0.7 copy-start.3
  3.5 0.7 copy-start.4
  4.2 0.7 copy-start.5
  4.9 6.5 %copy-start.7 = (bf16[1,512,512]{2,1,0:T(8,128)(2,1)S(1)}, bf16[1,512,512]{2,1,0:T(8,128)(2,1)}, u32[]{:S(2)}) copy-start(bf16[1,512,512]{2,1,0:T(8,128)(2,1)} %param.24) | copy-start | bytes 1572868
  4.9 6.5 %copy-start.8 = (bf16[1,512,512]{2,1,0:T(8,128)(2,1)S(1)}, bf16[1,512,512]{2,1,0:T(8,128)(2,1)}, u32[]{:S(2)}) copy-start(bf16[1,512,512]{2,1,0:T(8,128)(2,1)} %param.25) | copy-start | bytes 1572868
  4.9 12.8 %copy-start.9 = (bf16[1,512,512]{2,1,0:T(8,128)(2,1)S(1)}, bf16[1,512,512]{2,1,0:T(8,128)(2,1)}, u32[]{:S(2)}) copy-start(bf16[1,512,512]{2,1,0:T(8,128)(2,1)} %param.26) | copy-start | bytes 1572868
  4.9 12.8 %copy-start.10 = (bf16[1,512,512]{2,1,0:T(8,128)(2,1)S(1)}, bf16[1,512,512]{2,1,0:T(8,128)(2,1)}, u32[]{:S(2)}) copy-start(bf16[1,512,512]{2,1,0:T(8,128)(2,1)} %param.27) | copy-start | bytes 1572868
  5.9 5.5 %collective-permute-start = (bf16[528,512]{1,0:T(8,128)(2,1)S(1)}, bf16[528,512]{1,0:T(8,128)(2,1)S(1)}, u32[]{:S(2)}, u32[]{:S(2)}) collective-permute-start(bf16[528,512]{1,0:T(8,128)(2,1)S(1)} %get-tuple-element.63), channel_id=1, source_target_pairs={{27,26},{24,27},{29,28},{30,29},{11,10},{8,11},{13,12},{14,13}} | collective-permute-start | bytes 1622024 | tf_op jit(solution)/shard_map/ppermute | solution.py:402
  6.6 12.8 %collective-permute-start.1 = (bf16[528,512]{1,0:T(8,128)(2,1)S(1)}, bf16[528,512]{1,0:T(8,128)(2,1)S(1)}, u32[]{:S(2)}, u32[]{:S(2)}) collective-permute-start(bf16[528,512]{1,0:T(8,128)(2,1)S(1)} %get-tuple-element.68), channel_id=1, source_target_pairs={{24,26},{25,27},{30,28},{31,29},{8,10},{9,11},{14,12},{15,13}} | collective-permute-start | bytes 1622024 | tf_op jit(solution)/shard_map/ppermute | solution.py:402
  7.3 12.1 %collective-permute-start.2 = (bf16[528,512]{1,0:T(8,128)(2,1)S(1)}, bf16[528,512]{1,0:T(8,128)(2,1)S(1)}, u32[]{:S(2)}, u32[]{:S(2)}) collective-permute-start(bf16[528,512]{1,0:T(8,128)(2,1)S(1)} %get-tuple-element.69), channel_id=1, source_target_pairs={{25,26},{26,27},{31,28},{28,29},{9,10},{10,11},{15,12},{12,13}} | collective-permute-start | bytes 1622024 | tf_op jit(solution)/shard_map/ppermute | solution.py:402
  8.0 9.7 %copy-start = (bf16[1,2,256,512]{3,2,1,0:T(8,128)(2,1)S(1)}, bf16[1,2,256,512]{3,2,1,0:T(8,128)(2,1)}, u32[]{:S(2)}) copy-start(bf16[1,2,256,512]{3,2,1,0:T(8,128)(2,1)} %nodes.1) | copy-start | bytes 1572868
  11.5 7.9 %collective-permute-start.3 = (bf16[272,512]{1,0:T(8,128)(2,1)S(1)}, bf16[272,512]{1,0:T(8,128)(2,1)S(1)}, u32[]{:S(2)}, u32[]{:S(2)}) collective-permute-start(bf16[272,512]{1,0:T(8,128)(2,1)S(1)} %get-tuple-element.70), channel_id=1, source_target_pairs={{19,18},{16,19},{21,20},{22,21},{3,2},{0,3},{5,4},{6,5}} | collective-permute-start | bytes 835592 | tf_op jit(solution)/shard_map/ppermute | solution.py:402
  12.2 11.2 %collective-permute-start.4 = (bf16[272,512]{1,0:T(8,128)(2,1)S(1)}, bf16[272,512]{1,0:T(8,128)(2,1)S(1)}, u32[]{:S(2)}, u32[]{:S(2)}) collective-permute-start(bf16[272,512]{1,0:T(8,128)(2,1)S(1)} %get-tuple-element.71), channel_id=1, source_target_pairs={{16,18},{17,19},{22,20},{23,21},{0,2},{1,3},{6,4},{7,5}} | collective-permute-start | bytes 835592 | tf_op jit(solution)/shard_map/ppermute | solution.py:402
  16.3 11.7 %collective-permute-start.5 = (bf16[272,512]{1,0:T(8,128)(2,1)S(1)}, bf16[272,512]{1,0:T(8,128)(2,1)S(1)}, u32[]{:S(2)}, u32[]{:S(2)}) collective-permute-start(bf16[272,512]{1,0:T(8,128)(2,1)S(1)} %get-tuple-element.72), channel_id=1, source_target_pairs={{17,18},{18,19},{23,20},{20,21},{1,2},{2,3},{7,4},{4,5}} | collective-permute-start | bytes 835592 | tf_op jit(solution)/shard_map/ppermute | solution.py:402
  31.2 1.3 collective-permute-start.6
  32.5 1.0 copy-start.6
  34.1 1.5 collective-permute-start.7
  34.8 0.7 collective-permute-start.8
  36.7 2.1 %collective-permute-start.9 = (bf16[1024,512]{1,0:T(8,128)(2,1)S(1)}, bf16[1024,512]{1,0:T(8,128)(2,1)S(1)}, u32[]{:S(2)}, u32[]{:S(2)}) collective-permute-start(bf16[1024,512]{1,0:T(8,128)(2,1)S(1)} %get-tuple-element.96), channel_id=1, source_target_pairs={{18,10},{19,11},{20,12},{21,13}} | collective-permute-start | bytes 3145736 | tf_op jit(solution)/shard_map/ppermute | solution.py:402
  37.4 0.7 collective-permute-start.10
  38.1 0.7 collective-permute-start.11
  40.1 1.5 collective-permute-start.12
  40.9 0.7 collective-permute-start.13
  48.7 4.7 %collective-permute-start.17 = (bf16[384,512]{1,0:T(8,128)(2,1)S(1)}, bf16[384,512]{1,0:T(8,128)(2,1)S(1)}, u32[]{:S(2)}, u32[]{:S(2)}) collective-permute-start(bf16[384,512]{1,0:T(8,128)(2,1)S(1)} %get-tuple-element.109), channel_id=1, source_target_pairs={{2,4},{3,5},{4,0},{5,1},{10,12},{11,13},{12,8},{13,9},{18,20},{19,... | collective-permute-start | bytes 1179656 | tf_op jit(solution)/shard_map/ppermute | solution.py:402
  49.4 5.3 %collective-permute-start.18 = (bf16[384,512]{1,0:T(8,128)(2,1)S(1)}, bf16[384,512]{1,0:T(8,128)(2,1)S(1)}, u32[]{:S(2)}, u32[]{:S(2)}) collective-permute-start(bf16[384,512]{1,0:T(8,128)(2,1)S(1)} %get-tuple-element.110), channel_id=1, source_target_pairs={{2,5},{3,6},{4,1},{5,2},{10,13},{11,14},{12,9},{13,10},{18,21},{19... | collective-permute-start | bytes 1179656 | tf_op jit(solution)/shard_map/ppermute | solution.py:402
  50.1 84.4 %collective-permute-start.14 = (bf16[640,512]{1,0:T(8,128)(2,1)S(1)}, bf16[640,512]{1,0:T(8,128)(2,1)S(1)}, u32[]{:S(2)}, u32[]{:S(2)}) collective-permute-start(bf16[640,512]{1,0:T(8,128)(2,1)S(1)} %get-tuple-element.106), channel_id=1, source_target_pairs={{2,3},{3,0},{4,5},{5,6},{10,11},{11,8},{12,13},{13,14},{18,19},{19... | collective-permute-start | bytes 1966088 | tf_op jit(solution)/shard_map/ppermute | solution.py:402
  50.8 98.1 %collective-permute-start.15 = (bf16[640,512]{1,0:T(8,128)(2,1)S(1)}, bf16[640,512]{1,0:T(8,128)(2,1)S(1)}, u32[]{:S(2)}, u32[]{:S(2)}) collective-permute-start(bf16[640,512]{1,0:T(8,128)(2,1)S(1)} %get-tuple-element.107), channel_id=1, source_target_pairs={{2,0},{3,1},{4,6},{5,7},{10,8},{11,9},{12,14},{13,15},{18,16},{19,... | collective-permute-start | bytes 1966088 | tf_op jit(solution)/shard_map/ppermute | solution.py:402
  52.1 100.2 %collective-permute-start.16 = (bf16[640,512]{1,0:T(8,128)(2,1)S(1)}, bf16[640,512]{1,0:T(8,128)(2,1)S(1)}, u32[]{:S(2)}, u32[]{:S(2)}) collective-permute-start(bf16[640,512]{1,0:T(8,128)(2,1)S(1)} %get-tuple-element.108), channel_id=1, source_target_pairs={{2,1},{3,2},{4,7},{5,4},{10,9},{11,10},{12,15},{13,12},{18,17},{19... | collective-permute-start | bytes 1966088 | tf_op jit(solution)/shard_map/ppermute | solution.py:402
  53.4 75.9 %collective-permute-start.19 = (bf16[384,512]{1,0:T(8,128)(2,1)S(1)}, bf16[384,512]{1,0:T(8,128)(2,1)S(1)}, u32[]{:S(2)}, u32[]{:S(2)}) collective-permute-start(bf16[384,512]{1,0:T(8,128)(2,1)S(1)} %get-tuple-element.111), channel_id=1, source_target_pairs={{2,6},{3,7},{4,2},{5,3},{10,14},{11,15},{12,10},{13,11},{18,22},{1... | collective-permute-start | bytes 1179656 | tf_op jit(solution)/shard_map/ppermute | solution.py:402
  54.7 79.8 %collective-permute-start.20 = (bf16[384,512]{1,0:T(8,128)(2,1)S(1)}, bf16[384,512]{1,0:T(8,128)(2,1)S(1)}, u32[]{:S(2)}, u32[]{:S(2)}) collective-permute-start(bf16[384,512]{1,0:T(8,128)(2,1)S(1)} %get-tuple-element.112), channel_id=1, source_target_pairs={{2,7},{3,4},{4,3},{5,0},{10,15},{11,12},{12,11},{13,8},{18,23},{19... | collective-permute-start | bytes 1179656 | tf_op jit(solution)/shard_map/ppermute | solution.py:402

commit v6 on v5

--- a/solution.py
+++ b/solution.py
@@ -73,51 +73,43 @@
     return (sigma * (1.0 + pre * (1.0 - sigma))).astype(BF)
 
 
-def pack_kernel(span, batches, info, senders, receivers, tiles, edges, tops, *refs):
-    outs, seconds = refs[:span], refs[span : 2 * span - 1]
-    send_in, recv_in, sems = refs[2 * span - 1 :]
+def pack_kernel(span, batches, sections, info, senders, receivers, tiles, edges, tops, *refs):
+    own, own_top = refs[:2]
+    outs, seconds = refs[2 : span + 1], refs[span + 1 :]
     member = info[1]
     half = lax.div(member, span)
     offset = lax.rem(member, span)
     count = senders.shape[1]
     tile_count = tiles.shape[1]
     tile_len = count // tile_count
-    gets = [
-        pltpu.make_async_copy(senders, send_in, sems.at[0]),
-        pltpu.make_async_copy(receivers, recv_in, sems.at[1]),
-    ]
-    picks, loads, puts = [], [], []
+    top = info[0] == sections - 1
     for step in range(span):
         batch = lax.rem(offset - step + span, span) - base_of(half, span, batches)
-        picks.append(jnp.clip(batch, 0, batches - 1))
-        latents = outs[step].at[pl.ds(0, count)]
-        grads = outs[step].at[pl.ds(count + PAD, count)]
-        loads.append(pltpu.make_async_copy(edges.at[0, picks[step]], latents, sems.at[2 + step]))
-        puts.append(pltpu.make_async_copy(tops.at[picks[step]], grads, sems.at[2 + span + step]))
-    for copy in gets + loads + puts:
-        copy.start()
-    for copy in gets:
-        copy.wait()
-    for step in range(span):
-        batch = picks[step]
-        out = outs[step]
-        out[count : count + PAD] = jnp.zeros((PAD, out.shape[1]), BF)
+        batch = jnp.clip(batch, 0, batches - 1)
+        out = outs[step - 1] if step else own
+        out[:count] = edges[0, batch]
+        out[count:] = jnp.zeros((PAD, out.shape[1]), BF)
         for tile in range(tile_count):
             lanes = slice(tile * tile_len, (tile + 1) * tile_len)
-            send = pick_row(send_in, batch, lanes) + tiles[batch, tile, 0] * BLOCK
-            recv = pick_row(recv_in, batch, lanes) + tiles[batch, tile, 1] * BLOCK
+            send = pick_row(senders, batch, lanes) + tiles[batch, tile, 0] * BLOCK
+            recv = pick_row(receivers, batch, lanes) + tiles[batch, tile, 1] * BLOCK
             which = lax.broadcasted_iota(jnp.int32, (PAD, tile_len), 0)
             block = jnp.where(which == 0, send, jnp.where(which == 1, recv, 0))
-            out[count : count + PAD, lanes] = block.astype(F32).astype(BF)
-        loads[step].wait()
+            out[count:, lanes] = block.astype(F32).astype(BF)
         if step:
-            copy = pltpu.make_async_copy(
-                out.at[pl.ds(0, count + PAD)], seconds[step - 1], sems.at[1 + 2 * span + step]
-            )
-            copy.start()
-            puts.append(copy)
-    for copy in puts:
-        copy.wait()
+            second = seconds[step - 1]
+            second[count:] = out[count:]
+
+            @pl.when(top)
+            def _(second=second, batch=batch):
+                second[:count] = tops[batch]
+
+            @pl.when(jnp.logical_not(top))
+            def _(second=second, out=out):
+                second[:count] = out[:count]
+
+        else:
+            own_top[...] = tops[batch]
 
 
 def ready_kernel(span, batches, info, nodes, weights, turned, hidden, node_pre, feats_turned):
@@ -132,28 +124,27 @@
         turned[slot] = weights[slot].T
 
 
-def forward_kernel(span, batches, chunk, sections, info, own, *refs):
-    groups = (refs[: span - 1], refs[span - 1 : 2 * span - 2])
-    hidden, weights = refs[2 * span - 2 : 2 * span]
-    act_out, slope_out, part_out, hot_out, hots_out, pieces, tops, both, index = refs[2 * span :]
-    count = (own.shape[0] - PAD) // 2
+def takes_part(info, sections, group):
+    return lax.rem(sections - 1 - info[0], 2) == group
+
+
+def forward_kernel(span, chunk, sections, group, info, *refs):
+    @pl.when(takes_part(info, sections, group))
+    def _():
+        forward_step(span, chunk, *refs)
+
+
+def forward_step(span, chunk, own, *refs):
+    others = refs[: span - 1]
+    hidden, weights = refs[span - 1 : span + 1]
+    act_out, slope_out, part_out, hot_out, hots_out, pieces, both = refs[span + 1 :]
+    count = own.shape[0] - PAD
     node_count = part_out.shape[0]
-    for which, others in enumerate(groups):
-
-        @pl.when(lax.rem(sections - 1 - info[0], 2) == which)
-        def _(others=others, which=which):
-            for step in range(1, span):
-                pieces[step * count : (step + 1) * count] = others[step - 1][:count]
-                index[step] = others[step - 1][count : count + PAD, :count]
-                if which == 0:
-                    tops[step * count : (step + 1) * count] = others[step - 1][count + PAD :]
-
-    pieces[:count] = own[:count]
-    tops[:count] = own[count + PAD :]
-    index[0] = own[count : count + PAD, :count]
     for step in range(span):
+        piece = others[step - 1] if step else own
         run = slice(step * count, (step + 1) * count)
-        index_rows = index[step]
+        pieces[run] = piece[:count]
+        index_rows = piece[count:, :count]
         hots_out[:node_count, run] = hot_rows(index_rows, 0, node_count)
         hots_out[node_count:, run] = hot_rows(index_rows, 1, node_count)
         both[run, :node_count] = hot_columns(index_rows, 0, node_count)
@@ -170,58 +161,67 @@
     part_out[...] = matmul(total.astype(BF), weights[MSG]).astype(BF)
 
 
-def turn_kernel(pieces, act, edges_turned, act_turned):
-    rows = 2 * BLOCK
-    for at in range(0, act.shape[0], rows):
-        run = slice(at, at + rows)
-        edges_turned[:, run] = pieces[run].T
-        act_turned[:, run] = act[run].T
-
-
-def node_kernel(node_pre, part_own, part_other, weights, turned_first, out):
-    count = part_own.shape[0]
-    agg = (part_own[...].astype(F32) + part_other[...].astype(F32)).astype(BF)
-    pre = node_pre[...] + matmul(agg, weights[AGG])
-    sigma = jax.nn.sigmoid(pre)
-    out[:count] = agg
-    out[count : 2 * count] = (pre * sigma).astype(BF)
-    out[2 * count :] = slope_of(pre, sigma)
-
-
-def chain_kernel(span, batches, chunk, first, split, active, info, *refs):
-    incoming = refs[:2] if first else refs[:3]
-    refs = refs[len(incoming) :]
+def turn_kernel(sections, group, info, pieces, act, edges_turned, act_turned):
+    @pl.when(takes_part(info, sections, group))
+    def _():
+        rows = 2 * BLOCK
+        for at in range(0, act.shape[0], rows):
+            run = slice(at, at + rows)
+            edges_turned[:, run] = pieces[run].T
+            act_turned[:, run] = act[run].T
+
+
+def node_kernel(sections, group, info, node_pre, part_own, part_other, weights, turned_first, out):
+    @pl.when(takes_part(info, sections, group))
+    def _():
+        count = part_own.shape[0]
+        agg = (part_own[...].astype(F32) + part_other[...].astype(F32)).astype(BF)
+        pre = node_pre[...] + matmul(agg, weights[AGG])
+        sigma = jax.nn.sigmoid(pre)
+        out[:count] = agg
+        out[count : 2 * count] = (pre * sigma).astype(BF)
+        out[2 * count :] = slope_of(pre, sigma)
+
+
+def chain_kernel(span, batches, chunk, first, active, info, *refs):
+    several = span + 1 if first else 2
+    incoming, refs = refs[:several], refs[several:]
     kept = ()
     if not first:
         kept, refs = refs[:2], refs[2:]
-    common, refs = refs[:5], refs[5:]
 
     @pl.when(info[0] == active)
     def _():
-        chain_step(span, batches, chunk, first, split, info, incoming, *common, *refs)
+        chain_step(span, batches, chunk, first, info, incoming, *refs)
 
     if kept:
 
         @pl.when(info[0] != active)
         def _():
-            refs[0][...] = kept[0][...]
-            refs[1][...] = kept[1][...]
+            refs[5][...] = kept[0][...]
+            refs[6][...] = kept[1][...]
 
 
 def chain_step(
-    span, batches, chunk, first, split, info, incoming, hot, hots, slope, node_pack, turned, pay, keep, part_out, *rest
+    span, batches, chunk, first, info, incoming, hot, hots, slope, node_pack, turned, pay, keep, part_out, *rest
 ):
     member = info[1]
     batch = own_batch(member, span, batches)
     half = lax.div(member, span)
     total = slope.shape[0]
     if first:
-        top_nodes, came = incoming
+        top_nodes, pieces = incoming[0], incoming[1:]
+        came = rest[-1]
+        count = total // span
+        for step, piece in enumerate(pieces):
+            came[step * count : (step + 1) * count] = piece[:count]
         grad = top_nodes[batch]
     else:
-        came, part_own, cross = incoming
-        mine = part_own[...] if part_own.shape[0] == cross.shape[0] else came[total:]
-        grad = (mine.astype(F32) + cross[...].astype(F32)).astype(BF)
+        came, other = incoming
+        if came.shape[0] == total:
+            grad = other[...]
+        else:
+            grad = (came[total:].astype(F32) + other[...].astype(F32)).astype(BF)
     node_count = part_out.shape[0]
     node_at = 2 * total
     delta = (matmul(grad, turned[OUT]) * node_pack[2 * node_count :].astype(F32)).astype(BF)
@@ -237,7 +237,7 @@
         keep[total + at : total + at + chunk] = edge_delta
         below = (before + matmul(edge_delta, turned[EDGE])).astype(BF)
         pay[run] = below
-        if split:
+        if rest and not first:
             rest[0][run] = below
     sums = matmul(hots[...], keep[total : 2 * total]).astype(BF)
     keep[node_at + 2 * node_count :] = sums
@@ -249,7 +249,15 @@
     part_out[...] = part
 
 
-def grads_kernel(span, batches, groups, info, edges_turned, act_turned, feats_turned, node_pack, keep, pay, *refs):
+def grads_kernel(span, batches, groups, sections, info, *refs):
+    for group in range(2):
+
+        @pl.when(takes_part(info, sections, group))
+        def _(group=group):
+            grads_step(span, batches, groups, info, *refs[3 * group : 3 * group + 3], *refs[6:])
+
+
+def grads_step(span, batches, groups, info, edges_turned, act_turned, node_pack, feats_turned, keep, pay, *refs):
     near, far = refs[:span], refs[span : 2 * span]
     sums = refs[2 * span]
     member = info[1]
@@ -345,14 +353,14 @@
         nodes_out[0, batch] = rows.astype(BF)
 
 
-def call(kernel, name, in_specs, out_shapes, scratch, flops, touched, aliases={}, grant=GRANT, passed=0):
+def call(kernel, name, in_specs, out_shapes, scratch, flops, touched, aliases={}, grant=GRANT):
     many = isinstance(out_shapes, list)
     return pl.pallas_call(
         kernel,
         name=name,
         out_shape=out_shapes,
         in_specs=in_specs,
-        out_specs=[VMEM] * (len(out_shapes) - passed) + [ANY] * passed if many else VMEM,
+        out_specs=[VMEM] * len(out_shapes) if many else VMEM,
         scratch_shapes=scratch,
         input_output_aliases=aliases,
         compiler_params=pltpu.CompilerParams(vmem_limit_bytes=grant * 2**20),
@@ -410,20 +418,15 @@
         return jax.ShapeDtypeStruct((rows, cols), kind)
 
     packed = call(
-        functools.partial(pack_kernel, span, batches),
+        functools.partial(pack_kernel, span, batches, sections),
         "pack",
-        [SMEM, ANY, ANY, SMEM, ANY, ANY],
-        [like(2 * count + PAD)] * span + [like(count + PAD)] * (span - 1),
-        [
-            pltpu.VMEM((batches, count), jnp.int32),
-            pltpu.VMEM((batches, count), jnp.int32),
-            pltpu.SemaphoreType.DMA((2 + 3 * span,)),
-        ],
+        [SMEM, VMEM, VMEM, SMEM, VMEM, VMEM],
+        [like(count + PAD), like(count)] + [like(count + PAD)] * (2 * span - 2),
+        [],
         0,
         2**20,
-        passed=span - 1,
     )(info, senders, receivers, tile_blocks, layer_edges, top_edges)
-    own, first_out, second_out = packed[0], packed[1:span], packed[span:]
+    own, own_top, first_out, second_out = packed[0], packed[1], packed[2 : span + 1], packed[span + 1 :]
     groups_of = [list(range(sections - 1 - group, -1, -2)) for group in range(2)]
     first_in = [move(piece, groups_of[0], collect[step + 1]) for step, piece in enumerate(first_out)]
     own, w_send, w_recv, w_edge, w_msg, w_node, w_agg, w_out = lax.optimization_barrier(
@@ -446,39 +449,42 @@
     )(info, layer_nodes, weights)
     turned, hidden, node_pre, feats_turned = ready
     first_in[0], second_out = lax.optimization_barrier((first_in[0], second_out))
-    second_in = [move(piece, groups_of[1], collect[step + 1]) for step, piece in enumerate(second_out)]
-
-    act, slope, part, hot, hots, pieces, tops = call(
-        functools.partial(forward_kernel, span, batches, chunk, sections),
-        "forward",
-        [SMEM] + [VMEM] * (2 * span + 1),
-        [like(total), like(total), like(node_count), like(total, node_count), like(2 * node_count, total)]
-        + [like(total)] * 2,
-        [pltpu.VMEM((total, 2 * node_count), BF), pltpu.VMEM((span, PAD, count), BF)],
-        2 * 10**9,
-        6 * 2**20,
-    )(info, own, *first_in, *second_in, hidden, weights)
+    second_in = [move(piece, groups_of[1] + last, collect[step + 1]) for step, piece in enumerate(second_out)]
 
     swap = [(worker(m, h), worker(m, 1 - h)) for m, h in works]
-    part_other = move(part, every, swap)
-    edges_turned, act_turned = call(
-        turn_kernel,
-        "turn",
-        [VMEM] * 2,
-        [like(width, total), like(width, total)],
-        [],
-        0,
-        4 * 2**20,
-    )(pieces, act)
-    node_pack = call(
-        node_kernel,
-        "node_forward",
-        [VMEM] * 4 + [ANY],
-        like(3 * node_count),
-        [],
-        10**5,
-        2**10,
-    )(node_pre, part, part_other, weights, edges_turned)
+    stages, after = [], []
+    for group, arrived in enumerate((first_in, second_in)):
+        act, slope, part, hot, hots, pieces = call(
+            functools.partial(forward_kernel, span, chunk, sections, group),
+            "forward",
+            [SMEM] + [VMEM] * (span + 2),
+            [like(total), like(total), like(node_count), like(total, node_count), like(2 * node_count, total)]
+            + [like(total)],
+            [pltpu.VMEM((total, 2 * node_count), BF)],
+            2 * 10**9,
+            6 * 2**20,
+        )(info, own, *arrived, hidden, weights)
+        part_other = move(part, groups_of[group], swap)
+        edges_turned, act_turned = call(
+            functools.partial(turn_kernel, sections, group),
+            "turn",
+            [SMEM] + [VMEM] * 2,
+            [like(width, total), like(width, total)],
+            [],
+            0,
+            4 * 2**20,
+        )(info, pieces, act)
+        node_pack = call(
+            functools.partial(node_kernel, sections, group),
+            "node_forward",
+            [SMEM] + [VMEM] * 4 + [ANY],
+            like(3 * node_count),
+            [],
+            10**5,
+            2**10,
+        )(info, node_pre, part, part_other, weights, edges_turned)
+        stages.append((hot, hots, slope, node_pack))
+        after += [edges_turned, act_turned, node_pack]
 
     both_ways = [(worker(m, h), worker(m, h)) for m, h in works]
     rows = 5 * share + share // 2 + node_share
@@ -488,37 +494,36 @@
         first = moment == 0
         layer = sections - 1 - moment
         split = layer > 0 and layer % 2 == 0
-        inputs = (top_nodes, tops) if first else (*incoming, pay, keep)
+        inputs = (top_nodes, own_top, *second_in) if first else (*incoming, pay, keep)
         made = call(
-            functools.partial(chain_kernel, span, batches, chunk, first, split, layer),
+            functools.partial(chain_kernel, span, batches, chunk, first, layer),
             "chain",
             [SMEM] + [VMEM] * (len(inputs) + 5),
-            [like(total + node_count), like(2 * total + 4 * node_count), like(node_count)]
-            + [like(total)] * split,
-            [],
+            [like(total + node_count), like(2 * total + 4 * node_count), like(node_count)] + [like(total)] * split,
+            [pltpu.VMEM((total, width), BF)] if first else [],
             3 * 10**9,
             10 * 2**20,
-            {} if first else {4: 0, 5: 1},
-        )(info, *inputs, hot, hots, slope, node_pack, turned)
+            {} if first else {3: 0, 4: 1},
+        )(info, *inputs, *stages[moment % 2], turned)
         pay, keep, part = made[:3]
         if split:
-            mine = move(part, [layer], both_ways, -1)
             came = move(made[3], [layer], both_ways, -1)
-            incoming = (came, mine, move(mine, [layer - 1], swap))
+            summed = part.astype(F32) + move(part, [layer], swap).astype(F32)
+            incoming = (came, move(summed.astype(BF), [layer], both_ways, -1))
         elif layer > 0:
             cross = move(part, [layer], swap, -1)
             came = move(pay, [layer], both_ways, -1)
-            incoming = (came, info, cross)
+            incoming = (came, cross)
 
     out = call(
-        functools.partial(grads_kernel, span, batches, groups),
+        functools.partial(grads_kernel, span, batches, groups, sections),
         "weight_grads",
-        [SMEM] + [VMEM] * 6,
+        [SMEM] + [VMEM] * 9,
         [like(count + rows)] * span + [like(rows)] * span,
         [pltpu.VMEM((6, width, width), BF)],
         2 * 10**9,
         10 * 2**20,
-    )(info, edges_turned, act_turned, feats_turned, node_pack, keep, pay)
+    )(info, *after, feats_turned, keep, pay)
     across = [[(worker(m, h), (1 - h) * span + (m + step) % span) for m, h in works] for step in range(span)]
     far = [move(block, every, across[step]) for step, block in enumerate(out[span:])]
     near = [out[0]] + [move(out[step], every, deliver[step]) for step in range(1, span)]

time: 155 us -> 141 us (0.910)
  waiting for transfers between devices: 105 us -> 88.9 us
  Pallas kernels: 18.9 us -> 21.3 us
    ppermute x21 -> x22, waiting for transfers between devices: 105 us -> 88.9 us  [move(): return lax.ppermute(value, axes, pairs)]
    pallas_call x9 -> x12, Pallas kernels: 15.3 us -> 17.8 us  [the longest x4 7.24 us: body(): call(functools.partial(chain_kernel, span, batches, chunk, first, layer),...]
    ppermute x21 -> x22, starting transfers between devices: 21.1 us -> 21.7 us  [move(): return lax.ppermute(value, axes, pairs)]
  transfers between devices with their start and end apart: 21 -> 22, of which waited for: 6 -> 6; matrix products, arithmetic and copies ran while one was open for 2% -> 2% of each run, Pallas kernels for 1% -> 6%
where the time goes in v6:
time: 141 us
  waiting for transfers between devices  88.9 us (63%)
  starting transfers between devices  21.7 us (15%)
  Pallas kernels  21.3 us (15%)
  local copies, waits for them, and re-layouts  7.59 us (5%)
    ppermute x22, waiting for transfers between devices, move(): return lax.ppermute(value, axes, pairs)  88.9 us
    ppermute x22, starting transfers between devices, move(): return lax.ppermute(value, axes, pairs)  21.7 us
    unnamed x28, local copies, waits for them, and re-layouts  7.55 us
    pallas_call x4, Pallas kernels, body(): call(functools.partial(chain_kernel, span, batches, chunk, first, layer),...  7.24 us
    pallas_call x2, Pallas kernels, body(): call(functools.partial(forward_kernel, span, chunk, sections, group), 'fo...  3.67 us
    pallas_call x1, Pallas kernels, body(): call(functools.partial(grads_kernel, span, batches, groups, sections), 'w...  2.84 us
  transfers between devices with their start and end apart: 22, of which 6 were waited for; matrix products, arithmetic and copies ran while one was open for 2% of the time, Pallas kernels for 6%

profile of v6, /device:TPU:26, one launch (start us, length us, event | category | flops | bytes accessed | tf_op | source)
XLA Modules:
  0.0 140.7 jit_solution(17953830989833084383)
XLA Ops:
  0.7 1.0 copy-done.1
  1.8 1.0 copy-done.2
  4.9 0.8 pack.1
  7.7 1.1 constant_dynamic-update-slice_fusion.6
  8.8 1.1 constant_dynamic-update-slice_fusion.5
  9.9 1.1 constant_dynamic-update-slice_fusion.4
  11.2 1.6 %ready.1 = (bf16[7,512,512]{2,1,0:T(8,128)(2,1)S(1)}, bf16[512,512]{1,0:T(8,128)(2,1)S(1)}, f32[256,512]{1,0:T(8,128)S(1)}, bf16[512,256]{1,0:T(8,128)(2,1)S(1)}) custom-call(s32[2]{0:T(128)S(1)} %pad_add_fusion.info, bf16[1,2,256,512]{3,2,1,0:T(8,128)(2,1)S(1)} %copy-done, bf16[7,512,512]{2,1,0:T(8,128)(2,1)S(1)} %constant_dynamic-update-slice_fusion.weights.refs_5_), custom_call_target="tpu_custom_call" | custom-call | flops 400000000 | bytes 10485760 | tf_op jit(solution)/shard_map/ready/pallas_call | solution.py:436
  13.6 4.1 %collective-permute-start.5 = (bf16[272,512]{1,0:T(8,128)(2,1)S(1)}, bf16[272,512]{1,0:T(8,128)(2,1)S(1)}, u32[]{:S(2)}, u32[]{:S(2)}) collective-permute-start(bf16[272,512]{1,0:T(8,128)(2,1)S(1)} %get-tuple-element.93), channel_id=1, source_target_pairs={{16,18},{17,19},{22,20},{23,21},{0,2},{1,3},{6,4},{7,5},{24,26},{2... | collective-permute-start | bytes 835592 | tf_op jit(solution)/shard_map/ppermute | solution.py:410
  17.7 1.3 collective-permute-start.6
  21.8 3.0 %collective-permute-done.6.refs_3_.refs_4_ = bf16[272,512]{1,0:T(8,128)(2,1)S(1)} collective-permute-done((bf16[272,512]{1,0:T(8,128)(2,1)S(1)}, bf16[272,512]{1,0:T(8,128)(2,1)S(1)}, u32[]{:S(2)}, u32[]{:S(2)}) %collective-permute-start.6) | collective-permute-done | bytes 278560 | tf_op jit(solution)/shard_map/ppermute | solution.py:410
  25.3 0.7 collective-permute-start.8
  26.0 3.1 %forward.3 = (bf16[1024,512]{1,0:T(8,128)(2,1)S(1)}, bf16[1024,512]{1,0:T(8,128)(2,1)S(1)}, bf16[256,512]{1,0:T(8,128)(2,1)S(1)}, bf16[1024,256]{1,0:T(8,128)(2,...) custom-call(s32[2]{0:T(128)S(1)} %pad_add_fusion.info, ...), custom_call_target="tpu_custom_call" | custom-call | flops 2000000000 | bytes 6291456 | tf_op jit(solution)/shard_map/forward/pallas_call | solution.py:457
  30.5 1.2 turn.3
  31.7 1.0 node_forward.3.refs_7_.refs_5_
  32.7 1.3 chain.5
  34.0 0.7 collective-permute-start.10
  36.3 1.1 chain.6
  37.4 0.7 collective-permute-start.13
  38.8 4.3 %chain.7 = (bf16[1280,512]{1,0:T(8,128)(2,1)S(1)}, bf16[3072,512]{1,0:T(8,128)(2,1)S(1)}, bf16[256,512]{1,0:T(8,128)(2,1)}) custom-call(s32[2]{0:T(128)S(1)} %pad_add_fusion.info, bf16[1280,512]{1,0:T(8,128)(2,1)S(1)} %collective-permute-done.13.refs_0_, ...), custom_call_target="tpu_custom_call", output_to_operand_aliasing={{0}: (3, {}), {1}: (4, {})} | custom-call | flops 3000000000 | bytes 10485760 | tf_op jit(solution)/shard_map/chain/pallas_call | solution.py:498
  43.1 2.8 %weight_grads.1 = (bf16[640,512]{1,0:T(8,128)(2,1)S(1)}, bf16[640,512]{1,0:T(8,128)(2,1)S(1)}, bf16[640,512]{1,0:T(8,128)(2,1)S(1)}, bf16[640,512]{1,0:T(8,128)(...) custom-call(s32[2]{0:T(128)S(1)} %pad_add_fusion.info, ...), custom_call_target="tpu_custom_call" | custom-call | flops 2000000000 | bytes 10485760 | tf_op jit(solution)/shard_map/weight_grads/pallas_call | solution.py:518
  46.0 0.7 collective-permute-start.18
  46.7 0.7 collective-permute-start.19
  47.4 0.7 collective-permute-start.15
  48.1 1.3 collective-permute-start.16
  49.4 1.3 collective-permute-start.17
  50.7 1.3 collective-permute-start.20
  52.0 1.3 collective-permute-start.21
  53.3 63.1 %collective-permute-done.20.refs_6_ = bf16[384,512]{1,0:T(8,128)(2,1)S(1)} collective-permute-done((bf16[384,512]{1,0:T(8,128)(2,1)S(1)}, bf16[384,512]{1,0:T(8,128)(2,1)S(1)}, u32[]{:S(2)}, u32[]{:S(2)}) %collective-permute-start.20) | collective-permute-done | bytes 393248 | tf_op jit(solution)/shard_map/ppermute | solution.py:410
  116.4 4.6 %collective-permute-done.21.refs_7_ = bf16[384,512]{1,0:T(8,128)(2,1)S(1)} collective-permute-done((bf16[384,512]{1,0:T(8,128)(2,1)S(1)}, bf16[384,512]{1,0:T(8,128)(2,1)S(1)}, u32[]{:S(2)}, u32[]{:S(2)}) %collective-permute-start.21) | collective-permute-done | bytes 393248 | tf_op jit(solution)/shard_map/ppermute | solution.py:410
  121.0 15.1 %collective-permute-done.16.refs_2_ = bf16[640,512]{1,0:T(8,128)(2,1)S(1)} collective-permute-done((bf16[640,512]{1,0:T(8,128)(2,1)S(1)}, bf16[640,512]{1,0:T(8,128)(2,1)S(1)}, u32[]{:S(2)}, u32[]{:S(2)}) %collective-permute-start.16) | collective-permute-done | bytes 655392 | tf_op jit(solution)/shard_map/ppermute | solution.py:410
  136.1 2.7 %collective-permute-done.17.refs_3_ = bf16[640,512]{1,0:T(8,128)(2,1)S(1)} collective-permute-done((bf16[640,512]{1,0:T(8,128)(2,1)S(1)}, bf16[640,512]{1,0:T(8,128)(2,1)S(1)}, u32[]{:S(2)}, u32[]{:S(2)}) %collective-permute-start.17) | collective-permute-done | bytes 655392 | tf_op jit(solution)/shard_map/ppermute | solution.py:410
  138.8 1.9 %finish.1 = (bf16[1,2,32,512]{3,2,1,0:T(8,128)(2,1)}, bf16[1,2,256,512]{3,2,1,0:T(8,128)(2,1)}, f32[1,64,512]{2,1,0:T(8,128)}, f32[1,64,512]{2,1,0:T(8,128)}, f3...) custom-call(s32[2]{0:T(128)S(1)} %pad_add_fusion.info, ...), custom_call_target="tpu_custom_call" | custom-call | bytes 5242880 | tf_op jit(solution)/shard_map/finish/pallas_call | solution.py:531
  (57 shorter events, 11.7 us)
Async XLA Ops:
  0.7 1.0 copy-start.1
  1.8 1.0 copy-start.2
  2.8 0.7 copy-start.3
  3.5 0.7 copy-start.4
  4.9 6.2 %copy-start.7 = (bf16[1,512,512]{2,1,0:T(8,128)(2,1)S(1)}, bf16[1,512,512]{2,1,0:T(8,128)(2,1)}, u32[]{:S(2)}) copy-start(bf16[1,512,512]{2,1,0:T(8,128)(2,1)} %param.24) | copy-start | bytes 1572868
  4.9 6.2 %copy-start.8 = (bf16[1,512,512]{2,1,0:T(8,128)(2,1)S(1)}, bf16[1,512,512]{2,1,0:T(8,128)(2,1)}, u32[]{:S(2)}) copy-start(bf16[1,512,512]{2,1,0:T(8,128)(2,1)} %param.25) | copy-start | bytes 1572868
  4.9 6.3 %copy-start.9 = (bf16[1,512,512]{2,1,0:T(8,128)(2,1)S(1)}, bf16[1,512,512]{2,1,0:T(8,128)(2,1)}, u32[]{:S(2)}) copy-start(bf16[1,512,512]{2,1,0:T(8,128)(2,1)} %param.26) | copy-start | bytes 1572868
  4.9 6.3 %copy-start.10 = (bf16[1,512,512]{2,1,0:T(8,128)(2,1)S(1)}, bf16[1,512,512]{2,1,0:T(8,128)(2,1)}, u32[]{:S(2)}) copy-start(bf16[1,512,512]{2,1,0:T(8,128)(2,1)} %param.27) | copy-start | bytes 1572868
  5.6 7.3 %collective-permute-start = (bf16[272,512]{1,0:T(8,128)(2,1)S(1)}, bf16[272,512]{1,0:T(8,128)(2,1)S(1)}, u32[]{:S(2)}, u32[]{:S(2)}) collective-permute-start(bf16[272,512]{1,0:T(8,128)(2,1)S(1)} %get-tuple-element.71), channel_id=1, source_target_pairs={{27,26},{24,27},{29,28},{30,29},{11,10},{8,11},{13,12},{14,13}} | collective-permute-start | bytes 835592 | tf_op jit(solution)/shard_map/ppermute | solution.py:410
  6.3 12.7 %collective-permute-start.1 = (bf16[272,512]{1,0:T(8,128)(2,1)S(1)}, bf16[272,512]{1,0:T(8,128)(2,1)S(1)}, u32[]{:S(2)}, u32[]{:S(2)}) collective-permute-start(bf16[272,512]{1,0:T(8,128)(2,1)S(1)} %get-tuple-element.76), channel_id=1, source_target_pairs={{24,26},{25,27},{30,28},{31,29},{8,10},{9,11},{14,12},{15,13}} | collective-permute-start | bytes 835592 | tf_op jit(solution)/shard_map/ppermute | solution.py:410
  7.0 12.0 %collective-permute-start.2 = (bf16[272,512]{1,0:T(8,128)(2,1)S(1)}, bf16[272,512]{1,0:T(8,128)(2,1)S(1)}, u32[]{:S(2)}, u32[]{:S(2)}) collective-permute-start(bf16[272,512]{1,0:T(8,128)(2,1)S(1)} %get-tuple-element.77), channel_id=1, source_target_pairs={{25,26},{26,27},{31,28},{28,29},{9,10},{10,11},{15,12},{12,13}} | collective-permute-start | bytes 835592 | tf_op jit(solution)/shard_map/ppermute | solution.py:410
  7.7 3.5 %copy-start = (bf16[1,2,256,512]{3,2,1,0:T(8,128)(2,1)S(1)}, bf16[1,2,256,512]{3,2,1,0:T(8,128)(2,1)}, u32[]{:S(2)}) copy-start(bf16[1,2,256,512]{3,2,1,0:T(8,128)(2,1)} %nodes.1) | copy-start | bytes 1572868
  12.9 8.6 %collective-permute-start.4 = (bf16[272,512]{1,0:T(8,128)(2,1)S(1)}, bf16[272,512]{1,0:T(8,128)(2,1)S(1)}, u32[]{:S(2)}, u32[]{:S(2)}) collective-permute-start(bf16[272,512]{1,0:T(8,128)(2,1)S(1)} %get-tuple-element.92), channel_id=1, source_target_pairs={{19,18},{16,19},{21,20},{22,21},{3,2},{0,3},{5,4},{6,5},{27,26},{2... | collective-permute-start | bytes 835592 | tf_op jit(solution)/shard_map/ppermute | solution.py:410
  13.6 8.2 %collective-permute-start.5 = (bf16[272,512]{1,0:T(8,128)(2,1)S(1)}, bf16[272,512]{1,0:T(8,128)(2,1)S(1)}, u32[]{:S(2)}, u32[]{:S(2)}) collective-permute-start(bf16[272,512]{1,0:T(8,128)(2,1)S(1)} %get-tuple-element.93), channel_id=1, source_target_pairs={{16,18},{17,19},{22,20},{23,21},{0,2},{1,3},{6,4},{7,5},{24,26},{2... | collective-permute-start | bytes 835592 | tf_op jit(solution)/shard_map/ppermute | solution.py:410
  17.7 7.0 %collective-permute-start.6 = (bf16[272,512]{1,0:T(8,128)(2,1)S(1)}, bf16[272,512]{1,0:T(8,128)(2,1)S(1)}, u32[]{:S(2)}, u32[]{:S(2)}) collective-permute-start(bf16[272,512]{1,0:T(8,128)(2,1)S(1)} %get-tuple-element.94), channel_id=1, source_target_pairs={{17,18},{18,19},{23,20},{20,21},{1,2},{2,3},{7,4},{4,5},{25,26},{2... | collective-permute-start | bytes 835592 | tf_op jit(solution)/shard_map/ppermute | solution.py:410
  19.6 1.3 collective-permute-start.3
  20.9 3.9 %copy-start.6 = (bf16[2,256,512]{2,1,0:T(8,128)(2,1)S(1)}, bf16[2,256,512]{2,1,0:T(8,128)(2,1)}, u32[]{:S(2)}) copy-start(bf16[2,256,512]{2,1,0:T(8,128)(2,1)} %refs_0_.1) | copy-start | bytes 1572868
  25.3 7.4 %collective-permute-start.8 = (bf16[1280,512]{1,0:T(8,128)(2,1)S(1)}, bf16[1280,512]{1,0:T(8,128)(2,1)S(1)}, u32[]{:S(2)}, u32[]{:S(2)}) collective-permute-start(bf16[1280,512]{1,0:T(8,128)(2,1)S(1)} %get-tuple-element.106.refs_2_), channel_id=1, source_target_pairs={{26,18},{27,19},{28,20},{29,21}} | collective-permute-start | bytes 3932168 | tf_op jit(solution)/shard_map/ppermute | solution.py:410
  29.2 2.6 %collective-permute-start.7 = (bf16[256,512]{1,0:T(8,128)(2,1)S(1)}, bf16[256,512]{1,0:T(8,128)(2,1)S(1)}, u32[]{:S(2)}, u32[]{:S(2)}) collective-permute-start(bf16[256,512]{1,0:T(8,128)(2,1)S(1)} %get-tuple-element.99.part_own), channel_id=1, source_target_pairs={{18,20},{19,21},{20,18},{21,19},{2,4},{3,5},{4,2},{5,3}} | collective-permute-start | bytes 786440 | tf_op jit(solution)/shard_map/ppermute | solution.py:410
  29.9 2.9 %collective-permute-start.9 = (bf16[256,512]{1,0:T(8,128)(2,1)S(1)}, bf16[256,512]{1,0:T(8,128)(2,1)S(1)}, u32[]{:S(2)}, u32[]{:S(2)}) collective-permute-start(bf16[256,512]{1,0:T(8,128)(2,1)S(1)} %get-tuple-element.107), channel_id=1, source_target_pairs={{26,20},{27,21},{28,18},{29,19}} | collective-permute-start | bytes 786440 | tf_op jit(solution)/shard_map/ppermute | solution.py:410
  34.0 2.2 %collective-permute-start.10 = (bf16[1024,512]{1,0:T(8,128)(2,1)S(1)}, bf16[1024,512]{1,0:T(8,128)(2,1)S(1)}, u32[]{:S(2)}, u32[]{:S(2)}) collective-permute-start(bf16[1024,512]{1,0:T(8,128)(2,1)S(1)} %get-tuple-element.112), channel_id=1, source_target_pairs={{18,10},{19,11},{20,12},{21,13}} | collective-permute-start | bytes 3145736 | tf_op jit(solution)/shard_map/ppermute | solution.py:410
  34.8 0.7 collective-permute-start.11
  35.5 0.7 collective-permute-start.12
  37.4 1.5 %collective-permute-start.13 = (bf16[1280,512]{1,0:T(8,128)(2,1)S(1)}, bf16[1280,512]{1,0:T(8,128)(2,1)S(1)}, u32[]{:S(2)}, u32[]{:S(2)}) collective-permute-start(bf16[1280,512]{1,0:T(8,128)(2,1)S(1)} %get-tuple-element.116.refs_2_), channel_id=1, source_target_pairs={{10,2},{11,3},{12,4},{13,5}} | collective-permute-start | bytes 3932168 | tf_op jit(solution)/shard_map/ppermute | solution.py:410
  38.1 0.7 collective-permute-start.14
  46.0 4.7 %collective-permute-start.18 = (bf16[384,512]{1,0:T(8,128)(2,1)S(1)}, bf16[384,512]{1,0:T(8,128)(2,1)S(1)}, u32[]{:S(2)}, u32[]{:S(2)}) collective-permute-start(bf16[384,512]{1,0:T(8,128)(2,1)S(1)} %get-tuple-element.125), channel_id=1, source_target_pairs={{2,4},{3,5},{4,0},{5,1},{10,12},{11,13},{12,8},{13,9},{18,20},{19,... | collective-permute-start | bytes 1179656 | tf_op jit(solution)/shard_map/ppermute | solution.py:410
  46.7 5.3 %collective-permute-start.19 = (bf16[384,512]{1,0:T(8,128)(2,1)S(1)}, bf16[384,512]{1,0:T(8,128)(2,1)S(1)}, u32[]{:S(2)}, u32[]{:S(2)}) collective-permute-start(bf16[384,512]{1,0:T(8,128)(2,1)S(1)} %get-tuple-element.126), channel_id=1, source_target_pairs={{2,5},{3,6},{4,1},{5,2},{10,13},{11,14},{12,9},{13,10},{18,21},{19... | collective-permute-start | bytes 1179656 | tf_op jit(solution)/shard_map/ppermute | solution.py:410
  47.4 73.7 %collective-permute-start.15 = (bf16[640,512]{1,0:T(8,128)(2,1)S(1)}, bf16[640,512]{1,0:T(8,128)(2,1)S(1)}, u32[]{:S(2)}, u32[]{:S(2)}) collective-permute-start(bf16[640,512]{1,0:T(8,128)(2,1)S(1)} %get-tuple-element.122), channel_id=1, source_target_pairs={{2,3},{3,0},{4,5},{5,6},{10,11},{11,8},{12,13},{13,14},{18,19},{19... | collective-permute-start | bytes 1966088 | tf_op jit(solution)/shard_map/ppermute | solution.py:410
  48.1 88.0 %collective-permute-start.16 = (bf16[640,512]{1,0:T(8,128)(2,1)S(1)}, bf16[640,512]{1,0:T(8,128)(2,1)S(1)}, u32[]{:S(2)}, u32[]{:S(2)}) collective-permute-start(bf16[640,512]{1,0:T(8,128)(2,1)S(1)} %get-tuple-element.123), channel_id=1, source_target_pairs={{2,0},{3,1},{4,6},{5,7},{10,8},{11,9},{12,14},{13,15},{18,16},{19,... | collective-permute-start | bytes 1966088 | tf_op jit(solution)/shard_map/ppermute | solution.py:410
  49.4 89.5 %collective-permute-start.17 = (bf16[640,512]{1,0:T(8,128)(2,1)S(1)}, bf16[640,512]{1,0:T(8,128)(2,1)S(1)}, u32[]{:S(2)}, u32[]{:S(2)}) collective-permute-start(bf16[640,512]{1,0:T(8,128)(2,1)S(1)} %get-tuple-element.124), channel_id=1, source_target_pairs={{2,1},{3,2},{4,7},{5,4},{10,9},{11,10},{12,15},{13,12},{18,17},{19... | collective-permute-start | bytes 1966088 | tf_op jit(solution)/shard_map/ppermute | solution.py:410
  50.7 65.7 %collective-permute-start.20 = (bf16[384,512]{1,0:T(8,128)(2,1)S(1)}, bf16[384,512]{1,0:T(8,128)(2,1)S(1)}, u32[]{:S(2)}, u32[]{:S(2)}) collective-permute-start(bf16[384,512]{1,0:T(8,128)(2,1)S(1)} %get-tuple-element.127), channel_id=1, source_target_pairs={{2,6},{3,7},{4,2},{5,3},{10,14},{11,15},{12,10},{13,11},{18,22},{1... | collective-permute-start | bytes 1179656 | tf_op jit(solution)/shard_map/ppermute | solution.py:410
  52.0 69.0 %collective-permute-start.21 = (bf16[384,512]{1,0:T(8,128)(2,1)S(1)}, bf16[384,512]{1,0:T(8,128)(2,1)S(1)}, u32[]{:S(2)}, u32[]{:S(2)}) collective-permute-start(bf16[384,512]{1,0:T(8,128)(2,1)S(1)} %get-tuple-element.128), channel_id=1, source_target_pairs={{2,7},{3,4},{4,3},{5,0},{10,15},{11,12},{12,11},{13,8},{18,23},{19... | collective-permute-start | bytes 1179656 | tf_op jit(solution)/shard_map/ppermute | solution.py:410
  (1 other events, 0.7 us)

commit v7 on v6

--- a/solution.py
+++ b/solution.py
@@ -187,7 +187,7 @@
     several = span + 1 if first else 2
     incoming, refs = refs[:several], refs[several:]
     kept = ()
-    if not first:
+    if len(refs) > 8 and not first:
         kept, refs = refs[:2], refs[2:]
 
     @pl.when(info[0] == active)
@@ -249,10 +249,10 @@
     part_out[...] = part
 
 
-def grads_kernel(span, batches, groups, sections, info, *refs):
+def grads_kernel(span, batches, groups, sections, low, high, info, *refs):
     for group in range(2):
 
-        @pl.when(takes_part(info, sections, group))
+        @pl.when(takes_part(info, sections, group) & (info[0] >= low) & (info[0] < high))
         def _(group=group):
             grads_step(span, batches, groups, info, *refs[3 * group : 3 * group + 3], *refs[6:])
 
@@ -304,27 +304,32 @@
 
 
 def finish_kernel(span, batches, groups, info, *refs):
-    near, far = refs[:span], refs[span : 2 * span]
-    refs = refs[2 * span :]
+    sets = (refs[: 2 * span], refs[2 * span : 4 * span])
+    refs = refs[4 * span :]
     nodes_out, edges_out, send_out, recv_out, edge_out, msg_out, node_out, agg_out, out_out = refs[:9]
     held = refs[9]
     member = info[1]
     half = lax.div(member, span)
     offset = lax.rem(member, span)
     count = edges_out.shape[2]
-    for batch in range(batches):
-        turn = lax.rem(offset - base_of(half, span, batches) - batch + 2 * span, span)
-        turn_far = lax.rem(offset - batch + span, span)
-        for step in range(span):
-
-            @pl.when(turn == step)
-            def _(step=step, batch=batch):
-                edges_out[0, batch] = near[step][:count]
-                held[batch, half] = near[step][count:]
-
-            @pl.when(turn_far == step)
-            def _(step=step, batch=batch):
-                held[batch, 1 - half] = far[step][...]
+    for which in range(2):
+
+        @pl.when((info[0] == 0) == (which == 1))
+        def _(which=which):
+            near, far = sets[which][:span], sets[which][span:]
+            for batch in range(batches):
+                turn = lax.rem(offset - base_of(half, span, batches) - batch + 2 * span, span)
+                turn_far = lax.rem(offset - batch + span, span)
+                for step in range(span):
+
+                    @pl.when(turn == step)
+                    def _(step=step, batch=batch):
+                        edges_out[0, batch] = near[step][:count]
+                        held[batch, half] = near[step][count:]
+
+                    @pl.when(turn_far == step)
+                    def _(step=step, batch=batch):
+                        held[batch, 1 - half] = far[step][...]
 
     share = send_out.shape[1]
     for slot, out in enumerate((send_out, recv_out, edge_out, msg_out)):
@@ -490,11 +495,32 @@
     rows = 5 * share + share // 2 + node_share
     pay = keep = None
     incoming = None
+    across = [[(worker(m, h), (1 - h) * span + (m + step) % span) for m, h in works] for step in range(span)]
+
+    def weight_grads(low, high, keep, pay):
+        out = call(
+            functools.partial(grads_kernel, span, batches, groups, sections, low, high),
+            "weight_grads",
+            [SMEM] + [VMEM] * 9,
+            [like(count + rows)] * span + [like(rows)] * span,
+            [pltpu.VMEM((6, width, width), BF)],
+            2 * 10**10,
+            100 * 2**20,
+        )(info, *after, feats_turned, keep, pay)
+        layers = list(range(low, high))
+        far = [move(block, layers, across[step]) for step, block in enumerate(out[span:])]
+        near = [out[0]] + [move(out[step], layers, deliver[step]) for step in range(1, span)]
+        return near + far
+
+    sets = []
     for moment in range(sections):
         first = moment == 0
         layer = sections - 1 - moment
         split = layer > 0 and layer % 2 == 0
-        inputs = (top_nodes, own_top, *second_in) if first else (*incoming, pay, keep)
+        in_place = 0 < moment < sections - 1
+        inputs = (top_nodes, own_top, *second_in) if first else incoming
+        if in_place:
+            inputs = (*inputs, pay, keep)
         made = call(
             functools.partial(chain_kernel, span, batches, chunk, first, layer),
             "chain",
@@ -503,7 +529,7 @@
             [pltpu.VMEM((total, width), BF)] if first else [],
             3 * 10**9,
             10 * 2**20,
-            {} if first else {3: 0, 4: 1},
+            {3: 0, 4: 1} if in_place else {},
         )(info, *inputs, *stages[moment % 2], turned)
         pay, keep, part = made[:3]
         if split:
@@ -514,24 +540,14 @@
             cross = move(part, [layer], swap, -1)
             came = move(pay, [layer], both_ways, -1)
             incoming = (came, cross)
-
-    out = call(
-        functools.partial(grads_kernel, span, batches, groups, sections),
-        "weight_grads",
-        [SMEM] + [VMEM] * 9,
-        [like(count + rows)] * span + [like(rows)] * span,
-        [pltpu.VMEM((6, width, width), BF)],
-        2 * 10**9,
-        10 * 2**20,
-    )(info, *after, feats_turned, keep, pay)
-    across = [[(worker(m, h), (1 - h) * span + (m + step) % span) for m, h in works] for step in range(span)]
-    far = [move(block, every, across[step]) for step, block in enumerate(out[span:])]
-    near = [out[0]] + [move(out[step], every, deliver[step]) for step in range(1, span)]
+        if layer <= 1:
+            sets.append(weight_grads(layer, sections if layer else 1, keep, pay))
+
     grad_shape = jax.ShapeDtypeStruct((1, share, width), F32)
     return call(
         functools.partial(finish_kernel, span, batches, groups),
         "finish",
-        [SMEM] + [VMEM] * (2 * span),
+        [SMEM] + [VMEM] * (4 * span),
         [
             jax.ShapeDtypeStruct((1, batches, node_share, width), BF),
             jax.ShapeDtypeStruct((1, batches, count, width), BF),
@@ -540,7 +556,7 @@
         [pltpu.VMEM((batches, PARTS, rows, width), BF)],
         0,
         5 * 2**20,
-    )(info, *near, *far)
+    )(info, *sets[0], *sets[1])
 
 
 def solution(mesh):

time: 141 us -> 138 us (0.979)
  waiting for transfers between devices: 88.9 us -> 79.6 us
  starting transfers between devices: 21.7 us -> 26.7 us
    ppermute x22 -> x29, waiting for transfers between devices: 88.9 us -> 79.6 us  [move(): return lax.ppermute(value, axes, pairs)]
    ppermute x22 -> x29, starting transfers between devices: 21.7 us -> 26.7 us  [move(): return lax.ppermute(value, axes, pairs)]
    pallas_call x1 -> x2, Pallas kernels: 2.84 us -> 3.44 us  [weight_grads(): call(functools.partial(grads_kernel, span, batches, groups, sections, low...]
    unnamed x28 -> x36, local copies, waits for them, and re-layouts: 7.55 us -> 7.57 us
  transfers between devices with their start and end apart: 22 -> 29, of which waited for: 6 -> 6; matrix products, arithmetic and copies ran while one was open for 2% -> 3% of each run, Pallas kernels for 6% -> 12%
where the time goes in v7:
time: 138 us; the launch traced here: 137 us
  waiting for transfers between devices  79.6 us (58%)
  starting transfers between devices  26.7 us (19%)
  Pallas kernels  22.1 us (16%)
  local copies, waits for them, and re-layouts  7.61 us (6%)
    ppermute x29, waiting for transfers between devices, move(): return lax.ppermute(value, axes, pairs)  79.6 us
    ppermute x29, starting transfers between devices, move(): return lax.ppermute(value, axes, pairs)  26.7 us
    unnamed x36, local copies, waits for them, and re-layouts  7.57 us
    pallas_call x4, Pallas kernels, body(): call(functools.partial(chain_kernel, span, batches, chunk, first, layer),...  7.45 us
    pallas_call x2, Pallas kernels, body(): call(functools.partial(forward_kernel, span, chunk, sections, group), 'fo...  3.67 us
    pallas_call x2, Pallas kernels, weight_grads(): call(functools.partial(grads_kernel, span, batches, groups, sections, low...  3.44 us
  transfers between devices with their start and end apart: 29, of which 6 were waited for; matrix products, arithmetic and copies ran while one was open for 3% of the time, Pallas kernels for 12%

profile of v7, /device:TPU:26, one launch (start us, length us, event | category | flops | bytes accessed | tf_op | source)
XLA Modules:
  0.0 137.4 jit_solution(11740155973718784064)
XLA Ops:
  0.7 1.0 copy-done.1
  1.8 1.0 copy-done.2
  4.9 0.8 pack.1
  7.7 1.1 constant_dynamic-update-slice_fusion.6
  8.8 1.1 constant_dynamic-update-slice_fusion.5
  9.9 1.1 constant_dynamic-update-slice_fusion.4
  11.2 1.6 %ready.1 = (bf16[7,512,512]{2,1,0:T(8,128)(2,1)S(1)}, bf16[512,512]{1,0:T(8,128)(2,1)S(1)}, f32[256,512]{1,0:T(8,128)S(1)}, bf16[512,256]{1,0:T(8,128)(2,1)S(1)}) custom-call(s32[2]{0:T(128)S(1)} %pad_add_fusion.info, bf16[1,2,256,512]{3,2,1,0:T(8,128)(2,1)S(1)} %copy-done, bf16[7,512,512]{2,1,0:T(8,128)(2,1)S(1)} %constant_dynamic-update-slice_fusion.weights.refs_5_), custom_call_target="tpu_custom_call" | custom-call | flops 400000000 | bytes 10485760 | tf_op jit(solution)/shard_map/ready/pallas_call | solution.py:441
  13.6 4.1 %collective-permute-start.5 = (bf16[272,512]{1,0:T(8,128)(2,1)S(1)}, bf16[272,512]{1,0:T(8,128)(2,1)S(1)}, u32[]{:S(2)}, u32[]{:S(2)}) collective-permute-start(bf16[272,512]{1,0:T(8,128)(2,1)S(1)} %get-tuple-element.101), channel_id=1, source_target_pairs={{16,18},{17,19},{22,20},{23,21},{0,2},{1,3},{6,4},{7,5},{24,26},{2... | collective-permute-start | bytes 835592 | tf_op jit(solution)/shard_map/ppermute | solution.py:415
  17.7 1.3 collective-permute-start.6
  21.8 3.0 %collective-permute-done.6.refs_3_.refs_4_ = bf16[272,512]{1,0:T(8,128)(2,1)S(1)} collective-permute-done((bf16[272,512]{1,0:T(8,128)(2,1)S(1)}, bf16[272,512]{1,0:T(8,128)(2,1)S(1)}, u32[]{:S(2)}, u32[]{:S(2)}) %collective-permute-start.6) | collective-permute-done | bytes 278560 | tf_op jit(solution)/shard_map/ppermute | solution.py:415
  25.3 0.7 collective-permute-start.8
  26.0 3.1 %forward.3 = (bf16[1024,512]{1,0:T(8,128)(2,1)S(1)}, bf16[1024,512]{1,0:T(8,128)(2,1)S(1)}, bf16[256,512]{1,0:T(8,128)(2,1)S(1)}, bf16[1024,256]{1,0:T(8,128)(2,...) custom-call(s32[2]{0:T(128)S(1)} %pad_add_fusion.info, ...), custom_call_target="tpu_custom_call" | custom-call | flops 2000000000 | bytes 6291456 | tf_op jit(solution)/shard_map/forward/pallas_call | solution.py:462
  30.5 1.2 turn.3
  31.7 1.0 node_forward.3.refs_7_.refs_5_
  32.7 1.3 chain.5
  34.0 0.7 collective-permute-start.10
  36.3 1.1 chain.6
  38.1 0.7 collective-permute-start.20
  42.2 0.8 collective-permute-start.13
  43.1 4.5 %chain.7 = (bf16[1280,512]{1,0:T(8,128)(2,1)S(1)}, bf16[3072,512]{1,0:T(8,128)(2,1)S(1)}, bf16[256,512]{1,0:T(8,128)(2,1)}) custom-call(s32[2]{0:T(128)S(1)} %pad_add_fusion.info, bf16[1280,512]{1,0:T(8,128)(2,1)S(1)} %collective-permute-done.20.refs_0_, bf16[256,512]{1,0:T(8,128)(2,1)S(1)} %collective-permute-done.21.refs_1_, ...), custom_call_target="tpu_custom_call" | custom-call | flops 3000000000 | bytes 10485760 | tf_op jit(solution)/shard_map/chain/pallas_call | solution.py:524
  48.3 0.7 collective-permute-start.15
  49.0 2.9 %weight_grads.3 = (bf16[640,512]{1,0:T(8,128)(2,1)S(1)}, bf16[640,512]{1,0:T(8,128)(2,1)S(1)}, bf16[640,512]{1,0:T(8,128)(2,1)S(1)}, bf16[640,512]{1,0:T(8,128)(...) custom-call(s32[2]{0:T(128)S(1)} %pad_add_fusion.info, ...), custom_call_target="tpu_custom_call" | custom-call | flops 20000000000 | bytes 104857600 | tf_op jit(solution)/shard_map/weight_grads/pallas_call | solution.py:501
  53.3 0.7 collective-permute-start.22
  54.0 1.3 collective-permute-start.23
  55.3 1.3 collective-permute-start.24
  56.6 1.3 collective-permute-start.27
  58.0 1.3 collective-permute-start.28
  59.3 52.4 %collective-permute-done.27.refs_14_ = bf16[384,512]{1,0:T(8,128)(2,1)S(1)} collective-permute-done((bf16[384,512]{1,0:T(8,128)(2,1)S(1)}, bf16[384,512]{1,0:T(8,128)(2,1)S(1)}, u32[]{:S(2)}, u32[]{:S(2)}) %collective-permute-start.27) | collective-permute-done | bytes 393248 | tf_op jit(solution)/shard_map/ppermute | solution.py:415
  111.6 4.4 %collective-permute-done.28.refs_15_ = bf16[384,512]{1,0:T(8,128)(2,1)S(1)} collective-permute-done((bf16[384,512]{1,0:T(8,128)(2,1)S(1)}, bf16[384,512]{1,0:T(8,128)(2,1)S(1)}, u32[]{:S(2)}, u32[]{:S(2)}) %collective-permute-start.28) | collective-permute-done | bytes 393248 | tf_op jit(solution)/shard_map/ppermute | solution.py:415
  116.0 15.1 %collective-permute-done.23.refs_10_ = bf16[640,512]{1,0:T(8,128)(2,1)S(1)} collective-permute-done((bf16[640,512]{1,0:T(8,128)(2,1)S(1)}, bf16[640,512]{1,0:T(8,128)(2,1)S(1)}, u32[]{:S(2)}, u32[]{:S(2)}) %collective-permute-start.23) | collective-permute-done | bytes 655392 | tf_op jit(solution)/shard_map/ppermute | solution.py:415
  131.2 4.4 %collective-permute-done.24.refs_11_ = bf16[640,512]{1,0:T(8,128)(2,1)S(1)} collective-permute-done((bf16[640,512]{1,0:T(8,128)(2,1)S(1)}, bf16[640,512]{1,0:T(8,128)(2,1)S(1)}, u32[]{:S(2)}, u32[]{:S(2)}) %collective-permute-start.24) | collective-permute-done | bytes 655392 | tf_op jit(solution)/shard_map/ppermute | solution.py:415
  135.5 1.9 %finish.1 = (bf16[1,2,32,512]{3,2,1,0:T(8,128)(2,1)}, bf16[1,2,256,512]{3,2,1,0:T(8,128)(2,1)}, f32[1,64,512]{2,1,0:T(8,128)}, f32[1,64,512]{2,1,0:T(8,128)}, f3...) custom-call(s32[2]{0:T(128)S(1)} %pad_add_fusion.info, ...), custom_call_target="tpu_custom_call" | custom-call | bytes 5242880 | tf_op jit(solution)/shard_map/finish/pallas_call | solution.py:547
  (80 shorter events, 17.1 us)
Async XLA Ops:
  5.6 7.3 %collective-permute-start = (bf16[272,512]{1,0:T(8,128)(2,1)S(1)}, bf16[272,512]{1,0:T(8,128)(2,1)S(1)}, u32[]{:S(2)}, u32[]{:S(2)}) collective-permute-start(bf16[272,512]{1,0:T(8,128)(2,1)S(1)} %get-tuple-element.79), channel_id=1, source_target_pairs={{27,26},{24,27},{29,28},{30,29},{11,10},{8,11},{13,12},{14,13}} | collective-permute-start | bytes 835592 | tf_op jit(solution)/shard_map/ppermute | solution.py:415
  6.3 12.7 %collective-permute-start.1 = (bf16[272,512]{1,0:T(8,128)(2,1)S(1)}, bf16[272,512]{1,0:T(8,128)(2,1)S(1)}, u32[]{:S(2)}, u32[]{:S(2)}) collective-permute-start(bf16[272,512]{1,0:T(8,128)(2,1)S(1)} %get-tuple-element.84), channel_id=1, source_target_pairs={{24,26},{25,27},{30,28},{31,29},{8,10},{9,11},{14,12},{15,13}} | collective-permute-start | bytes 835592 | tf_op jit(solution)/shard_map/ppermute | solution.py:415
  7.0 12.0 %collective-permute-start.2 = (bf16[272,512]{1,0:T(8,128)(2,1)S(1)}, bf16[272,512]{1,0:T(8,128)(2,1)S(1)}, u32[]{:S(2)}, u32[]{:S(2)}) collective-permute-start(bf16[272,512]{1,0:T(8,128)(2,1)S(1)} %get-tuple-element.85), channel_id=1, source_target_pairs={{25,26},{26,27},{31,28},{28,29},{9,10},{10,11},{15,12},{12,13}} | collective-permute-start | bytes 835592 | tf_op jit(solution)/shard_map/ppermute | solution.py:415
  12.9 8.6 %collective-permute-start.4 = (bf16[272,512]{1,0:T(8,128)(2,1)S(1)}, bf16[272,512]{1,0:T(8,128)(2,1)S(1)}, u32[]{:S(2)}, u32[]{:S(2)}) collective-permute-start(bf16[272,512]{1,0:T(8,128)(2,1)S(1)} %get-tuple-element.100), channel_id=1, source_target_pairs={{19,18},{16,19},{21,20},{22,21},{3,2},{0,3},{5,4},{6,5},{27,26},{2... | collective-permute-start | bytes 835592 | tf_op jit(solution)/shard_map/ppermute | solution.py:415
  13.6 8.2 %collective-permute-start.5 = (bf16[272,512]{1,0:T(8,128)(2,1)S(1)}, bf16[272,512]{1,0:T(8,128)(2,1)S(1)}, u32[]{:S(2)}, u32[]{:S(2)}) collective-permute-start(bf16[272,512]{1,0:T(8,128)(2,1)S(1)} %get-tuple-element.101), channel_id=1, source_target_pairs={{16,18},{17,19},{22,20},{23,21},{0,2},{1,3},{6,4},{7,5},{24,26},{2... | collective-permute-start | bytes 835592 | tf_op jit(solution)/shard_map/ppermute | solution.py:415
  17.7 7.0 %collective-permute-start.6 = (bf16[272,512]{1,0:T(8,128)(2,1)S(1)}, bf16[272,512]{1,0:T(8,128)(2,1)S(1)}, u32[]{:S(2)}, u32[]{:S(2)}) collective-permute-start(bf16[272,512]{1,0:T(8,128)(2,1)S(1)} %get-tuple-element.102), channel_id=1, source_target_pairs={{17,18},{18,19},{23,20},{20,21},{1,2},{2,3},{7,4},{4,5},{25,26},{2... | collective-permute-start | bytes 835592 | tf_op jit(solution)/shard_map/ppermute | solution.py:415
  19.6 1.3 collective-permute-start.3
  20.9 18.0 %copy-start.6 = (bf16[512,1024]{1,0:T(8,128)(2,1)}, bf16[512,1024]{1,0:T(8,128)(2,1)S(1)}, u32[]{:S(2)}) copy-start(bf16[512,1024]{1,0:T(8,128)(2,1)S(1)} %get-tuple-element.97.refs_1_) | copy-start | bytes 3145732
  25.3 7.4 %collective-permute-start.8 = (bf16[1280,512]{1,0:T(8,128)(2,1)S(1)}, bf16[1280,512]{1,0:T(8,128)(2,1)S(1)}, u32[]{:S(2)}, u32[]{:S(2)}) collective-permute-start(bf16[1280,512]{1,0:T(8,128)(2,1)S(1)} %get-tuple-element.114.refs_2_), channel_id=1, source_target_pairs={{26,18},{27,19},{28,20},{29,21}} | collective-permute-start | bytes 3932168 | tf_op jit(solution)/shard_map/ppermute | solution.py:415
  29.2 2.6 %collective-permute-start.7 = (bf16[256,512]{1,0:T(8,128)(2,1)S(1)}, bf16[256,512]{1,0:T(8,128)(2,1)S(1)}, u32[]{:S(2)}, u32[]{:S(2)}) collective-permute-start(bf16[256,512]{1,0:T(8,128)(2,1)S(1)} %get-tuple-element.107.part_own), channel_id=1, source_target_pairs={{18,20},{19,21},{20,18},{21,19},{2,4},{3,5},{4,2},{5,3}} | collective-permute-start | bytes 786440 | tf_op jit(solution)/shard_map/ppermute | solution.py:415
  29.9 2.9 %collective-permute-start.9 = (bf16[256,512]{1,0:T(8,128)(2,1)S(1)}, bf16[256,512]{1,0:T(8,128)(2,1)S(1)}, u32[]{:S(2)}, u32[]{:S(2)}) collective-permute-start(bf16[256,512]{1,0:T(8,128)(2,1)S(1)} %get-tuple-element.115), channel_id=1, source_target_pairs={{26,20},{27,21},{28,18},{29,19}} | collective-permute-start | bytes 786440 | tf_op jit(solution)/shard_map/ppermute | solution.py:415
  31.7 7.1 %copy-start.8 = (bf16[512,1024]{1,0:T(8,128)(2,1)}, bf16[512,1024]{1,0:T(8,128)(2,1)S(1)}, u32[]{:S(2)}) copy-start(bf16[512,1024]{1,0:T(8,128)(2,1)S(1)} %get-tuple-element.106.refs_4_) | copy-start | bytes 3145732
  34.0 2.2 %collective-permute-start.10 = (bf16[1024,512]{1,0:T(8,128)(2,1)S(1)}, bf16[1024,512]{1,0:T(8,128)(2,1)S(1)}, u32[]{:S(2)}, u32[]{:S(2)}) collective-permute-start(bf16[1024,512]{1,0:T(8,128)(2,1)S(1)} %get-tuple-element.120), channel_id=1, source_target_pairs={{18,10},{19,11},{20,12},{21,13}} | collective-permute-start | bytes 3145736 | tf_op jit(solution)/shard_map/ppermute | solution.py:415
  34.8 0.7 collective-permute-start.11
  35.6 0.7 collective-permute-start.12
  37.4 4.1 %collective-permute-start.21 = (bf16[256,512]{1,0:T(8,128)(2,1)S(1)}, bf16[256,512]{1,0:T(8,128)(2,1)S(1)}, u32[]{:S(2)}, u32[]{:S(2)}) collective-permute-start(bf16[256,512]{1,0:T(8,128)(2,1)S(1)} %get-tuple-element.134), channel_id=1, source_target_pairs={{10,4},{11,5},{12,2},{13,3}} | collective-permute-start | bytes 786440 | tf_op jit(solution)/shard_map/ppermute | solution.py:415
  38.1 4.1 %collective-permute-start.20 = (bf16[1280,512]{1,0:T(8,128)(2,1)S(1)}, bf16[1280,512]{1,0:T(8,128)(2,1)S(1)}, u32[]{:S(2)}, u32[]{:S(2)}) collective-permute-start(bf16[1280,512]{1,0:T(8,128)(2,1)S(1)} %get-tuple-element.125.refs_8_), channel_id=1, source_target_pairs={{10,2},{11,3},{12,4},{13,5}} | collective-permute-start | bytes 3932168 | tf_op jit(solution)/shard_map/ppermute | solution.py:415
  39.4 8.1 %collective-permute-start.16 = (bf16[384,512]{1,0:T(8,128)(2,1)S(1)}, bf16[384,512]{1,0:T(8,128)(2,1)S(1)}, u32[]{:S(2)}, u32[]{:S(2)}) collective-permute-start(bf16[384,512]{1,0:T(8,128)(2,1)S(1)} %get-tuple-element.130), channel_id=1, source_target_pairs={{10,12},{11,13},{12,8},{13,9},{18,20},{19,21},{20,16},{21,17},{26,... | collective-permute-start | bytes 1179656 | tf_op jit(solution)/shard_map/ppermute | solution.py:415
  40.1 8.2 %collective-permute-start.17 = (bf16[384,512]{1,0:T(8,128)(2,1)S(1)}, bf16[384,512]{1,0:T(8,128)(2,1)S(1)}, u32[]{:S(2)}, u32[]{:S(2)}) collective-permute-start(bf16[384,512]{1,0:T(8,128)(2,1)S(1)} %get-tuple-element.131), channel_id=1, source_target_pairs={{10,13},{11,14},{12,9},{13,10},{18,21},{19,22},{20,17},{21,18},{26... | collective-permute-start | bytes 1179656 | tf_op jit(solution)/shard_map/ppermute | solution.py:415
  40.8 11.1 %collective-permute-start.18 = (bf16[384,512]{1,0:T(8,128)(2,1)S(1)}, bf16[384,512]{1,0:T(8,128)(2,1)S(1)}, u32[]{:S(2)}, u32[]{:S(2)}) collective-permute-start(bf16[384,512]{1,0:T(8,128)(2,1)S(1)} %get-tuple-element.132), channel_id=1, source_target_pairs={{10,14},{11,15},{12,10},{13,11},{18,22},{19,23},{20,18},{21,19},{2... | collective-permute-start | bytes 1179656 | tf_op jit(solution)/shard_map/ppermute | solution.py:415
  41.5 11.1 %collective-permute-start.19 = (bf16[384,512]{1,0:T(8,128)(2,1)S(1)}, bf16[384,512]{1,0:T(8,128)(2,1)S(1)}, u32[]{:S(2)}, u32[]{:S(2)}) collective-permute-start(bf16[384,512]{1,0:T(8,128)(2,1)S(1)} %get-tuple-element.133), channel_id=1, source_target_pairs={{10,15},{11,12},{12,11},{13,8},{18,23},{19,20},{20,19},{21,16},{26... | collective-permute-start | bytes 1179656 | tf_op jit(solution)/shard_map/ppermute | solution.py:415
  42.2 6.8 %copy-start.7 = (bf16[512,1024]{1,0:T(8,128)(2,1)S(1)}, bf16[512,1024]{1,0:T(8,128)(2,1)}, u32[]{:S(2)}) copy-start(bf16[512,1024]{1,0:T(8,128)(2,1)} %copy-done.6) | copy-start | bytes 3145732
  42.2 11.0 %collective-permute-start.13 = (bf16[640,512]{1,0:T(8,128)(2,1)S(1)}, bf16[640,512]{1,0:T(8,128)(2,1)S(1)}, u32[]{:S(2)}, u32[]{:S(2)}) collective-permute-start(bf16[640,512]{1,0:T(8,128)(2,1)S(1)} %get-tuple-element.127), channel_id=1, source_target_pairs={{10,11},{11,8},{12,13},{13,14},{18,19},{19,16},{20,21},{21,22},{26... | collective-permute-start | bytes 1966088 | tf_op jit(solution)/shard_map/ppermute | solution.py:415
  47.6 6.4 %collective-permute-start.14 = (bf16[640,512]{1,0:T(8,128)(2,1)S(1)}, bf16[640,512]{1,0:T(8,128)(2,1)S(1)}, u32[]{:S(2)}, u32[]{:S(2)}) collective-permute-start(bf16[640,512]{1,0:T(8,128)(2,1)S(1)} %get-tuple-element.128), channel_id=1, source_target_pairs={{10,8},{11,9},{12,14},{13,15},{18,16},{19,17},{20,22},{21,23},{26,... | collective-permute-start | bytes 1966088 | tf_op jit(solution)/shard_map/ppermute | solution.py:415
  48.3 7.0 %collective-permute-start.15 = (bf16[640,512]{1,0:T(8,128)(2,1)S(1)}, bf16[640,512]{1,0:T(8,128)(2,1)S(1)}, u32[]{:S(2)}, u32[]{:S(2)}) collective-permute-start(bf16[640,512]{1,0:T(8,128)(2,1)S(1)} %get-tuple-element.129), channel_id=1, source_target_pairs={{10,9},{11,10},{12,15},{13,12},{18,17},{19,18},{20,23},{21,20},{26... | collective-permute-start | bytes 1966088 | tf_op jit(solution)/shard_map/ppermute | solution.py:415
  51.9 4.7 %collective-permute-start.25 = (bf16[384,512]{1,0:T(8,128)(2,1)S(1)}, bf16[384,512]{1,0:T(8,128)(2,1)S(1)}, u32[]{:S(2)}, u32[]{:S(2)}) collective-permute-start(bf16[384,512]{1,0:T(8,128)(2,1)S(1)} %get-tuple-element.141), channel_id=1, source_target_pairs={{2,4},{3,5},{4,0},{5,1}} | collective-permute-start | bytes 1179656 | tf_op jit(solution)/shard_map/ppermute | solution.py:415
  52.6 5.3 %collective-permute-start.26 = (bf16[384,512]{1,0:T(8,128)(2,1)S(1)}, bf16[384,512]{1,0:T(8,128)(2,1)S(1)}, u32[]{:S(2)}, u32[]{:S(2)}) collective-permute-start(bf16[384,512]{1,0:T(8,128)(2,1)S(1)} %get-tuple-element.142), channel_id=1, source_target_pairs={{2,5},{3,6},{4,1},{5,2}} | collective-permute-start | bytes 1179656 | tf_op jit(solution)/shard_map/ppermute | solution.py:415
  53.3 62.7 %collective-permute-start.22 = (bf16[640,512]{1,0:T(8,128)(2,1)S(1)}, bf16[640,512]{1,0:T(8,128)(2,1)S(1)}, u32[]{:S(2)}, u32[]{:S(2)}) collective-permute-start(bf16[640,512]{1,0:T(8,128)(2,1)S(1)} %get-tuple-element.138), channel_id=1, source_target_pairs={{2,3},{3,0},{4,5},{5,6}} | collective-permute-start | bytes 1966088 | tf_op jit(solution)/shard_map/ppermute | solution.py:415
  54.0 77.1 %collective-permute-start.23 = (bf16[640,512]{1,0:T(8,128)(2,1)S(1)}, bf16[640,512]{1,0:T(8,128)(2,1)S(1)}, u32[]{:S(2)}, u32[]{:S(2)}) collective-permute-start(bf16[640,512]{1,0:T(8,128)(2,1)S(1)} %get-tuple-element.139), channel_id=1, source_target_pairs={{2,0},{3,1},{4,6},{5,7}} | collective-permute-start | bytes 1966088 | tf_op jit(solution)/shard_map/ppermute | solution.py:415
  55.3 80.2 %collective-permute-start.24 = (bf16[640,512]{1,0:T(8,128)(2,1)S(1)}, bf16[640,512]{1,0:T(8,128)(2,1)S(1)}, u32[]{:S(2)}, u32[]{:S(2)}) collective-permute-start(bf16[640,512]{1,0:T(8,128)(2,1)S(1)} %get-tuple-element.140), channel_id=1, source_target_pairs={{2,1},{3,2},{4,7},{5,4}} | collective-permute-start | bytes 1966088 | tf_op jit(solution)/shard_map/ppermute | solution.py:415
  56.6 55.0 %collective-permute-start.27 = (bf16[384,512]{1,0:T(8,128)(2,1)S(1)}, bf16[384,512]{1,0:T(8,128)(2,1)S(1)}, u32[]{:S(2)}, u32[]{:S(2)}) collective-permute-start(bf16[384,512]{1,0:T(8,128)(2,1)S(1)} %get-tuple-element.143), channel_id=1, source_target_pairs={{2,6},{3,7},{4,2},{5,3}} | collective-permute-start | bytes 1179656 | tf_op jit(solution)/shard_map/ppermute | solution.py:415
  58.0 58.1 %collective-permute-start.28 = (bf16[384,512]{1,0:T(8,128)(2,1)S(1)}, bf16[384,512]{1,0:T(8,128)(2,1)S(1)}, u32[]{:S(2)}, u32[]{:S(2)}) collective-permute-start(bf16[384,512]{1,0:T(8,128)(2,1)S(1)} %get-tuple-element.144), channel_id=1, source_target_pairs={{2,7},{3,4},{4,3},{5,0}} | collective-permute-start | bytes 1179656 | tf_op jit(solution)/shard_map/ppermute | solution.py:415
  (12 other events, 43.2 us)

commit v8 on v7

--- a/solution.py
+++ b/solution.py
@@ -41,6 +41,14 @@
 
 def worker_of(batch, half, span, batches):
     return half * span + place_of(batch, half, span, batches)
+
+
+def far_order(span):
+    return sorted(range(span), key=lambda step: (1 - step % 2, step))
+
+
+def near_order(span):
+    return [0] + [step for step in far_order(span) if step]
 
 
 def own_batch(member, span, batches):
@@ -297,10 +305,11 @@
         at_node = pl.multiple_of(total + owner * node_share, node_share)
         block[start + 5 * share + share // 2 :] = pay[pl.ds(at_node, node_share)]
 
-    for step in range(span):
-        near[step][:count] = pay[step * count : (step + 1) * count]
-        fill(near[step], count, half * span + lax.rem(offset + step, span))
-        fill(far[step], 0, (1 - half) * span + lax.rem(batch + step, span))
+    for block, step in zip(near, near_order(span)):
+        block[:count] = pay[step * count : (step + 1) * count]
+        fill(block, count, half * span + lax.rem(offset + step, span))
+    for block, step in zip(far, far_order(span)):
+        fill(block, 0, (1 - half) * span + lax.rem(batch + step, span))
 
 
 def finish_kernel(span, batches, groups, info, *refs):
@@ -320,16 +329,18 @@
             for batch in range(batches):
                 turn = lax.rem(offset - base_of(half, span, batches) - batch + 2 * span, span)
                 turn_far = lax.rem(offset - batch + span, span)
-                for step in range(span):
+                for block, step in zip(near, near_order(span)):
 
                     @pl.when(turn == step)
-                    def _(step=step, batch=batch):
-                        edges_out[0, batch] = near[step][:count]
-                        held[batch, half] = near[step][count:]
+                    def _(block=block, batch=batch):
+                        edges_out[0, batch] = block[:count]
+                        held[batch, half] = block[count:]
+
+                for block, step in zip(far, far_order(span)):
 
                     @pl.when(turn_far == step)
-                    def _(step=step, batch=batch):
-                        held[batch, 1 - half] = far[step][...]
+                    def _(block=block, batch=batch):
+                        held[batch, 1 - half] = block[...]
 
     share = send_out.shape[1]
     for slot, out in enumerate((send_out, recv_out, edge_out, msg_out)):
@@ -508,8 +519,9 @@
             100 * 2**20,
         )(info, *after, feats_turned, keep, pay)
         layers = list(range(low, high))
-        far = [move(block, layers, across[step]) for step, block in enumerate(out[span:])]
-        near = [out[0]] + [move(out[step], layers, deliver[step]) for step in range(1, span)]
+        far = [move(block, layers, across[step]) for block, step in zip(out[span:], far_order(span))]
+        near = [out[0]]
+        near += [move(block, layers, deliver[step]) for block, step in zip(out[1:span], near_order(span)[1:])]
         return near + far
 
     sets = []

time: 138 us -> 140 us (1.014)
  the two profiles are of different devices: /device:TPU:26 before, /device:TPU:24 now
where the time goes in v8:
time: 140 us; the launch traced here: 139 us
  waiting for transfers between devices  82.3 us (59%)
  starting transfers between devices  25.8 us (18%)
  Pallas kernels  22.1 us (16%)
  local copies, waits for them, and re-layouts  7.61 us (5%)
    ppermute x29, waiting for transfers between devices, move(): return lax.ppermute(value, axes, pairs)  82.3 us
    ppermute x29, starting transfers between devices, move(): return lax.ppermute(value, axes, pairs)  25.8 us
    unnamed x36, local copies, waits for them, and re-layouts  7.57 us
    pallas_call x4, Pallas kernels, body(): call(functools.partial(chain_kernel, span, batches, chunk, first, layer),...  7.44 us
    pallas_call x2, Pallas kernels, body(): call(functools.partial(forward_kernel, span, chunk, sections, group), 'fo...  3.67 us
    pallas_call x2, Pallas kernels, weight_grads(): call(functools.partial(grads_kernel, span, batches, groups, sections, low...  3.44 us
  transfers between devices with their start and end apart: 29, of which 4 were waited for; matrix products, arithmetic and copies ran while one was open for 3% of the time, Pallas kernels for 12%

profile of v8, /device:TPU:24, one launch (start us, length us, event | category | flops | bytes accessed | tf_op | source)
XLA Modules:
  0.0 139.3 jit_solution(3318698106707597779)
XLA Ops:
  0.7 1.0 copy-done.1
  1.8 1.0 copy-done.2
  4.9 0.8 pack.1
  7.7 1.1 constant_dynamic-update-slice_fusion.6
  8.8 1.1 constant_dynamic-update-slice_fusion.5
  9.9 1.1 constant_dynamic-update-slice_fusion.4
  11.2 1.6 %ready.1 = (bf16[7,512,512]{2,1,0:T(8,128)(2,1)S(1)}, bf16[512,512]{1,0:T(8,128)(2,1)S(1)}, f32[256,512]{1,0:T(8,128)S(1)}, bf16[512,256]{1,0:T(8,128)(2,1)S(1)}) custom-call(s32[2]{0:T(128)S(1)} %pad_add_fusion.info, bf16[1,2,256,512]{3,2,1,0:T(8,128)(2,1)S(1)} %copy-done, bf16[7,512,512]{2,1,0:T(8,128)(2,1)S(1)} %constant_dynamic-update-slice_fusion.weights.refs_5_), custom_call_target="tpu_custom_call" | custom-call | flops 400000000 | bytes 10485760 | tf_op jit(solution)/shard_map/ready/pallas_call | solution.py:452
  12.9 3.3 %collective-permute-start.4 = (bf16[272,512]{1,0:T(8,128)(2,1)S(1)}, bf16[272,512]{1,0:T(8,128)(2,1)S(1)}, u32[]{:S(2)}, u32[]{:S(2)}) collective-permute-start(bf16[272,512]{1,0:T(8,128)(2,1)S(1)} %get-tuple-element.100), channel_id=1, source_target_pairs={{19,18},{16,19},{21,20},{22,21},{3,2},{0,3},{5,4},{6,5},{27,26},{2... | collective-permute-start | bytes 835592 | tf_op jit(solution)/shard_map/ppermute | solution.py:426
  16.2 1.3 collective-permute-start.5
  20.6 2.6 %collective-permute-done.5.refs_2_.refs_3_ = bf16[272,512]{1,0:T(8,128)(2,1)S(1)} collective-permute-done((bf16[272,512]{1,0:T(8,128)(2,1)S(1)}, bf16[272,512]{1,0:T(8,128)(2,1)S(1)}, u32[]{:S(2)}, u32[]{:S(2)}) %collective-permute-start.5) | collective-permute-done | bytes 278560 | tf_op jit(solution)/shard_map/ppermute | solution.py:426
  23.8 0.7 collective-permute-start.8
  24.5 3.1 %forward.3 = (bf16[1024,512]{1,0:T(8,128)(2,1)S(1)}, bf16[1024,512]{1,0:T(8,128)(2,1)S(1)}, bf16[256,512]{1,0:T(8,128)(2,1)S(1)}, bf16[1024,256]{1,0:T(8,128)(2,...) custom-call(s32[2]{0:T(128)S(1)} %pad_add_fusion.info, ...), custom_call_target="tpu_custom_call" | custom-call | flops 2000000000 | bytes 6291456 | tf_op jit(solution)/shard_map/forward/pallas_call | solution.py:473
  29.0 1.2 turn.3
  30.2 1.0 node_forward.3.refs_7_.refs_5_
  31.2 1.3 chain.5
  32.5 0.7 collective-permute-start.10
  34.7 1.1 chain.6
  36.5 0.7 collective-permute-start.20
  40.7 0.8 collective-permute-start.13
  41.6 4.5 %chain.7 = (bf16[1280,512]{1,0:T(8,128)(2,1)S(1)}, bf16[3072,512]{1,0:T(8,128)(2,1)S(1)}, bf16[256,512]{1,0:T(8,128)(2,1)}) custom-call(s32[2]{0:T(128)S(1)} %pad_add_fusion.info, bf16[1280,512]{1,0:T(8,128)(2,1)S(1)} %collective-permute-done.20.refs_0_, bf16[256,512]{1,0:T(8,128)(2,1)S(1)} %collective-permute-done.21.refs_1_, ...), custom_call_target="tpu_custom_call" | custom-call | flops 3000000000 | bytes 10485760 | tf_op jit(solution)/shard_map/chain/pallas_call | solution.py:536
  46.0 0.7 collective-permute-start.14
  46.8 0.7 collective-permute-start.15
  47.5 2.9 %weight_grads.3 = (bf16[640,512]{1,0:T(8,128)(2,1)S(1)}, bf16[640,512]{1,0:T(8,128)(2,1)S(1)}, bf16[640,512]{1,0:T(8,128)(2,1)S(1)}, bf16[640,512]{1,0:T(8,128)(...) custom-call(s32[2]{0:T(128)S(1)} %pad_add_fusion.info, ...), custom_call_target="tpu_custom_call" | custom-call | flops 20000000000 | bytes 104857600 | tf_op jit(solution)/shard_map/weight_grads/pallas_call | solution.py:512
  50.4 1.3 collective-permute-start.25
  52.4 1.3 collective-permute-start.22
  53.7 0.7 collective-permute-start.23
  54.4 1.3 collective-permute-start.24
  55.7 46.5 %collective-permute-done.25.refs_12_ = bf16[384,512]{1,0:T(8,128)(2,1)S(1)} collective-permute-done((bf16[384,512]{1,0:T(8,128)(2,1)S(1)}, bf16[384,512]{1,0:T(8,128)(2,1)S(1)}, u32[]{:S(2)}, u32[]{:S(2)}) %collective-permute-start.25) | collective-permute-done | bytes 393248 | tf_op jit(solution)/shard_map/ppermute | solution.py:426
  102.9 1.3 collective-permute-start.28
  104.2 13.6 %collective-permute-done.28.refs_15_ = bf16[384,512]{1,0:T(8,128)(2,1)S(1)} collective-permute-done((bf16[384,512]{1,0:T(8,128)(2,1)S(1)}, bf16[384,512]{1,0:T(8,128)(2,1)S(1)}, u32[]{:S(2)}, u32[]{:S(2)}) %collective-permute-start.28) | collective-permute-done | bytes 393248 | tf_op jit(solution)/shard_map/ppermute | solution.py:426
  117.8 19.6 %collective-permute-done.24.refs_11_ = bf16[640,512]{1,0:T(8,128)(2,1)S(1)} collective-permute-done((bf16[640,512]{1,0:T(8,128)(2,1)S(1)}, bf16[640,512]{1,0:T(8,128)(2,1)S(1)}, u32[]{:S(2)}, u32[]{:S(2)}) %collective-permute-start.24) | collective-permute-done | bytes 655392 | tf_op jit(solution)/shard_map/ppermute | solution.py:426
  137.4 1.9 %finish.1 = (bf16[1,2,32,512]{3,2,1,0:T(8,128)(2,1)}, bf16[1,2,256,512]{3,2,1,0:T(8,128)(2,1)}, f32[1,64,512]{2,1,0:T(8,128)}, f32[1,64,512]{2,1,0:T(8,128)}, f3...) custom-call(s32[2]{0:T(128)S(1)} %pad_add_fusion.info, ...), custom_call_target="tpu_custom_call" | custom-call | bytes 5242880 | tf_op jit(solution)/shard_map/finish/pallas_call | solution.py:559
  (80 shorter events, 16.1 us)
Async XLA Ops:
  5.6 7.3 %collective-permute-start = (bf16[272,512]{1,0:T(8,128)(2,1)S(1)}, bf16[272,512]{1,0:T(8,128)(2,1)S(1)}, u32[]{:S(2)}, u32[]{:S(2)}) collective-permute-start(bf16[272,512]{1,0:T(8,128)(2,1)S(1)} %get-tuple-element.79), channel_id=1, source_target_pairs={{27,26},{24,27},{29,28},{30,29},{11,10},{8,11},{13,12},{14,13}} | collective-permute-start | bytes 835592 | tf_op jit(solution)/shard_map/ppermute | solution.py:426
  6.3 11.9 %collective-permute-start.1 = (bf16[272,512]{1,0:T(8,128)(2,1)S(1)}, bf16[272,512]{1,0:T(8,128)(2,1)S(1)}, u32[]{:S(2)}, u32[]{:S(2)}) collective-permute-start(bf16[272,512]{1,0:T(8,128)(2,1)S(1)} %get-tuple-element.84), channel_id=1, source_target_pairs={{24,26},{25,27},{30,28},{31,29},{8,10},{9,11},{14,12},{15,13}} | collective-permute-start | bytes 835592 | tf_op jit(solution)/shard_map/ppermute | solution.py:426
  7.0 11.2 %collective-permute-start.2 = (bf16[272,512]{1,0:T(8,128)(2,1)S(1)}, bf16[272,512]{1,0:T(8,128)(2,1)S(1)}, u32[]{:S(2)}, u32[]{:S(2)}) collective-permute-start(bf16[272,512]{1,0:T(8,128)(2,1)S(1)} %get-tuple-element.85), channel_id=1, source_target_pairs={{25,26},{26,27},{31,28},{28,29},{9,10},{10,11},{15,12},{12,13}} | collective-permute-start | bytes 835592 | tf_op jit(solution)/shard_map/ppermute | solution.py:426
  12.9 7.7 %collective-permute-start.4 = (bf16[272,512]{1,0:T(8,128)(2,1)S(1)}, bf16[272,512]{1,0:T(8,128)(2,1)S(1)}, u32[]{:S(2)}, u32[]{:S(2)}) collective-permute-start(bf16[272,512]{1,0:T(8,128)(2,1)S(1)} %get-tuple-element.100), channel_id=1, source_target_pairs={{19,18},{16,19},{21,20},{22,21},{3,2},{0,3},{5,4},{6,5},{27,26},{2... | collective-permute-start | bytes 835592 | tf_op jit(solution)/shard_map/ppermute | solution.py:426
  16.2 7.0 %collective-permute-start.5 = (bf16[272,512]{1,0:T(8,128)(2,1)S(1)}, bf16[272,512]{1,0:T(8,128)(2,1)S(1)}, u32[]{:S(2)}, u32[]{:S(2)}) collective-permute-start(bf16[272,512]{1,0:T(8,128)(2,1)S(1)} %get-tuple-element.101), channel_id=1, source_target_pairs={{16,18},{17,19},{22,20},{23,21},{0,2},{1,3},{6,4},{7,5},{24,26},{2... | collective-permute-start | bytes 835592 | tf_op jit(solution)/shard_map/ppermute | solution.py:426
  17.5 5.7 %collective-permute-start.6 = (bf16[272,512]{1,0:T(8,128)(2,1)S(1)}, bf16[272,512]{1,0:T(8,128)(2,1)S(1)}, u32[]{:S(2)}, u32[]{:S(2)}) collective-permute-start(bf16[272,512]{1,0:T(8,128)(2,1)S(1)} %get-tuple-element.102), channel_id=1, source_target_pairs={{17,18},{18,19},{23,20},{20,21},{1,2},{2,3},{7,4},{4,5},{25,26},{2... | collective-permute-start | bytes 835592 | tf_op jit(solution)/shard_map/ppermute | solution.py:426
  18.8 1.3 collective-permute-start.3
  20.0 17.3 %copy-start.6 = (bf16[512,1024]{1,0:T(8,128)(2,1)}, bf16[512,1024]{1,0:T(8,128)(2,1)S(1)}, u32[]{:S(2)}) copy-start(bf16[512,1024]{1,0:T(8,128)(2,1)S(1)} %get-tuple-element.97.refs_1_) | copy-start | bytes 3145732
  23.8 7.4 %collective-permute-start.8 = (bf16[1280,512]{1,0:T(8,128)(2,1)S(1)}, bf16[1280,512]{1,0:T(8,128)(2,1)S(1)}, u32[]{:S(2)}, u32[]{:S(2)}) collective-permute-start(bf16[1280,512]{1,0:T(8,128)(2,1)S(1)} %get-tuple-element.114.refs_2_), channel_id=1, source_target_pairs={{26,18},{27,19},{28,20},{29,21}} | collective-permute-start | bytes 3932168 | tf_op jit(solution)/shard_map/ppermute | solution.py:426
  27.6 2.6 %collective-permute-start.7 = (bf16[256,512]{1,0:T(8,128)(2,1)S(1)}, bf16[256,512]{1,0:T(8,128)(2,1)S(1)}, u32[]{:S(2)}, u32[]{:S(2)}) collective-permute-start(bf16[256,512]{1,0:T(8,128)(2,1)S(1)} %get-tuple-element.107.part_own), channel_id=1, source_target_pairs={{18,20},{19,21},{20,18},{21,19},{2,4},{3,5},{4,2},{5,3}} | collective-permute-start | bytes 786440 | tf_op jit(solution)/shard_map/ppermute | solution.py:426
  28.3 2.9 %collective-permute-start.9 = (bf16[256,512]{1,0:T(8,128)(2,1)S(1)}, bf16[256,512]{1,0:T(8,128)(2,1)S(1)}, u32[]{:S(2)}, u32[]{:S(2)}) collective-permute-start(bf16[256,512]{1,0:T(8,128)(2,1)S(1)} %get-tuple-element.115), channel_id=1, source_target_pairs={{26,20},{27,21},{28,18},{29,19}} | collective-permute-start | bytes 786440 | tf_op jit(solution)/shard_map/ppermute | solution.py:426
  30.2 7.1 %copy-start.8 = (bf16[512,1024]{1,0:T(8,128)(2,1)}, bf16[512,1024]{1,0:T(8,128)(2,1)S(1)}, u32[]{:S(2)}) copy-start(bf16[512,1024]{1,0:T(8,128)(2,1)S(1)} %get-tuple-element.106.refs_4_) | copy-start | bytes 3145732
  32.5 2.2 %collective-permute-start.10 = (bf16[1024,512]{1,0:T(8,128)(2,1)S(1)}, bf16[1024,512]{1,0:T(8,128)(2,1)S(1)}, u32[]{:S(2)}, u32[]{:S(2)}) collective-permute-start(bf16[1024,512]{1,0:T(8,128)(2,1)S(1)} %get-tuple-element.120), channel_id=1, source_target_pairs={{18,10},{19,11},{20,12},{21,13}} | collective-permute-start | bytes 3145736 | tf_op jit(solution)/shard_map/ppermute | solution.py:426
  33.3 0.7 collective-permute-start.11
  34.0 0.7 collective-permute-start.12
  35.9 4.1 %collective-permute-start.21 = (bf16[256,512]{1,0:T(8,128)(2,1)S(1)}, bf16[256,512]{1,0:T(8,128)(2,1)S(1)}, u32[]{:S(2)}, u32[]{:S(2)}) collective-permute-start(bf16[256,512]{1,0:T(8,128)(2,1)S(1)} %get-tuple-element.134), channel_id=1, source_target_pairs={{10,4},{11,5},{12,2},{13,3}} | collective-permute-start | bytes 786440 | tf_op jit(solution)/shard_map/ppermute | solution.py:426
  36.5 4.1 %collective-permute-start.20 = (bf16[1280,512]{1,0:T(8,128)(2,1)S(1)}, bf16[1280,512]{1,0:T(8,128)(2,1)S(1)}, u32[]{:S(2)}, u32[]{:S(2)}) collective-permute-start(bf16[1280,512]{1,0:T(8,128)(2,1)S(1)} %get-tuple-element.125.refs_8_), channel_id=1, source_target_pairs={{10,2},{11,3},{12,4},{13,5}} | collective-permute-start | bytes 3932168 | tf_op jit(solution)/shard_map/ppermute | solution.py:426
  37.9 8.1 %collective-permute-start.16 = (bf16[384,512]{1,0:T(8,128)(2,1)S(1)}, bf16[384,512]{1,0:T(8,128)(2,1)S(1)}, u32[]{:S(2)}, u32[]{:S(2)}) collective-permute-start(bf16[384,512]{1,0:T(8,128)(2,1)S(1)} %get-tuple-element.130), channel_id=1, source_target_pairs={{10,13},{11,14},{12,9},{13,10},{18,21},{19,22},{20,17},{21,18},{26... | collective-permute-start | bytes 1179656 | tf_op jit(solution)/shard_map/ppermute | solution.py:426
  38.6 8.1 %collective-permute-start.17 = (bf16[384,512]{1,0:T(8,128)(2,1)S(1)}, bf16[384,512]{1,0:T(8,128)(2,1)S(1)}, u32[]{:S(2)}, u32[]{:S(2)}) collective-permute-start(bf16[384,512]{1,0:T(8,128)(2,1)S(1)} %get-tuple-element.131), channel_id=1, source_target_pairs={{10,15},{11,12},{12,11},{13,8},{18,23},{19,20},{20,19},{21,16},{26... | collective-permute-start | bytes 1179656 | tf_op jit(solution)/shard_map/ppermute | solution.py:426
  39.3 11.1 %collective-permute-start.18 = (bf16[384,512]{1,0:T(8,128)(2,1)S(1)}, bf16[384,512]{1,0:T(8,128)(2,1)S(1)}, u32[]{:S(2)}, u32[]{:S(2)}) collective-permute-start(bf16[384,512]{1,0:T(8,128)(2,1)S(1)} %get-tuple-element.132), channel_id=1, source_target_pairs={{10,12},{11,13},{12,8},{13,9},{18,20},{19,21},{20,16},{21,17},{26,... | collective-permute-start | bytes 1179656 | tf_op jit(solution)/shard_map/ppermute | solution.py:426
  40.0 11.7 %collective-permute-start.19 = (bf16[384,512]{1,0:T(8,128)(2,1)S(1)}, bf16[384,512]{1,0:T(8,128)(2,1)S(1)}, u32[]{:S(2)}, u32[]{:S(2)}) collective-permute-start(bf16[384,512]{1,0:T(8,128)(2,1)S(1)} %get-tuple-element.133), channel_id=1, source_target_pairs={{10,14},{11,15},{12,10},{13,11},{18,22},{19,23},{20,18},{21,19},{2... | collective-permute-start | bytes 1179656 | tf_op jit(solution)/shard_map/ppermute | solution.py:426
  40.7 6.8 %copy-start.7 = (bf16[512,1024]{1,0:T(8,128)(2,1)S(1)}, bf16[512,1024]{1,0:T(8,128)(2,1)}, u32[]{:S(2)}) copy-start(bf16[512,1024]{1,0:T(8,128)(2,1)} %copy-done.6) | copy-start | bytes 3145732
  40.7 11.7 %collective-permute-start.13 = (bf16[640,512]{1,0:T(8,128)(2,1)S(1)}, bf16[640,512]{1,0:T(8,128)(2,1)S(1)}, u32[]{:S(2)}, u32[]{:S(2)}) collective-permute-start(bf16[640,512]{1,0:T(8,128)(2,1)S(1)} %get-tuple-element.127), channel_id=1, source_target_pairs={{10,11},{11,8},{12,13},{13,14},{18,19},{19,16},{20,21},{21,22},{26... | collective-permute-start | bytes 1966088 | tf_op jit(solution)/shard_map/ppermute | solution.py:426
  46.0 7.6 %collective-permute-start.14 = (bf16[640,512]{1,0:T(8,128)(2,1)S(1)}, bf16[640,512]{1,0:T(8,128)(2,1)S(1)}, u32[]{:S(2)}, u32[]{:S(2)}) collective-permute-start(bf16[640,512]{1,0:T(8,128)(2,1)S(1)} %get-tuple-element.128), channel_id=1, source_target_pairs={{10,9},{11,10},{12,15},{13,12},{18,17},{19,18},{20,23},{21,20},{26... | collective-permute-start | bytes 1966088 | tf_op jit(solution)/shard_map/ppermute | solution.py:426
  46.8 7.6 %collective-permute-start.15 = (bf16[640,512]{1,0:T(8,128)(2,1)S(1)}, bf16[640,512]{1,0:T(8,128)(2,1)S(1)}, u32[]{:S(2)}, u32[]{:S(2)}) collective-permute-start(bf16[640,512]{1,0:T(8,128)(2,1)S(1)} %get-tuple-element.129), channel_id=1, source_target_pairs={{10,8},{11,9},{12,14},{13,15},{18,16},{19,17},{20,22},{21,23},{26,... | collective-permute-start | bytes 1966088 | tf_op jit(solution)/shard_map/ppermute | solution.py:426
  50.4 51.8 %collective-permute-start.25 = (bf16[384,512]{1,0:T(8,128)(2,1)S(1)}, bf16[384,512]{1,0:T(8,128)(2,1)S(1)}, u32[]{:S(2)}, u32[]{:S(2)}) collective-permute-start(bf16[384,512]{1,0:T(8,128)(2,1)S(1)} %get-tuple-element.141), channel_id=1, source_target_pairs={{2,5},{3,6},{4,1},{5,2}} | collective-permute-start | bytes 1179656 | tf_op jit(solution)/shard_map/ppermute | solution.py:426
  51.7 51.2 %collective-permute-start.26 = (bf16[384,512]{1,0:T(8,128)(2,1)S(1)}, bf16[384,512]{1,0:T(8,128)(2,1)S(1)}, u32[]{:S(2)}, u32[]{:S(2)}) collective-permute-start(bf16[384,512]{1,0:T(8,128)(2,1)S(1)} %get-tuple-element.142), channel_id=1, source_target_pairs={{2,7},{3,4},{4,3},{5,0}} | collective-permute-start | bytes 1179656 | tf_op jit(solution)/shard_map/ppermute | solution.py:426
  52.4 65.4 %collective-permute-start.22 = (bf16[640,512]{1,0:T(8,128)(2,1)S(1)}, bf16[640,512]{1,0:T(8,128)(2,1)S(1)}, u32[]{:S(2)}, u32[]{:S(2)}) collective-permute-start(bf16[640,512]{1,0:T(8,128)(2,1)S(1)} %get-tuple-element.138), channel_id=1, source_target_pairs={{2,3},{3,0},{4,5},{5,6}} | collective-permute-start | bytes 1966088 | tf_op jit(solution)/shard_map/ppermute | solution.py:426
  53.7 64.1 %collective-permute-start.23 = (bf16[640,512]{1,0:T(8,128)(2,1)S(1)}, bf16[640,512]{1,0:T(8,128)(2,1)S(1)}, u32[]{:S(2)}, u32[]{:S(2)}) collective-permute-start(bf16[640,512]{1,0:T(8,128)(2,1)S(1)} %get-tuple-element.139), channel_id=1, source_target_pairs={{2,1},{3,2},{4,7},{5,4}} | collective-permute-start | bytes 1966088 | tf_op jit(solution)/shard_map/ppermute | solution.py:426
  54.4 83.0 %collective-permute-start.24 = (bf16[640,512]{1,0:T(8,128)(2,1)S(1)}, bf16[640,512]{1,0:T(8,128)(2,1)S(1)}, u32[]{:S(2)}, u32[]{:S(2)}) collective-permute-start(bf16[640,512]{1,0:T(8,128)(2,1)S(1)} %get-tuple-element.140), channel_id=1, source_target_pairs={{2,0},{3,1},{4,6},{5,7}} | collective-permute-start | bytes 1966088 | tf_op jit(solution)/shard_map/ppermute | solution.py:426
  102.2 2.0 %collective-permute-start.27 = (bf16[384,512]{1,0:T(8,128)(2,1)S(1)}, bf16[384,512]{1,0:T(8,128)(2,1)S(1)}, u32[]{:S(2)}, u32[]{:S(2)}) collective-permute-start(bf16[384,512]{1,0:T(8,128)(2,1)S(1)} %get-tuple-element.143), channel_id=1, source_target_pairs={{2,4},{3,5},{4,0},{5,1}} | collective-permute-start | bytes 1179656 | tf_op jit(solution)/shard_map/ppermute | solution.py:426
  102.9 14.9 %collective-permute-start.28 = (bf16[384,512]{1,0:T(8,128)(2,1)S(1)}, bf16[384,512]{1,0:T(8,128)(2,1)S(1)}, u32[]{:S(2)}, u32[]{:S(2)}) collective-permute-start(bf16[384,512]{1,0:T(8,128)(2,1)S(1)} %get-tuple-element.144), channel_id=1, source_target_pairs={{2,6},{3,7},{4,2},{5,3}} | collective-permute-start | bytes 1179656 | tf_op jit(solution)/shard_map/ppermute | solution.py:426
  (12 other events, 42.5 us)

commit v9 on v7

--- a/solution.py
+++ b/solution.py
@@ -508,9 +508,8 @@
             100 * 2**20,
         )(info, *after, feats_turned, keep, pay)
         layers = list(range(low, high))
-        far = [move(block, layers, across[step]) for step, block in enumerate(out[span:])]
         near = [out[0]] + [move(out[step], layers, deliver[step]) for step in range(1, span)]
-        return near + far
+        return near, list(out[span:]), layers
 
     sets = []
     for moment in range(sections):
@@ -541,8 +540,13 @@
             came = move(pay, [layer], both_ways, -1)
             incoming = (came, cross)
         if layer <= 1:
+            if sets:
+                pay, sets[0][1][:] = lax.optimization_barrier((pay, sets[0][1]))
             sets.append(weight_grads(layer, sections if layer else 1, keep, pay))
 
+    blocks = []
+    for near, far, layers in sets:
+        blocks += near + [move(block, layers, across[step]) for step, block in enumerate(far)]
     grad_shape = jax.ShapeDtypeStruct((1, share, width), F32)
     return call(
         functools.partial(finish_kernel, span, batches, groups),
@@ -556,7 +560,7 @@
         [pltpu.VMEM((batches, PARTS, rows, width), BF)],
         0,
         5 * 2**20,
-    )(info, *sets[0], *sets[1])
+    )(info, *blocks)
 
 
 def solution(mesh):

time: 138 us -> 138 us (level)
  waiting for transfers between devices: 79.6 us -> 78.2 us
    ppermute x29, waiting for transfers between devices: 79.6 us -> 78.2 us  [move(): return lax.ppermute(value, axes, pairs)]
    unnamed x36 -> x40, local copies, waits for them, and re-layouts: 7.57 us -> 7.58 us
  transfers between devices with their start and end apart: 29 -> 29, of which waited for: 6 -> 6; matrix products, arithmetic and copies ran while one was open for 3% -> 3% of each run, Pallas kernels for 12% -> 13%
where the time goes in v9:
time: 138 us; the launch traced here: 137 us
  waiting for transfers between devices  78.2 us (57%)
  starting transfers between devices  26.6 us (19%)
  Pallas kernels  23 us (17%)
  local copies, waits for them, and re-layouts  7.62 us (6%)
    ppermute x29, waiting for transfers between devices, move(): return lax.ppermute(value, axes, pairs)  78.2 us
    ppermute x29, starting transfers between devices, move(): return lax.ppermute(value, axes, pairs)  26.6 us
    unnamed x40, local copies, waits for them, and re-layouts  7.58 us
    pallas_call x4, Pallas kernels, body(): call(functools.partial(chain_kernel, span, batches, chunk, first, layer),...  7.43 us
    pallas_call x2, Pallas kernels, weight_grads(): call(functools.partial(grads_kernel, span, batches, groups, sections, low...  4.34 us
    pallas_call x2, Pallas kernels, body(): call(functools.partial(forward_kernel, span, chunk, sections, group), 'fo...  3.67 us
  transfers between devices with their start and end apart: 29, of which 6 were waited for; matrix products, arithmetic and copies ran while one was open for 3% of the time, Pallas kernels for 13%

profile of v9, /device:TPU:26, one launch (start us, length us, event | category | flops | bytes accessed | tf_op | source)
XLA Modules:
  0.0 136.9 jit_solution(6381365799626134257)
XLA Ops:
  0.7 1.0 copy-done.1
  1.8 1.0 copy-done.2
  4.9 0.8 pack.1
  7.7 1.1 constant_dynamic-update-slice_fusion.6
  8.8 1.1 constant_dynamic-update-slice_fusion.5
  9.9 1.1 constant_dynamic-update-slice_fusion.4
  11.2 1.6 %ready.1 = (bf16[7,512,512]{2,1,0:T(8,128)(2,1)S(1)}, bf16[512,512]{1,0:T(8,128)(2,1)S(1)}, f32[256,512]{1,0:T(8,128)S(1)}, bf16[512,256]{1,0:T(8,128)(2,1)S(1)}) custom-call(s32[2]{0:T(128)S(1)} %pad_add_fusion.info, bf16[1,2,256,512]{3,2,1,0:T(8,128)(2,1)S(1)} %copy-done, bf16[7,512,512]{2,1,0:T(8,128)(2,1)S(1)} %constant_dynamic-update-slice_fusion.weights.refs_5_), custom_call_target="tpu_custom_call" | custom-call | flops 400000000 | bytes 10485760 | tf_op jit(solution)/shard_map/ready/pallas_call | solution.py:441
  13.6 4.1 %collective-permute-start.5 = (bf16[272,512]{1,0:T(8,128)(2,1)S(1)}, bf16[272,512]{1,0:T(8,128)(2,1)S(1)}, u32[]{:S(2)}, u32[]{:S(2)}) collective-permute-start(bf16[272,512]{1,0:T(8,128)(2,1)S(1)} %get-tuple-element.106), channel_id=1, source_target_pairs={{16,18},{17,19},{22,20},{23,21},{0,2},{1,3},{6,4},{7,5},{24,26},{2... | collective-permute-start | bytes 835592 | tf_op jit(solution)/shard_map/ppermute | solution.py:415
  17.7 1.3 collective-permute-start.6
  21.8 3.0 %collective-permute-done.6.refs_3_.refs_4_ = bf16[272,512]{1,0:T(8,128)(2,1)S(1)} collective-permute-done((bf16[272,512]{1,0:T(8,128)(2,1)S(1)}, bf16[272,512]{1,0:T(8,128)(2,1)S(1)}, u32[]{:S(2)}, u32[]{:S(2)}) %collective-permute-start.6) | collective-permute-done | bytes 278560 | tf_op jit(solution)/shard_map/ppermute | solution.py:415
  25.3 0.7 collective-permute-start.8
  26.1 3.1 %forward.3 = (bf16[1024,512]{1,0:T(8,128)(2,1)S(1)}, bf16[1024,512]{1,0:T(8,128)(2,1)S(1)}, bf16[256,512]{1,0:T(8,128)(2,1)S(1)}, bf16[1024,256]{1,0:T(8,128)(2,...) custom-call(s32[2]{0:T(128)S(1)} %pad_add_fusion.info, ...), custom_call_target="tpu_custom_call" | custom-call | flops 2000000000 | bytes 6291456 | tf_op jit(solution)/shard_map/forward/pallas_call | solution.py:462
  30.5 1.2 turn.3
  31.8 1.0 node_forward.3.refs_7_.refs_5_
  32.8 1.3 chain.5
  34.1 0.7 collective-permute-start.10
  36.3 1.1 chain.6
  37.4 0.7 collective-permute-start.16
  38.2 1.5 %weight_grads.2 = (bf16[640,512]{1,0:T(8,128)(2,1)S(1)}, bf16[640,512]{1,0:T(8,128)(2,1)S(1)}, bf16[640,512]{1,0:T(8,128)(2,1)S(1)}, bf16[640,512]{1,0:T(8,128)(...) custom-call(s32[2]{0:T(128)S(1)} %pad_add_fusion.info, ...), custom_call_target="tpu_custom_call" | custom-call | flops 20000000000 | bytes 104857600 | tf_op jit(solution)/shard_map/weight_grads/pallas_call | solution.py:501
  40.4 0.7 collective-permute-start.14
  41.8 0.8 collective-permute-start.15
  42.6 4.5 %chain.7 = (bf16[1280,512]{1,0:T(8,128)(2,1)S(1)}, bf16[3072,512]{1,0:T(8,128)(2,1)S(1)}, bf16[256,512]{1,0:T(8,128)(2,1)}) custom-call(s32[2]{0:T(128)S(1)} %pad_add_fusion.info, bf16[1280,512]{1,0:T(8,128)(2,1)S(1)} %collective-permute-done.16.refs_0_, bf16[256,512]{1,0:T(8,128)(2,1)S(1)} %collective-permute-done.17.refs_1_, ...), custom_call_target="tpu_custom_call" | custom-call | flops 3000000000 | bytes 10485760 | tf_op jit(solution)/shard_map/chain/pallas_call | solution.py:523
  49.9 2.9 %weight_grads.3 = (bf16[640,512]{1,0:T(8,128)(2,1)S(1)}, bf16[640,512]{1,0:T(8,128)(2,1)S(1)}, bf16[640,512]{1,0:T(8,128)(2,1)S(1)}, bf16[640,512]{1,0:T(8,128)(...) custom-call(s32[2]{0:T(128)S(1)} %pad_add_fusion.info, ...), custom_call_target="tpu_custom_call" | custom-call | flops 20000000000 | bytes 104857600 | tf_op jit(solution)/shard_map/weight_grads/pallas_call | solution.py:501
  54.9 1.3 collective-permute-start.23
  56.2 1.3 collective-permute-start.24
  57.5 1.3 collective-permute-start.27
  58.9 1.3 collective-permute-start.28
  60.2 60.7 %collective-permute-done.27.refs_14_ = bf16[384,512]{1,0:T(8,128)(2,1)S(1)} collective-permute-done((bf16[384,512]{1,0:T(8,128)(2,1)S(1)}, bf16[384,512]{1,0:T(8,128)(2,1)S(1)}, u32[]{:S(2)}, u32[]{:S(2)}) %collective-permute-start.27) | collective-permute-done | bytes 393248 | tf_op jit(solution)/shard_map/ppermute | solution.py:415
  120.9 5.1 %collective-permute-done.28.refs_15_ = bf16[384,512]{1,0:T(8,128)(2,1)S(1)} collective-permute-done((bf16[384,512]{1,0:T(8,128)(2,1)S(1)}, bf16[384,512]{1,0:T(8,128)(2,1)S(1)}, u32[]{:S(2)}, u32[]{:S(2)}) %collective-permute-start.28) | collective-permute-done | bytes 393248 | tf_op jit(solution)/shard_map/ppermute | solution.py:415
  126.0 3.3 %collective-permute-done.23.refs_10_ = bf16[640,512]{1,0:T(8,128)(2,1)S(1)} collective-permute-done((bf16[640,512]{1,0:T(8,128)(2,1)S(1)}, bf16[640,512]{1,0:T(8,128)(2,1)S(1)}, u32[]{:S(2)}, u32[]{:S(2)}) %collective-permute-start.23) | collective-permute-done | bytes 655392 | tf_op jit(solution)/shard_map/ppermute | solution.py:415
  129.3 5.7 %collective-permute-done.24.refs_11_ = bf16[640,512]{1,0:T(8,128)(2,1)S(1)} collective-permute-done((bf16[640,512]{1,0:T(8,128)(2,1)S(1)}, bf16[640,512]{1,0:T(8,128)(2,1)S(1)}, u32[]{:S(2)}, u32[]{:S(2)}) %collective-permute-start.24) | collective-permute-done | bytes 655392 | tf_op jit(solution)/shard_map/ppermute | solution.py:415
  135.0 1.9 %finish.1 = (bf16[1,2,32,512]{3,2,1,0:T(8,128)(2,1)}, bf16[1,2,256,512]{3,2,1,0:T(8,128)(2,1)}, f32[1,64,512]{2,1,0:T(8,128)}, f32[1,64,512]{2,1,0:T(8,128)}, f3...) custom-call(s32[2]{0:T(128)S(1)} %pad_add_fusion.info, ...), custom_call_target="tpu_custom_call" | custom-call | bytes 5242880 | tf_op jit(solution)/shard_map/finish/pallas_call | solution.py:551
  (84 shorter events, 17.2 us)
Async XLA Ops:
  5.6 7.3 %collective-permute-start = (bf16[272,512]{1,0:T(8,128)(2,1)S(1)}, bf16[272,512]{1,0:T(8,128)(2,1)S(1)}, u32[]{:S(2)}, u32[]{:S(2)}) collective-permute-start(bf16[272,512]{1,0:T(8,128)(2,1)S(1)} %get-tuple-element.84), channel_id=1, source_target_pairs={{27,26},{24,27},{29,28},{30,29},{11,10},{8,11},{13,12},{14,13}} | collective-permute-start | bytes 835592 | tf_op jit(solution)/shard_map/ppermute | solution.py:415
  6.3 12.7 %collective-permute-start.1 = (bf16[272,512]{1,0:T(8,128)(2,1)S(1)}, bf16[272,512]{1,0:T(8,128)(2,1)S(1)}, u32[]{:S(2)}, u32[]{:S(2)}) collective-permute-start(bf16[272,512]{1,0:T(8,128)(2,1)S(1)} %get-tuple-element.89), channel_id=1, source_target_pairs={{24,26},{25,27},{30,28},{31,29},{8,10},{9,11},{14,12},{15,13}} | collective-permute-start | bytes 835592 | tf_op jit(solution)/shard_map/ppermute | solution.py:415
  7.0 12.1 %collective-permute-start.2 = (bf16[272,512]{1,0:T(8,128)(2,1)S(1)}, bf16[272,512]{1,0:T(8,128)(2,1)S(1)}, u32[]{:S(2)}, u32[]{:S(2)}) collective-permute-start(bf16[272,512]{1,0:T(8,128)(2,1)S(1)} %get-tuple-element.90), channel_id=1, source_target_pairs={{25,26},{26,27},{31,28},{28,29},{9,10},{10,11},{15,12},{12,13}} | collective-permute-start | bytes 835592 | tf_op jit(solution)/shard_map/ppermute | solution.py:415
  12.9 25.3 %copy-start.11 = (bf16[512,256]{1,0:T(8,128)(2,1)}, bf16[512,256]{1,0:T(8,128)(2,1)S(1)}, u32[]{:S(2)}) copy-start(bf16[512,256]{1,0:T(8,128)(2,1)S(1)} %get-tuple-element.113.refs_6_) | copy-start | bytes 786436
  12.9 8.6 %collective-permute-start.4 = (bf16[272,512]{1,0:T(8,128)(2,1)S(1)}, bf16[272,512]{1,0:T(8,128)(2,1)S(1)}, u32[]{:S(2)}, u32[]{:S(2)}) collective-permute-start(bf16[272,512]{1,0:T(8,128)(2,1)S(1)} %get-tuple-element.105), channel_id=1, source_target_pairs={{19,18},{16,19},{21,20},{22,21},{3,2},{0,3},{5,4},{6,5},{27,26},{2... | collective-permute-start | bytes 835592 | tf_op jit(solution)/shard_map/ppermute | solution.py:415
  13.6 8.2 %collective-permute-start.5 = (bf16[272,512]{1,0:T(8,128)(2,1)S(1)}, bf16[272,512]{1,0:T(8,128)(2,1)S(1)}, u32[]{:S(2)}, u32[]{:S(2)}) collective-permute-start(bf16[272,512]{1,0:T(8,128)(2,1)S(1)} %get-tuple-element.106), channel_id=1, source_target_pairs={{16,18},{17,19},{22,20},{23,21},{0,2},{1,3},{6,4},{7,5},{24,26},{2... | collective-permute-start | bytes 835592 | tf_op jit(solution)/shard_map/ppermute | solution.py:415
  17.7 7.0 %collective-permute-start.6 = (bf16[272,512]{1,0:T(8,128)(2,1)S(1)}, bf16[272,512]{1,0:T(8,128)(2,1)S(1)}, u32[]{:S(2)}, u32[]{:S(2)}) collective-permute-start(bf16[272,512]{1,0:T(8,128)(2,1)S(1)} %get-tuple-element.107), channel_id=1, source_target_pairs={{17,18},{18,19},{23,20},{20,21},{1,2},{2,3},{7,4},{4,5},{25,26},{2... | collective-permute-start | bytes 835592 | tf_op jit(solution)/shard_map/ppermute | solution.py:415
  19.6 1.3 collective-permute-start.3
  20.9 17.3 %copy-start.6 = (bf16[512,1024]{1,0:T(8,128)(2,1)}, bf16[512,1024]{1,0:T(8,128)(2,1)S(1)}, u32[]{:S(2)}) copy-start(bf16[512,1024]{1,0:T(8,128)(2,1)S(1)} %get-tuple-element.102.refs_1_) | copy-start | bytes 3145732
  25.3 7.4 %collective-permute-start.8 = (bf16[1280,512]{1,0:T(8,128)(2,1)S(1)}, bf16[1280,512]{1,0:T(8,128)(2,1)S(1)}, u32[]{:S(2)}, u32[]{:S(2)}) collective-permute-start(bf16[1280,512]{1,0:T(8,128)(2,1)S(1)} %get-tuple-element.119.refs_2_), channel_id=1, source_target_pairs={{26,18},{27,19},{28,20},{29,21}} | collective-permute-start | bytes 3932168 | tf_op jit(solution)/shard_map/ppermute | solution.py:415
  29.2 2.6 %collective-permute-start.7 = (bf16[256,512]{1,0:T(8,128)(2,1)S(1)}, bf16[256,512]{1,0:T(8,128)(2,1)S(1)}, u32[]{:S(2)}, u32[]{:S(2)}) collective-permute-start(bf16[256,512]{1,0:T(8,128)(2,1)S(1)} %get-tuple-element.112.part_own), channel_id=1, source_target_pairs={{18,20},{19,21},{20,18},{21,19},{2,4},{3,5},{4,2},{5,3}} | collective-permute-start | bytes 786440 | tf_op jit(solution)/shard_map/ppermute | solution.py:415
  29.9 2.9 %collective-permute-start.9 = (bf16[256,512]{1,0:T(8,128)(2,1)S(1)}, bf16[256,512]{1,0:T(8,128)(2,1)S(1)}, u32[]{:S(2)}, u32[]{:S(2)}) collective-permute-start(bf16[256,512]{1,0:T(8,128)(2,1)S(1)} %get-tuple-element.120), channel_id=1, source_target_pairs={{26,20},{27,21},{28,18},{29,19}} | collective-permute-start | bytes 786440 | tf_op jit(solution)/shard_map/ppermute | solution.py:415
  34.1 2.2 %collective-permute-start.10 = (bf16[1024,512]{1,0:T(8,128)(2,1)S(1)}, bf16[1024,512]{1,0:T(8,128)(2,1)S(1)}, u32[]{:S(2)}, u32[]{:S(2)}) collective-permute-start(bf16[1024,512]{1,0:T(8,128)(2,1)S(1)} %get-tuple-element.125), channel_id=1, source_target_pairs={{18,10},{19,11},{20,12},{21,13}} | collective-permute-start | bytes 3145736 | tf_op jit(solution)/shard_map/ppermute | solution.py:415
  34.8 0.7 collective-permute-start.11
  35.6 0.7 collective-permute-start.12
  37.4 5.2 %collective-permute-start.16 = (bf16[1280,512]{1,0:T(8,128)(2,1)S(1)}, bf16[1280,512]{1,0:T(8,128)(2,1)S(1)}, u32[]{:S(2)}, u32[]{:S(2)}) collective-permute-start(bf16[1280,512]{1,0:T(8,128)(2,1)S(1)} %get-tuple-element.130.refs_8_), channel_id=1, source_target_pairs={{10,2},{11,3},{12,4},{13,5}} | collective-permute-start | bytes 3932168 | tf_op jit(solution)/shard_map/ppermute | solution.py:415
  39.7 8.8 %collective-permute-start.13 = (bf16[640,512]{1,0:T(8,128)(2,1)S(1)}, bf16[640,512]{1,0:T(8,128)(2,1)S(1)}, u32[]{:S(2)}, u32[]{:S(2)}) collective-permute-start(bf16[640,512]{1,0:T(8,128)(2,1)S(1)} %get-tuple-element.132), channel_id=1, source_target_pairs={{10,11},{11,8},{12,13},{13,14},{18,19},{19,16},{20,21},{21,22},{26... | collective-permute-start | bytes 1966088 | tf_op jit(solution)/shard_map/ppermute | solution.py:415
  40.4 8.8 %collective-permute-start.14 = (bf16[640,512]{1,0:T(8,128)(2,1)S(1)}, bf16[640,512]{1,0:T(8,128)(2,1)S(1)}, u32[]{:S(2)}, u32[]{:S(2)}) collective-permute-start(bf16[640,512]{1,0:T(8,128)(2,1)S(1)} %get-tuple-element.133), channel_id=1, source_target_pairs={{10,8},{11,9},{12,14},{13,15},{18,16},{19,17},{20,22},{21,23},{26,... | collective-permute-start | bytes 1966088 | tf_op jit(solution)/shard_map/ppermute | solution.py:415
  41.1 1.6 %collective-permute-start.17 = (bf16[256,512]{1,0:T(8,128)(2,1)S(1)}, bf16[256,512]{1,0:T(8,128)(2,1)S(1)}, u32[]{:S(2)}, u32[]{:S(2)}) collective-permute-start(bf16[256,512]{1,0:T(8,128)(2,1)S(1)} %get-tuple-element.135), channel_id=1, source_target_pairs={{10,4},{11,5},{12,2},{13,3}} | collective-permute-start | bytes 786440 | tf_op jit(solution)/shard_map/ppermute | solution.py:415
  41.7 8.1 %copy-start.7 = (bf16[512,1024]{1,0:T(8,128)(2,1)S(1)}, bf16[512,1024]{1,0:T(8,128)(2,1)}, u32[]{:S(2)}) copy-start(bf16[512,1024]{1,0:T(8,128)(2,1)} %copy-done.6) | copy-start | bytes 3145732
  41.8 11.0 %collective-permute-start.15 = (bf16[640,512]{1,0:T(8,128)(2,1)S(1)}, bf16[640,512]{1,0:T(8,128)(2,1)S(1)}, u32[]{:S(2)}, u32[]{:S(2)}) collective-permute-start(bf16[640,512]{1,0:T(8,128)(2,1)S(1)} %get-tuple-element.134), channel_id=1, source_target_pairs={{10,9},{11,10},{12,15},{13,12},{18,17},{19,18},{20,23},{21,20},{26... | collective-permute-start | bytes 1966088 | tf_op jit(solution)/shard_map/ppermute | solution.py:415
  47.1 6.4 %collective-permute-start.18 = (bf16[384,512]{1,0:T(8,128)(2,1)}, bf16[384,512]{1,0:T(8,128)(2,1)S(1)}, u32[]{:S(2)}, u32[]{:S(2)}) collective-permute-start(bf16[384,512]{1,0:T(8,128)(2,1)} %get-tuple-element.141), channel_id=1, source_target_pairs={{10,12},{11,13},{12,8},{13,9},{18,20},{19,21},{20,16},{21,17},{26,... | collective-permute-start | bytes 1179656 | tf_op jit(solution)/shard_map/ppermute | solution.py:415
  47.8 6.4 %collective-permute-start.19 = (bf16[384,512]{1,0:T(8,128)(2,1)}, bf16[384,512]{1,0:T(8,128)(2,1)S(1)}, u32[]{:S(2)}, u32[]{:S(2)}) collective-permute-start(bf16[384,512]{1,0:T(8,128)(2,1)} %get-tuple-element.142), channel_id=1, source_target_pairs={{10,13},{11,14},{12,9},{13,10},{18,21},{19,22},{20,17},{21,18},{26... | collective-permute-start | bytes 1179656 | tf_op jit(solution)/shard_map/ppermute | solution.py:415
  48.5 6.4 %collective-permute-start.20 = (bf16[384,512]{1,0:T(8,128)(2,1)S(1)}, bf16[384,512]{1,0:T(8,128)(2,1)S(1)}, u32[]{:S(2)}, u32[]{:S(2)}) collective-permute-start(bf16[384,512]{1,0:T(8,128)(2,1)S(1)} %get-tuple-element.143), channel_id=1, source_target_pairs={{10,14},{11,15},{12,10},{13,11},{18,22},{19,23},{20,18},{21,19},{2... | collective-permute-start | bytes 1179656 | tf_op jit(solution)/shard_map/ppermute | solution.py:415
  49.2 7.0 %collective-permute-start.21 = (bf16[384,512]{1,0:T(8,128)(2,1)S(1)}, bf16[384,512]{1,0:T(8,128)(2,1)S(1)}, u32[]{:S(2)}, u32[]{:S(2)}) collective-permute-start(bf16[384,512]{1,0:T(8,128)(2,1)S(1)} %get-tuple-element.144), channel_id=1, source_target_pairs={{10,15},{11,12},{12,11},{13,8},{18,23},{19,20},{20,19},{21,16},{26... | collective-permute-start | bytes 1179656 | tf_op jit(solution)/shard_map/ppermute | solution.py:415
  52.8 4.7 %collective-permute-start.25 = (bf16[384,512]{1,0:T(8,128)(2,1)S(1)}, bf16[384,512]{1,0:T(8,128)(2,1)S(1)}, u32[]{:S(2)}, u32[]{:S(2)}) collective-permute-start(bf16[384,512]{1,0:T(8,128)(2,1)S(1)} %get-tuple-element.151), channel_id=1, source_target_pairs={{2,4},{3,5},{4,0},{5,1}} | collective-permute-start | bytes 1179656 | tf_op jit(solution)/shard_map/ppermute | solution.py:415
  53.5 5.3 %collective-permute-start.26 = (bf16[384,512]{1,0:T(8,128)(2,1)S(1)}, bf16[384,512]{1,0:T(8,128)(2,1)S(1)}, u32[]{:S(2)}, u32[]{:S(2)}) collective-permute-start(bf16[384,512]{1,0:T(8,128)(2,1)S(1)} %get-tuple-element.152), channel_id=1, source_target_pairs={{2,5},{3,6},{4,1},{5,2}} | collective-permute-start | bytes 1179656 | tf_op jit(solution)/shard_map/ppermute | solution.py:415
  54.2 71.8 %collective-permute-start.22 = (bf16[640,512]{1,0:T(8,128)(2,1)S(1)}, bf16[640,512]{1,0:T(8,128)(2,1)S(1)}, u32[]{:S(2)}, u32[]{:S(2)}) collective-permute-start(bf16[640,512]{1,0:T(8,128)(2,1)S(1)} %get-tuple-element.148), channel_id=1, source_target_pairs={{2,3},{3,0},{4,5},{5,6}} | collective-permute-start | bytes 1966088 | tf_op jit(solution)/shard_map/ppermute | solution.py:415
  54.9 74.4 %collective-permute-start.23 = (bf16[640,512]{1,0:T(8,128)(2,1)S(1)}, bf16[640,512]{1,0:T(8,128)(2,1)S(1)}, u32[]{:S(2)}, u32[]{:S(2)}) collective-permute-start(bf16[640,512]{1,0:T(8,128)(2,1)S(1)} %get-tuple-element.149), channel_id=1, source_target_pairs={{2,0},{3,1},{4,6},{5,7}} | collective-permute-start | bytes 1966088 | tf_op jit(solution)/shard_map/ppermute | solution.py:415
  56.2 78.8 %collective-permute-start.24 = (bf16[640,512]{1,0:T(8,128)(2,1)S(1)}, bf16[640,512]{1,0:T(8,128)(2,1)S(1)}, u32[]{:S(2)}, u32[]{:S(2)}) collective-permute-start(bf16[640,512]{1,0:T(8,128)(2,1)S(1)} %get-tuple-element.150), channel_id=1, source_target_pairs={{2,1},{3,2},{4,7},{5,4}} | collective-permute-start | bytes 1966088 | tf_op jit(solution)/shard_map/ppermute | solution.py:415
  57.5 63.3 %collective-permute-start.27 = (bf16[384,512]{1,0:T(8,128)(2,1)S(1)}, bf16[384,512]{1,0:T(8,128)(2,1)S(1)}, u32[]{:S(2)}, u32[]{:S(2)}) collective-permute-start(bf16[384,512]{1,0:T(8,128)(2,1)S(1)} %get-tuple-element.153), channel_id=1, source_target_pairs={{2,6},{3,7},{4,2},{5,3}} | collective-permute-start | bytes 1179656 | tf_op jit(solution)/shard_map/ppermute | solution.py:415
  58.9 67.1 %collective-permute-start.28 = (bf16[384,512]{1,0:T(8,128)(2,1)S(1)}, bf16[384,512]{1,0:T(8,128)(2,1)S(1)}, u32[]{:S(2)}, u32[]{:S(2)}) collective-permute-start(bf16[384,512]{1,0:T(8,128)(2,1)S(1)} %get-tuple-element.154), channel_id=1, source_target_pairs={{2,7},{3,4},{4,3},{5,0}} | collective-permute-start | bytes 1179656 | tf_op jit(solution)/shard_map/ppermute | solution.py:415
  (14 other events, 59.2 us)
